TPU v7x, 512 devices: a whole 4x4x16 slice. The times are simulated.
512 devices in a mesh: seq: 32 (over z, x_hi), mp: 16 (over x_lo, y, core).
Axes of the slice: x: 4 (x_hi: 2, x_lo: 2; x = x_hi * 2 + x_lo), y: 4, z: 16, core: 2. Of those that a mesh axis runs over, the one named last changes fastest.
Arguments:
- queries: bfloat16 [4096, 4096], P('seq', 'mp'), may hold values from -100 to 100
- stretch_keys: bfloat16 [4096, 4096], P('seq', 'mp'), may hold values from -6 to 6
- stretch_values: bfloat16 [4096, 4096], P('seq', 'mp'), may hold values from -5 to 5
- cache_keys: bfloat16 [4096, 4096], P('seq', 'mp'), may hold values from -5 to 5
- cache_values: bfloat16 [4096, 4096], P('seq', 'mp'), may hold values from -5 to 5
- cache_lengths: int32 [32], P('seq'), may hold values from 1 to 128, as said below
- frame_mask: int32 [4, 4], replicated, may hold values from 0 to 1, as said below
- out_weight: bfloat16 [4096, 5120], P('mp'), may hold values from -0.09375 to 0.09375
- head_weight: bfloat16 [5120, 64], P('mp'), may hold values from -0.8359375 to 0.8359375
- previous_latent: bfloat16 [2, 32, 128, 16], P(None, 'mp', 'seq'), may hold values from -2 to 2
- conv_weight: bfloat16 [3, 3, 3, 16, 384], replicated, may hold values from -0.3125 to 0.3125
- conv_bias: float32 [384], replicated, may hold values from -1.5 to 1.5
- norm_gain: float32 [384], replicated, may hold values from 0.5 to 1.5
Outputs:
- decoded: bfloat16 [4, 32, 128, 384], P(None, 'mp', 'seq')
Inputs may be any that keep to these rules, and one draw needn't show every extreme that they name: `cache_lengths`: some index of seq has all 128 slots filled. `frame_mask`: the diagonal is 1 and the entries above it are 0.
All inputs are finite; a program needn't handle non-finite values.
Results may differ from a plain program's by a relative error of at most 0.034.
Values may be sent and summed in bfloat16 or wider, within the bound.
No kernel may reach another device: no remote copies, remote signals or barrier semaphores. Data moves between devices by JAX's collectives and lax.ppermute only.
A program may use at most 64 MiB of HBM per device.

v0:
```python
import math

import jax
import jax.numpy as jnp
from jax import lax
from jax.sharding import PartitionSpec as P

HD = 128
LATC = 16
CH = 384
FR = 4


def padded_2(value, sides, width):
    for axis, dim in sides:
        devices, length = (lax.axis_size(axis), value.shape[dim])
        up = [(i, (i + 1) % devices) for i in range(devices - 1)]
        down = [(j, i) for i, j in up]
        last = lax.slice_in_dim(value, length - width, length, axis=dim)
        first = lax.slice_in_dim(value, 0, width, axis=dim)
        before = lax.ppermute(last, axis, up)
        after = lax.ppermute(first, axis, down)
        value = jnp.concatenate([before, value, after], axis=dim)
    return value


def body(
    queries,
    stretch_keys,
    stretch_values,
    cache_keys,
    cache_values,
    cache_lengths,
    frame_mask,
    out_weight,
    head_weight,
    previous_latent,
    conv_weight,
    conv_bias,
    norm_gain,
):
    cycle = lax.axis_size("seq")
    place = lax.axis_index("seq")
    tok_rows = queries.shape[0]
    heads_here = queries.shape[1] // HD
    per_frame = tok_rows * cycle // FR
    slot_rows = cache_keys.shape[0]
    scale = 1.0 / math.sqrt(HD)

    def stretch_frames(anchor):
        return (anchor * tok_rows + jnp.arange(tok_rows)) // per_frame

    cache_code = jnp.where(jnp.arange(slot_rows) < cache_lengths[0], -1, FR).astype(jnp.int32)
    codes = jnp.concatenate([cache_code, stretch_frames(place)])
    keys_all = jnp.concatenate([cache_keys, stretch_keys], 0)
    values_all = jnp.concatenate([cache_values, stretch_values], 0)
    key_total = keys_all.shape[0]

    def attend(state, query, allowed, keys, values, code):
        top_old, total_old, summed = state
        query_heads = query.reshape(tok_rows, heads_here, HD)
        key_heads = keys.reshape(-1, heads_here, HD)
        value_heads = values.reshape(-1, heads_here, HD)
        visible = code[None, :] == -1
        for frame in range(FR):
            visible = visible | (code[None, :] == frame) & (allowed[:, frame : frame + 1] == 1)
        scores = (
            jnp.einsum("qhd,khd->hqk", query_heads, key_heads, preferred_element_type=jnp.float32)
            * scale
        )
        scores = jnp.where(visible[None], scores, -1e30)
        top_new = jnp.maximum(top_old, jnp.max(scores, -1))
        weights = jnp.where(visible[None], jnp.exp(scores - top_new[:, :, None]), 0.0)
        factor = jnp.exp(top_old - top_new)
        total_new = total_old * factor + jnp.sum(weights, -1)
        added = jnp.einsum(
            "hqk,khd->qhd",
            weights.astype(jnp.bfloat16),
            value_heads,
            preferred_element_type=jnp.float32,
        )
        summed = summed * factor.T[:, :, None] + added
        return (top_new, total_new, summed)

    start_state = (
        jnp.full((heads_here, tok_rows), -1e30, jnp.float32),
        jnp.zeros((heads_here, tok_rows), jnp.float32),
        jnp.zeros((tok_rows, heads_here, HD), jnp.float32),
    )
    onehot = (stretch_frames(place)[:, None] == jnp.arange(FR)[None, :]).astype(jnp.int32)
    own_allowed = jnp.dot(onehot, frame_mask)
    state = start_state
    keys = lax.all_gather(keys_all, "seq", axis=0, tiled=True)
    values = lax.all_gather(values_all, "seq", axis=0, tiled=True)
    code = lax.all_gather(codes, "seq", axis=0, tiled=True)
    group = 4
    span = group * key_total
    blocks = (
        keys.reshape(-1, span, keys.shape[1]),
        values.reshape(-1, span, values.shape[1]),
        code.reshape(-1, span),
    )

    def one_block(inner, block):
        return (attend(inner, queries, own_allowed, block[0], block[1], block[2]), None)

    state, unused = lax.scan(one_block, state, blocks)
    attended = (
        (state[2] / state[1].T[:, :, None]).astype(jnp.bfloat16).reshape(tok_rows, heads_here * HD)
    )
    proj_terms = jnp.dot(attended, out_weight, preferred_element_type=jnp.float32)
    projected = lax.psum_scatter(
        proj_terms.astype(jnp.bfloat16), "mp", scatter_dimension=1, tiled=True
    )
    partial_value = jnp.dot(projected, head_weight, preferred_element_type=jnp.float32)
    patch_rows = tok_rows // (2 * cycle)
    frame_rows_px = tok_rows // FR
    rows_mp = frame_rows_px // lax.axis_size("mp")
    latent = lax.psum(partial_value.astype(jnp.bfloat16), "mp")
    grid = latent.reshape(patch_rows, 2 * cycle, 2, 2, LATC).transpose(0, 2, 1, 3, 4)
    moved = lax.all_to_all(
        grid.reshape(2 * patch_rows, cycle, 4, LATC), "seq", split_axis=1, concat_axis=0, tiled=True
    ).reshape(FR, frame_rows_px, 4, LATC)
    tile = lax.dynamic_slice_in_dim(moved, lax.axis_index("mp") * rows_mp, rows_mp, 1)
    stacked = jnp.concatenate([previous_latent, tile], 0)
    padded = padded_2(stacked, (("seq", 2), ("mp", 1)), 1)
    cols_here = tile.shape[2]
    pieces = []
    for step_t in range(3):
        for step_y in range(3):
            for step_x in range(3):
                pieces.append(
                    padded[
                        step_t : step_t + FR,
                        step_y : step_y + rows_mp,
                        step_x : step_x + cols_here,
                        :,
                    ]
                )
    columns = jnp.stack(pieces, 3).reshape(-1, 27 * LATC)
    conv = (
        jnp.dot(columns, conv_weight.reshape(27 * LATC, CH), preferred_element_type=jnp.float32)
        + conv_bias
    )
    meansq = jnp.mean(conv * conv, -1, keepdims=True)
    normed = conv * lax.rsqrt(meansq + 1e-06) * norm_gain
    return jax.nn.silu(normed).astype(jnp.bfloat16).reshape(FR, rows_mp, cols_here, CH)


def solution(mesh):
    return jax.shard_map(
        body,
        mesh=mesh,
        in_specs=(
            P("seq", "mp"),
            P("seq", "mp"),
            P("seq", "mp"),
            P("seq", "mp"),
            P("seq", "mp"),
            P("seq"),
            P(),
            P("mp", None),
            P("mp", None),
            P(None, "mp", "seq", None),
            P(),
            P(),
            P(),
        ),
        out_specs=P(None, "mp", "seq", None),
        check_vma=False,
    )
```

profile of v0, /device:TPU:1, one launch (start us, length us, event | category | flops | bytes accessed | tf_op | source)
XLA Modules:
  0.0 605.9 jit_solution(1538676679394822303)
XLA Ops:
  6.5 1.7 pad_maximum_fusion
  8.3 1.5 pad_maximum_fusion.1
  10.6 69.1 %all-gather = s32[32,1,256]{2,1,0:T(1,128)S(1)} all-gather(s32[1,1,256]{2,1,0:T(1,128)S(1)} %bitcast.194), channel_id=1, replica_groups=mesh['seq'=32,'mp'=16] {'seq'}, dimensions={0}, use_global_device_ids=true | all-gather | bytes 33792 | tf_op jit(solution)/shard_map/all_gather | solution.py:95
  80.7 91.1 %all-gather.4.cloned.1.call-done = bf16[8192,256]{1,0:T(8,128)(2,1)} async-done(((bf16[256,256]{1,0:T(8,128)(2,1)}), bf16[8192,256]{1,0:T(8,128)(2,1)}) %all-gather.4.cloned.1.call-update) | async-done | bytes 4194320 | tf_op jit(solution)/shard_map/all_gather | solution.py:93
  171.8 161.6 %all-gather.6.cloned.1.call-done = bf16[8192,256]{1,0:T(8,128)(2,1)} async-done(((bf16[256,256]{1,0:T(8,128)(2,1)}), bf16[8192,256]{1,0:T(8,128)(2,1)}) %all-gather.6.cloned.1.call-update) | async-done | bytes 4194320 | tf_op jit(solution)/shard_map/all_gather | solution.py:94
  333.4 88.7 %while.15 = (s32[]{:T(128)}, f32[2,128]{1,0:T(2,128)S(1)}, f32[2,128]{1,0:T(2,128)S(1)}, f32[128,2,128]{0,2,1:T(8,128)S(1)}, s32[8,1024]{1,0:T(8,128)S(1)}, /*in...) while((s32[]{:T(128)}, f32[2,128]{1,0:T(2,128)S(1)}, ...), condition=%wide.region_3.4_spmd.clone, body=%wide.region_0.3_spmd.clone.sunk | while | flops 137731072 | bytes 13731001 | solution.py:107
  334.7 2.1 constant_dynamic-slice_fusion.5
  336.8 2.0 copy.60
  338.9 2.4 fusion.47
  342.3 1.9 fusion.51
  345.8 2.1 constant_dynamic-slice_fusion.5
  347.9 2.0 copy.60
  350.0 2.4 fusion.47
  353.4 1.9 fusion.51
  356.9 2.1 constant_dynamic-slice_fusion.5
  359.0 2.0 copy.60
  361.1 2.4 fusion.47
  364.5 1.9 fusion.51
  368.0 2.1 constant_dynamic-slice_fusion.5
  370.1 2.0 copy.60
  372.1 2.4 fusion.47
  375.6 1.9 fusion.51
  379.1 2.1 constant_dynamic-slice_fusion.5
  381.2 2.0 copy.60
  383.2 2.4 fusion.47
  386.7 1.9 fusion.51
  390.1 2.1 constant_dynamic-slice_fusion.5
  392.3 2.0 copy.60
  394.3 2.4 fusion.47
  397.8 1.9 fusion.51
  401.2 2.1 constant_dynamic-slice_fusion.5
  403.4 2.0 copy.60
  405.4 2.4 fusion.47
  408.9 1.9 fusion.51
  412.3 2.1 constant_dynamic-slice_fusion.5
  414.5 2.0 copy.60
  416.5 2.4 fusion.47
  420.0 1.9 fusion.51
  422.2 2.2 convolution_convert_fusion
  424.4 69.7 %reduce-scatter.2.cloned.1.call-done = bf16[128,320]{0,1:T(8,128)(2,1)} async-done(((bf16[128,5120]{0,1:T(8,128)(2,1)}), bf16[128,320]{0,1:T(8,128)(2,1)}) %reduce-scatter.2.cloned.1.call-update) | async-done | bytes 81936 | tf_op jit(solution)/shard_map/reduce_scatter | solution.py:112
  495.4 53.8 %psum.7 = bf16[4,32,4,16]{3,2,1,0:T(4,128)(2,1)S(1)} all-reduce(bf16[4,32,4,16]{3,2,1,0:T(4,128)(2,1)S(1)} %bitcast.187), channel_id=1, replica_groups=mesh['seq'=32,'mp'=16] {'mp'}, use_global_device_ids=true, to_apply=%region_5.6 | all-reduce | flops 8192 | bytes 32768 | tf_op jit(solution)/shard_map/psum | solution.py:119
  550.0 13.7 %all-to-all-start = ((bf16[32,2,128]{2,1,0:T(2,128)(2,1)}), bf16[32,2,128]{2,1,0:T(2,128)(2,1)S(1)}, u32[]{:S(2)}, u32[]{:S(2)}) async-start(bf16[32,2,128]{2,1,0:T(2,128)(2,1)} %reshape.236), calls=%async_computation.1 | async-start | bytes 32768 | tf_op jit(solution)/shard_map/all_to_all | solution.py:121
  563.8 13.5 %all-to-all-done = bf16[32,2,128]{2,1,0:T(2,128)(2,1)S(1)} async-done(((bf16[32,2,128]{2,1,0:T(2,128)(2,1)}), bf16[32,2,128]{2,1,0:T(2,128)(2,1)S(1)}, u32[]{:S(2)}, u32[]{:S(2)}) %all-to-all-start) | async-done | bytes 16416 | tf_op jit(solution)/shard_map/all_to_all | solution.py:121
  577.5 2.3 collective-permute-start
  579.9 1.3 collective-permute-start.1
  581.2 4.5 collective-permute-done.1
  585.8 6.4 %collective-permute-start.2 = (bf16[6,1,6,16]{3,1,0,2:T(2,128)(2,1)S(1)}, bf16[6,1,6,16]{3,1,0,2:T(2,128)(2,1)S(1)}, u32[]{:S(2)}, u32[]{:S(2)}) collective-permute-start(bf16[6,1,6,16]{3,1,0,2:T(2,128)(2,1)S(1)} %get-tuple-element.148), channel_id=1, source_target_pairs={{0,1},{1,2},{2,3},{3,4},{4,5},{5,6},{6,7},{7,8},{8,9},{9,10},{10,1... | collective-permute-start | bytes 3464 | tf_op jit(solution)/shard_map/ppermute | solution.py:21
  592.2 4.1 collective-permute-start.3
  (175 shorter events, 26.9 us)
Async XLA Ops:
  6.5 415.6 %copy-start = (bf16[256,5120]{1,0:T(8,128)(2,1)S(1)}, bf16[256,5120]{1,0:T(8,128)(2,1)}, u32[]{:S(2)}) copy-start(bf16[256,5120]{1,0:T(8,128)(2,1)} %param.22) | copy-start | bytes 7864324
  6.5 165.3 %all-gather.4.cloned.1.call-start = ((), (), s32[]{:S(2)}) async-start(), calls=%async_computation.2 | async-start | bytes 4325376 | tf_op jit(solution)/shard_map/all_gather | solution.py:93
  8.2 325.2 %all-gather.6.cloned.1.call-start = ((), (), s32[]{:S(2)}) async-start(), calls=%async_computation.3 | async-start | bytes 4325376 | tf_op jit(solution)/shard_map/all_gather | solution.py:94
  9.9 484.3 %reduce-scatter.2.cloned.1.call-start = ((), (), s32[]{:S(2)}) async-start(), calls=%async_computation.4 | async-start | bytes 1392640 | tf_op jit(solution)/shard_map/reduce_scatter | solution.py:112
  333.4 5.5 copy-start.2
  342.3 1.9 copy-start.1
  344.5 5.5 copy-start.2
  353.4 1.9 copy-start.1
  355.6 5.5 copy-start.2
  364.5 1.9 copy-start.1
  366.7 5.5 copy-start.2
  375.6 1.9 copy-start.1
  377.8 5.5 copy-start.2
  386.7 1.9 copy-start.1
  388.8 5.5 copy-start.2
  397.8 1.9 copy-start.1
  399.9 5.5 copy-start.2
  408.9 1.9 copy-start.1
  411.0 5.5 copy-start.2
  420.0 1.9 copy-start.1
  422.1 72.0 %copy-start.4 = (bf16[320,64]{0,1:T(8,128)(2,1)S(1)}, bf16[320,64]{0,1:T(8,128)(2,1)}, u32[]{:S(2)}) copy-start(bf16[320,64]{0,1:T(8,128)(2,1)} %param.23) | copy-start | bytes 122884
  422.2 141.6 %copy-start.5 = (bf16[2,2,4,16]{3,2,1,0:T(4,128)(2,1)S(1)}, bf16[2,2,4,16]{3,2,1,0:T(4,128)(2,1)}, u32[]{:S(2)}) copy-start(bf16[2,2,4,16]{3,2,1,0:T(4,128)(2,1)} %param.24) | copy-start | bytes 1540
  424.4 173.9 %copy-start.3 = (bf16[3,3,3,16,384]{4,3,2,1,0:T(8,128)(2,1)S(1)}, bf16[3,3,3,16,384]{4,3,2,1,0:T(8,128)(2,1)}, u32[]{:S(2)}) copy-start(bf16[3,3,3,16,384]{4,3,2,1,0:T(8,128)(2,1)} %param.25) | copy-start | bytes 995332
  424.4 174.0 %copy-start.6 = (f32[384]{0:T(512)S(1)}, f32[384]{0:T(512)}, u32[]{:S(2)}) copy-start(f32[384]{0:T(512)} %param.26) | copy-start | bytes 4612
  424.4 174.3 %copy-start.7 = (f32[384]{0:T(512)S(1)}, f32[384]{0:T(512)}, u32[]{:S(2)}) copy-start(f32[384]{0:T(512)} %param.27) | copy-start | bytes 4612
  550.0 27.2 %all-to-all-start = ((bf16[32,2,128]{2,1,0:T(2,128)(2,1)}), bf16[32,2,128]{2,1,0:T(2,128)(2,1)S(1)}, u32[]{:S(2)}, u32[]{:S(2)}) async-start(bf16[32,2,128]{2,1,0:T(2,128)(2,1)} %reshape.236), calls=%async_computation.1 | async-start | bytes 32768 | tf_op jit(solution)/shard_map/all_to_all | solution.py:121
  577.5 3.6 collective-permute-start
  579.9 5.8 collective-permute-start.1
  585.8 10.6 %collective-permute-start.2 = (bf16[6,1,6,16]{3,1,0,2:T(2,128)(2,1)S(1)}, bf16[6,1,6,16]{3,1,0,2:T(2,128)(2,1)S(1)}, u32[]{:S(2)}, u32[]{:S(2)}) collective-permute-start(bf16[6,1,6,16]{3,1,0,2:T(2,128)(2,1)S(1)} %get-tuple-element.148), channel_id=1, source_target_pairs={{0,1},{1,2},{2,3},{3,4},{4,5},{5,6},{6,7},{7,8},{8,9},{9,10},{10,1... | collective-permute-start | bytes 3464 | tf_op jit(solution)/shard_map/ppermute | solution.py:21
  592.2 5.1 collective-permute-start.3
Sparse Core Ops, SparseCore 0:
  10.5 161.3 all-gather.3
  174.9 158.4 all-gather.5
  424.6 69.5 reduce-scatter.1
where the time goes:
time: 613 us; the launch traced here: 606 us
  waiting for transfers between devices  341 us (56%)
  blocking collectives  123 us (20%)
  local copies, waits for them, and re-layouts  44.3 us (7%)
  matrix products  38.9 us (6%)
  starting transfers between devices  27.9 us (5%)
  other arithmetic  15.9 us (3%)
  between operations  14.2 us (2%)
    all_gather x1, waiting for transfers between devices, body(): values = lax.all_gather(values_all, 'seq', axis=0, tiled=True)  162 us
    all_gather x1, waiting for transfers between devices, body(): keys = lax.all_gather(keys_all, 'seq', axis=0, tiled=True)  91.1 us
    reduce_scatter x1, waiting for transfers between devices, body(): lax.psum_scatter(proj_terms.astype(jnp.bfloat16), 'mp', scatter_dimension...  69.7 us
    all_gather x1, blocking collectives, body(): code = lax.all_gather(codes, 'seq', axis=0, tiled=True)  69.1 us
    psum x1, blocking collectives, body(): latent = lax.psum(partial_value.astype(jnp.bfloat16), 'mp')  53.8 us
    dynamic_slice x24, local copies, waits for them, and re-layouts, body(): state, unused = lax.scan(one_block, state, blocks)  41.4 us
    dot_general x8, matrix products, attend(): jnp.einsum('qhd,khd->hqk', query_heads, key_heads, preferred_element_type...  19.6 us
    dot_general x8, matrix products, attend(): jnp.einsum('hqk,khd->qhd', weights.astype(jnp.bfloat16), value_heads, pre...  14.8 us
  transfers between devices with their start and end apart: 8, of which 6 were waited for; matrix products, arithmetic and copies ran while one was open for 0% of the time, Pallas kernels for 0%

commit v1 on v0

v1 whole, which is shorter than its diff:
```python
import math

import jax
import jax.numpy as jnp
import numpy as np
from jax import lax
from jax.experimental import pallas as pl
from jax.experimental.pallas import tpu as pltpu
from jax.sharding import Mesh, PartitionSpec as P

HD = 128
LATC = 16
CH = 384
FR = 4
NZ = 16
NEG = -1e30
C2 = math.log2(math.e) / math.sqrt(HD)
F32 = jnp.float32
BF16 = jnp.bfloat16
FAR = [[(4 * j + i) * 2 + k for j in range(4) for k in range(2)] for i in range(4)]
NEAR = [[(4 * i + j) * 2 + k for j in range(4) for k in range(2)] for i in range(4)]
NT = (((1,), (1,)), ((), ()))


def dot_nt(a, b):
    return lax.dot_general(a, b, NT, preferred_element_type=F32)


def attend_kernel(fm_ref, pos_ref, q_ref, kv_ref, w2t_ref, pv_ref, out_ref, pt_ref):
    group = pos_ref[0] // 4
    lane = lax.broadcasted_iota(jnp.int32, (1, HD), 1)
    row_frame = lax.broadcasted_iota(jnp.int32, (128, 1), 0) // 32
    block_bias = jnp.zeros((128, 1), F32)
    for f in range(FR):
        here = jnp.where(fm_ref[f, group] == 1, 0.0, NEG)
        block_bias = jnp.where(row_frame == f, here, block_bias)
    block_bias = jnp.broadcast_to(block_bias, (128, 128))
    cache_bias = []
    for s in range(8):
        filled = kv_ref[s, 512:528, :].astype(F32)[0:1]
        cache_bias.append(jnp.where(lane.astype(F32) < filled, 0.0, NEG))

    def block(b, carry):
        q = q_ref[:, b].reshape(128, HD)
        scores = []
        for s in range(8):
            raw = dot_nt(q, kv_ref[s, 0:256, :]) * C2
            bias = jnp.concatenate(
                [jnp.broadcast_to(cache_bias[s], (128, 128)), block_bias], axis=1
            )
            scores.append(raw + bias)
        top = scores[0]
        for s in range(1, 8):
            top = jnp.maximum(top, scores[s])
        top = jnp.max(top, axis=1, keepdims=True)
        total = jnp.zeros((128, 256), F32)
        acc = jnp.zeros((128, HD), F32)
        for s in range(8):
            weights = jnp.exp2(scores[s] - top)
            total = total + weights
            acc = acc + jnp.dot(
                weights.astype(BF16), kv_ref[s, 256:512, :], preferred_element_type=F32
            )
        total = jnp.sum(total, axis=1, keepdims=True)
        attended = (acc / total).astype(BF16)
        pt_ref[b, 0:64] = dot_nt(w2t_ref[...], attended)
        level = jnp.broadcast_to(top + jnp.log2(total), (128, 128)).T[0:8]
        high = level.astype(BF16).astype(F32)
        mid = (level - high).astype(BF16).astype(F32)
        low = level - high - mid
        part = lax.broadcasted_iota(jnp.int32, (8, 128), 0)
        pt_ref[b, 64:72] = jnp.where(
            part == 0, high, jnp.where(part == 1, mid, jnp.where(part == 2, low, 0.0))
        )
        return carry

    lax.fori_loop(0, 8, block, 0)
    column = lax.broadcasted_iota(jnp.int32, (72, 128), 1) % 8
    for z in range(NZ):
        b = z // 2
        own = pt_ref[b]
        if z % 2 == 0:
            chunk = jnp.where(column <= 4, own, 0.0)
            if b > 0:
                chunk = jnp.where(column == 7, pt_ref[b - 1], chunk)
        else:
            chunk = jnp.where(column >= 3, own, 0.0)
            if b < 7:
                chunk = jnp.where(column == 0, pt_ref[b + 1], chunk)
        out_ref[z, 0:64] = chunk[0:64].astype(BF16)
        out_ref[z, 64:80] = jnp.concatenate([chunk[64:72], pv_ref[...]], axis=0).astype(BF16)


def spread_kernel(pos_ref, y_ref, pv_ref, pick_ref, out_ref, rhs_ref):
    z, h, m = pos_ref[0], pos_ref[1], pos_ref[2]
    odd = z % 2 == 1
    column = lax.broadcasted_iota(jnp.int32, (64, 128), 1) % 8
    rhs_ref[...] = jnp.zeros_like(rhs_ref)
    for r in range(4):
        levels = []
        for g in range(4):
            tail = y_ref[4 * g + r, 64:80].astype(F32)
            levels.append(tail[0:1] + tail[1:2] + tail[2:3])
        top = jnp.maximum(jnp.maximum(levels[0], levels[1]), jnp.maximum(levels[2], levels[3]))
        shares = [jnp.exp2(level - top) for level in levels]
        whole = shares[0] + shares[1] + shares[2] + shares[3]
        value = jnp.zeros((64, 128), F32)
        for g in range(4):
            value = value + (shares[g] / whole) * y_ref[4 * g + r, 0:64].astype(F32)
        turned = jnp.where(
            column < 4, pltpu.roll(value, 124, 1), pltpu.roll(value, 4, 1)
        )
        value = jnp.where(odd, turned, value)
        rhs_ref[0:64, 128 * r : 128 * r + 128] = value.astype(BF16)
    left = y_ref[jnp.maximum(z - 1, 0), 64:80].astype(F32)[8:16]
    right = y_ref[jnp.minimum(z + 1, NZ - 1), 64:80].astype(F32)[8:16]
    left = jnp.where((z > 0) & (h == 1), left, 0.0)
    right = jnp.where((z < NZ - 1) & (h == 0), right, 0.0)
    rows = jnp.concatenate([pv_ref[...], left, right], axis=0)[:, 0:64].astype(BF16)
    item = lax.broadcasted_iota(jnp.int32, (24, 256), 0)
    spot = lax.broadcasted_iota(jnp.int32, (24, 256), 1)
    kind, index = item // 8, item % 8
    patch, frame = index // 2, index % 2
    cell = jnp.where(kind == 0, 2 * h + patch, jnp.where(kind == 1, 7, 4))
    wanted = (kind == 0) & (patch < 2) | (kind == 1) & (patch == 1) | (kind == 2) & (patch == 0)
    place = wanted & (spot // 128 == frame) & ((spot // 8) % 16 == m) & (spot % 8 == cell)
    place = jnp.where(place, 1.0, 0.0).astype(BF16)
    moved = lax.dot_general(rows, place, (((0,), (0,)), ((), ())), preferred_element_type=F32)
    rhs_ref[64:128, 512:768] = moved.astype(BF16)
    for part in range(4):
        got = dot_nt(pick_ref[384 * part : 384 * part + 384, :], rhs_ref[...])
        out_ref[8 * part : 8 * part + 8] = got.astype(BF16).reshape(8, 48, 128)


def picks():
    pick = np.zeros((2, 16, 3, 4, 4, 768), np.float32)
    cells = ((7, 0, 1, 2), (1, 2, 3, 4))
    for h in range(2):
        for m in range(16):
            for dr in range(3):
                row = m + dr - 1
                if not 0 <= row < 16:
                    continue
                for cc in range(4):
                    c = cells[h][cc]
                    for f in range(4):
                        pick[h, m, dr, cc, f, (row // 4) * 128 + f * 32 + (row % 4) * 8 + c] = 1
                        if f < 2:
                            pick[h, m, dr, cc, f, 512 + f * 128 + row * 8 + c] = 1
    return pick.reshape(1536, 768)


def decode_kernel(r_ref, w_ref, bias_ref, gain_ref, out_ref, z_ref):
    total = jnp.zeros((48, 128), F32)
    for s in range(32):
        total = total + r_ref[s].astype(F32)
    total = total.astype(BF16).astype(F32)
    z_ref[...] = jnp.zeros_like(z_ref)
    for dr in range(3):
        for cc in range(4):
            at = dr * 16 + cc * 4
            z_ref[dr, cc * 6 + 2 : cc * 6 + 6] = total[at : at + 4, 0:64]
            z_ref[dr, cc * 6 : cc * 6 + 2] = total[at : at + 2, 64:128]
    for a in range(2):
        for b in range(2):
            conv = jnp.zeros((16, CH), F32)
            for dt in range(3):
                pieces = []
                for i in range(2):
                    for j in range(2):
                        start = (b + j) * 6 + dt
                        pieces.append(z_ref[a + i, start : start + 16])
                lhs = jnp.concatenate(pieces, axis=1).astype(BF16)
                conv = conv + jnp.dot(lhs, w_ref[a, b, dt], preferred_element_type=F32)
            conv = conv + bias_ref[...]
            meansq = jnp.mean(conv * conv, axis=1, keepdims=True)
            normed = conv * lax.rsqrt(meansq + 1e-06) * gain_ref[...]
            decoded = (normed / (1.0 + jnp.exp(-normed))).astype(BF16)
            for c in range(2):
                for f in range(FR):
                    out_ref[f, a, 2 * c + b] = decoded[c * 6 + f]


def body(
    queries,
    stretch_keys,
    stretch_values,
    cache_keys,
    cache_values,
    cache_lengths,
    frame_mask,
    out_weight,
    head_weight,
    previous_latent,
    conv_weight,
    conv_bias,
    norm_gain,
):
    z, h, m = lax.axis_index("z"), lax.axis_index("h"), lax.axis_index("mp")
    pos = jnp.stack([z, h, m]).astype(jnp.int32)
    vmem = pl.BlockSpec(memory_space=pltpu.VMEM)
    smem = pl.BlockSpec(memory_space=pltpu.SMEM)
    params = pltpu.CompilerParams(vmem_limit_bytes=40 * 1024 * 1024)

    q = queries.reshape(2, 8, 8, 2, HD).transpose(3, 1, 0, 2, 4).reshape(1, 2, 8, 16, HD)
    q = jnp.broadcast_to(q, (4, 2, 8, 16, HD)).reshape(8, 8, 16, HD)
    q = lax.all_to_all(q, ("z", "h"), 0, 0, tiled=True, axis_index_groups=FAR)
    filled = jnp.broadcast_to(cache_lengths[0].astype(BF16), (16, 2 * HD))
    kv = jnp.concatenate([cache_keys, stretch_keys, cache_values, stretch_values, filled], 0)
    kv = kv.reshape(1, 528, 2, HD).transpose(0, 2, 1, 3)
    kv = jnp.broadcast_to(kv, (4, 2, 528, HD)).reshape(8, 528, HD)
    kv = lax.all_to_all(kv, ("z", "h"), 0, 0, tiled=True, axis_index_groups=NEAR)
    hw = jnp.broadcast_to(head_weight[None], (16,) + head_weight.shape)
    hw = lax.all_to_all(hw, "mp", 0, 0, tiled=True).reshape(-1, 64)
    rows = lax.dynamic_slice_in_dim(out_weight, h * HD, HD, 0)
    w2t = lax.dot_general(
        hw, rows, (((0,), (1,)), ((), ())), preferred_element_type=F32
    ).astype(BF16)
    pv = previous_latent.reshape(2, 2, 2, 2, LATC).transpose(2, 0, 1, 3, 4).reshape(4, 64)
    pv = jnp.pad(pv.astype(F32), ((0, 4), (0, 64)))

    partial = pl.pallas_call(
        attend_kernel,
        out_shape=jax.ShapeDtypeStruct((NZ, 80, 128), BF16),
        in_specs=[smem, smem, vmem, vmem, vmem, vmem],
        out_specs=vmem,
        scratch_shapes=[pltpu.VMEM((8, 72, 128), F32)],
        compiler_params=params,
        name="attend",
    )(frame_mask, pos, q, kv, w2t, pv)
    partial = lax.all_to_all(partial, "z", 0, 0, tiled=True)
    spread = pl.pallas_call(
        spread_kernel,
        out_shape=jax.ShapeDtypeStruct((32, 48, 128), BF16),
        in_specs=[smem, vmem, vmem, vmem],
        out_specs=vmem,
        scratch_shapes=[pltpu.VMEM((128, 768), BF16)],
        compiler_params=params,
        name="spread",
    )(pos, partial, pv, jnp.asarray(picks(), BF16))
    spread = lax.all_to_all(spread, ("h", "mp"), 0, 0, tiled=True)
    taps = []
    for a in range(2):
        for b in range(2):
            w = jnp.pad(conv_weight, ((0, 0), (1 - a, a), (1 - b, b), (0, 0), (0, 0)))
            w = w.reshape(3, 2, 2, 2, 2, LATC, CH).transpose(0, 1, 3, 2, 4, 5, 6)
            taps.append(w.reshape(3, 256, CH))
    taps = jnp.stack(taps).reshape(2, 2, 3, 256, CH)
    return pl.pallas_call(
        decode_kernel,
        out_shape=jax.ShapeDtypeStruct((FR, 2, 4, CH), BF16),
        in_specs=[vmem] * 4,
        out_specs=vmem,
        scratch_shapes=[pltpu.VMEM((3, 40, 64), F32)],
        compiler_params=params,
        name="decode",
    )(spread, taps, conv_bias.reshape(1, CH), norm_gain.reshape(1, CH))


def solution(mesh):
    fine = Mesh(mesh.devices.reshape(NZ, 2, 16), ("z", "h", "mp"))
    seq = ("z", "h")
    return jax.shard_map(
        body,
        mesh=fine,
        in_specs=(
            P(seq, "mp"),
            P(seq, "mp"),
            P(seq, "mp"),
            P(seq, "mp"),
            P(seq, "mp"),
            P(seq),
            P(),
            P("mp", None),
            P("mp", None),
            P(None, "mp", seq, None),
            P(),
            P(),
            P(),
        ),
        out_specs=P(None, "mp", seq, None),
        check_vma=False,
    )
```

time: 613 us -> 151 us (0.25)
  waiting for transfers between devices: 341 us -> 48.9 us
  blocking collectives: 123 us -> 18.1 us
  matrix products: 38.9 us -> 1.66 us
  local copies, waits for them, and re-layouts: 44.3 us -> 16.9 us
  starting transfers between devices: 27.9 us -> 50 us
  other arithmetic: 15.9 us -> 1.87 us
  between operations: 14.2 us -> 0.81 us
  Pallas kernels: 0 us -> 11.7 us
    all_gather x2 -> x0, waiting for transfers between devices: 253 us -> none  [the longest x1 162 us: body(): values = lax.all_gather(values_all, 'seq', axis=0, tiled=True)]
    reduce_scatter x1 -> x0, waiting for transfers between devices: 69.7 us -> none  [body(): lax.psum_scatter(proj_terms.astype(jnp.bfloat16), 'mp', scatter_dimension...]
    all_gather x1 -> x0, blocking collectives: 69.1 us -> none  [body(): code = lax.all_gather(codes, 'seq', axis=0, tiled=True)]
    psum x1 -> x0, blocking collectives: 53.8 us -> none  [body(): latent = lax.psum(partial_value.astype(jnp.bfloat16), 'mp')]
    dynamic_slice x25 -> x0, local copies, waits for them, and re-layouts: 41.5 us -> none  [the longest x24 41.4 us: body(): state, unused = lax.scan(one_block, state, blocks)]
    dot_general x20 -> x1, matrix products: 38.9 us -> 1.66 us  [body(): lax.dot_general(hw, rows, (((0,), (1,)), ((), ())), preferred_element_typ...]
    all_to_all x1 -> x4, starting transfers between devices: 13.7 us -> 50 us  [the longest x1 15.2 us: body(): spread = lax.all_to_all(spread, ('h', 'mp'), 0, 0, tiled=True)]
    all_to_all x1 -> x4, waiting for transfers between devices: 13.5 us -> 48.9 us  [the longest x1 18.1 us: body(): lax.all_to_all(kv, ('z', 'h'), 0, 0, tiled=True, axis_index_groups=NEAR)]
  transfers between devices with their start and end apart: 8 -> 4, of which waited for: 6 -> 4; matrix products, arithmetic and copies ran while one was open for 0% -> 8% of each run, Pallas kernels for 0% -> 0%
where the time goes in v1:
time: 151 us; the launch traced here: 150 us
  starting transfers between devices  50 us (33%)
  waiting for transfers between devices  48.9 us (32%)
  blocking collectives  18.1 us (12%)
  local copies, waits for them, and re-layouts  16.9 us (11%)
  Pallas kernels  11.7 us (8%)
  other arithmetic  1.87 us (1%)
  matrix products  1.66 us (1%)
    all_to_all x1, blocking collectives, body(): partial = lax.all_to_all(partial, 'z', 0, 0, tiled=True)  18.1 us
    all_to_all x1, waiting for transfers between devices, body(): lax.all_to_all(kv, ('z', 'h'), 0, 0, tiled=True, axis_index_groups=NEAR)  18.1 us
    all_to_all x1, starting transfers between devices, body(): spread = lax.all_to_all(spread, ('h', 'mp'), 0, 0, tiled=True)  15.2 us
    all_to_all x1, starting transfers between devices, body(): q = lax.all_to_all(q, ('z', 'h'), 0, 0, tiled=True, axis_index_groups=FAR)  13.5 us
    all_to_all x1, waiting for transfers between devices, body(): hw = lax.all_to_all(hw, 'mp', 0, 0, tiled=True).reshape(-1, 64)  13 us
    all_to_all x1, starting transfers between devices, body(): lax.all_to_all(kv, ('z', 'h'), 0, 0, tiled=True, axis_index_groups=NEAR)  11 us
    all_to_all x1, waiting for transfers between devices, body(): q = lax.all_to_all(q, ('z', 'h'), 0, 0, tiled=True, axis_index_groups=FAR)  10.3 us
    all_to_all x1, starting transfers between devices, body(): hw = lax.all_to_all(hw, 'mp', 0, 0, tiled=True).reshape(-1, 64)  10.3 us
  transfers between devices with their start and end apart: 4, of which 4 were waited for; matrix products, arithmetic and copies ran while one was open for 8% of the time, Pallas kernels for 0%

profile of v1, /device:TPU:1, one launch (start us, length us, event | category | flops | bytes accessed | tf_op | source)
XLA Modules:
  0.0 150.0 jit_solution(16232904171428705319)
XLA Ops:
  0.0 0.0 copy-start
  0.0 0.0 copy-start.6
  0.0 1.9 %broadcast_in_dim.28 = bf16[16,320,64]{1,2,0:T(8,128)(2,1)} broadcast(bf16[320,64]{0,1:T(8,128)(2,1)} %param.22), dimensions={1,2} | broadcast | bytes 696320 | tf_op jit(solution)/shard_map/broadcast_in_dim | solution.py:213
  2.0 10.3 %all-to-all-start.2 = ((bf16[16,320,64]{1,2,0:T(8,128)(2,1)}), bf16[16,320,64]{1,2,0:T(8,128)(2,1)S(1)}, u32[]{:S(2)}, u32[]{:S(2)}) async-start(bf16[16,320,64]{1,2,0:T(8,128)(2,1)} %broadcast_in_dim.28), calls=%async_computation.2 | async-start | bytes 1572864 | tf_op jit(solution)/shard_map/all_to_all | solution.py:214
  12.2 0.0 copy-done.6
  12.3 13.0 %all-to-all-done.2 = bf16[16,320,64]{1,2,0:T(8,128)(2,1)S(1)} async-done(((bf16[16,320,64]{1,2,0:T(8,128)(2,1)}), bf16[16,320,64]{1,2,0:T(8,128)(2,1)S(1)}, u32[]{:S(2)}, u32[]{:S(2)}) %all-to-all-start.2) | async-done | bytes 655392 | tf_op jit(solution)/shard_map/all_to_all | solution.py:214
  25.3 0.0 copy-start.4
  25.3 0.8 broadcast_in_dim.24
  26.1 0.2 copy-done.4
  26.3 13.5 %all-to-all-start = ((bf16[8,8,16,128]{3,2,1,0:T(8,128)(2,1)}), bf16[8,8,16,128]{3,2,1,0:T(8,128)(2,1)S(1)}, u32[]{:S(2)}, u32[]{:S(2)}) async-start(bf16[8,8,16,128]{3,2,1,0:T(8,128)(2,1)} %bitcast.52), calls=%async_computation | async-start | bytes 524288 | tf_op jit(solution)/shard_map/all_to_all | solution.py:207
  40.5 0.8 constant_dynamic-update-slice_fusion.4
  41.3 0.8 constant_dynamic-update-slice_fusion.3
  42.2 0.8 constant_dynamic-update-slice_fusion.2
  43.0 0.0 copy-start.7
  43.0 0.9 constant_dynamic-update-slice_fusion.1
  43.9 0.1 reshape.48
  44.0 10.3 %all-to-all-done.q_ref = bf16[8,8,16,128]{3,2,1,0:T(8,128)(2,1)S(1)} async-done(((bf16[8,8,16,128]{3,2,1,0:T(8,128)(2,1)}), bf16[8,8,16,128]{3,2,1,0:T(8,128)(2,1)S(1)}, u32[]{:S(2)}, u32[]{:S(2)}) %all-to-all-start) | async-done | bytes 262176 | tf_op jit(solution)/shard_map/all_to_all | solution.py:207
  54.3 1.1 broadcast_in_dim.27
  55.4 11.0 %all-to-all-start.1 = ((bf16[8,528,128]{2,1,0:T(8,128)(2,1)}), bf16[8,528,128]{2,1,0:T(8,128)(2,1)}, u32[]{:S(2)}, u32[]{:S(2)}) async-start(bf16[8,528,128]{2,1,0:T(8,128)(2,1)} %bitcast.42), calls=%async_computation.1 | async-start | bytes 2162688 | tf_op jit(solution)/shard_map/all_to_all | solution.py:212
  66.5 0.0 copy-done.7
  66.5 0.1 convert_element_type.37
  66.6 0.1 pad_add_fusion.pos_ref
  66.6 2.5 %copy.46 = bf16[16,320,64]{1,0,2:T(8,128)(2,1)} copy(bf16[16,320,64]{1,2,0:T(8,128)(2,1)} %copy-done.4) | data formatting | bytes 1310720 | tf_op jit(solution)/shard_map/all_to_all | solution.py:214
  69.1 2.4 %reshape.50 = bf16[5120,64]{0,1:T(8,128)(2,1)} reshape(bf16[16,320,64]{1,0,2:T(8,128)(2,1)} %copy.46) | data formatting | bytes 1310720 | tf_op jit(solution)/shard_map/reshape | solution.py:214
  71.6 0.0 copy-done
  71.6 1.7 %fusion.5.w2t_ref = bf16[64,128]{1,0:T(8,128)(2,1)S(1)} fusion(bf16[5120,64]{0,1:T(8,128)(2,1)} %reshape.50, bf16[256,5120]{1,0:T(8,128)(2,1)S(1)} %copy-done, s32[]{:T(128)S(6)} %select_n.3), kind=kOutput, calls=%fused_computation.4 | convolution fusion | flops 83894272 | bytes 1982468 | tf_op jit(solution)/shard_map/dot_general | solution.py:216
  73.2 18.1 %all-to-all-done.1.kv_ref = bf16[8,528,128]{2,1,0:T(8,128)(2,1)} async-done(((bf16[8,528,128]{2,1,0:T(8,128)(2,1)}), bf16[8,528,128]{2,1,0:T(8,128)(2,1)}, u32[]{:S(2)}, u32[]{:S(2)}) %all-to-all-start.1) | async-done | bytes 1081376 | tf_op jit(solution)/shard_map/all_to_all | solution.py:212
  91.3 0.0 copy-done.3
  91.3 8.2 %attend.1 = bf16[16,80,128]{2,1,0:T(8,128)(2,1)S(1)} custom-call(s32[4,4]{1,0:T(4,128)S(1)} %copy-done.3, s32[3]{0:T(128)S(1)} %pad_add_fusion.pos_ref, bf16[8,8,16,128]{3,2,1,0:T(8,128)(2,1)S(1)} %all-to-all-done.q_ref, bf16[8,528,128]{2,1,0:T(8,128)(2,1)} %all-to-all-done.1.kv_ref, bf16[64,128]{1,0:T(8,128)(2,1)S(1)} %fusion.5.w2t_ref, ...), custom_call_target="tpu_custom_call" | custom-call | tf_op jit(solution)/shard_map/attend/pallas_call | solution.py:222
  99.5 0.0 copy-start.5
  99.5 18.1 %all_to_all.25.y_ref = bf16[16,80,128]{2,1,0:T(8,128)(2,1)S(1)} all-to-all(bf16[16,80,128]{2,1,0:T(8,128)(2,1)S(1)} %attend.1), channel_id=1, replica_groups=mesh['z'=16,'h'=2,'mp'=16] {'z'}, dimensions={0} | all-to-all | bytes 655360 | tf_op jit(solution)/shard_map/all_to_all | solution.py:231
  117.7 1.7 %copy-done.2 = bf16[1536,768]{1,0:T(8,128)(2,1)S(1)} copy-done((bf16[1536,768]{1,0:T(8,128)(2,1)S(1)}, bf16[1536,768]{1,0:T(8,128)(2,1)}, u32[]{:S(2)}) %copy-start.2) | copy-done | bytes 2359320
  119.3 2.2 %spread.1 = bf16[32,48,128]{2,1,0:T(8,128)(2,1)} custom-call(s32[3]{0:T(128)S(1)} %pad_add_fusion.pos_ref, bf16[16,80,128]{2,1,0:T(8,128)(2,1)S(1)} %all_to_all.25.y_ref, f32[8,128]{1,0:T(8,128)S(1)} %pad_convert_fusion.pv_ref, bf16[1536,768]{1,0:T(8,128)(2,1)S(1)} %copy-done.2), custom_call_target="tpu_custom_call" | custom-call | tf_op jit(solution)/shard_map/spread/pallas_call | solution.py:232
  121.5 15.2 %all-to-all-start.4 = ((bf16[32,48,128]{2,1,0:T(8,128)(2,1)}), bf16[32,48,128]{2,1,0:T(8,128)(2,1)S(1)}, u32[]{:S(2)}, u32[]{:S(2)}) async-start(bf16[32,48,128]{2,1,0:T(8,128)(2,1)} %spread.1), calls=%async_computation.4 | async-start | bytes 786432 | tf_op jit(solution)/shard_map/all_to_all | solution.py:241
  136.7 0.0 copy-done.5
  136.7 0.3 fusion.9
  137.0 0.0 copy-start.8
  137.0 0.0 copy-start.9
  137.0 0.1 copy.48
  137.1 0.1 copy.49
  137.2 0.1 copy.50
  137.3 0.1 copy.51
  137.4 0.3 copy-done.8
  137.7 0.0 copy-done.9
  137.7 1.8 %pad_maximum_fusion = bf16[4,3,256,384]{3,2,1,0:T(8,128)(2,1)} fusion(bf16[1,3,256,384]{3,2,1,0:T(8,128)(2,1)S(1)} %bitcast.46, bf16[1,3,256,384]{3,2,1,0:T(8,128)(2,1)S(1)} %bitcast.45, bf16[1,3,256,384]{3,2,1,0:T(8,128)(2,1)S(1)} %bitcast.44, bf16[1,3,256,384]{3,2,1,0:T(8,128)(2,1)S(1)} %bitcast.43), kind=kLoop, calls=%fused_computation | loop fusion | flops 3538944 | bytes 4718592 | tf_op jit(solution)/shard_map/stack | solution.py:248
  139.5 7.5 %all-to-all-done.4.r_ref = bf16[32,48,128]{2,1,0:T(8,128)(2,1)S(1)} async-done(((bf16[32,48,128]{2,1,0:T(8,128)(2,1)}), bf16[32,48,128]{2,1,0:T(8,128)(2,1)S(1)}, u32[]{:S(2)}, u32[]{:S(2)}) %all-to-all-start.4) | async-done | bytes 393248 | tf_op jit(solution)/shard_map/all_to_all | solution.py:241
  147.0 1.7 %copy-done.1 = bf16[4,3,256,384]{3,2,1,0:T(8,128)(2,1)S(1)} copy-done((bf16[4,3,256,384]{3,2,1,0:T(8,128)(2,1)S(1)}, bf16[4,3,256,384]{3,2,1,0:T(8,128)(2,1)}, u32[]{:S(2)}) %copy-start.1) | copy-done | bytes 2359320
  148.7 1.3 decode.1
  (10 shorter events, 0.1 us)
Async XLA Ops:
  0.0 71.6 %copy-start = (bf16[256,5120]{1,0:T(8,128)(2,1)S(1)}, bf16[256,5120]{1,0:T(8,128)(2,1)}, u32[]{:S(2)}) copy-start(bf16[256,5120]{1,0:T(8,128)(2,1)} %param.21) | copy-start | bytes 7864324
  0.0 12.2 %copy-start.6 = (bf16[128,256]{1,0:T(8,128)(2,1)S(1)}, bf16[128,256]{1,0:T(8,128)(2,1)}, u32[]{:S(2)}) copy-start(bf16[128,256]{1,0:T(8,128)(2,1)} %param.14) | copy-start | bytes 196612
  2.0 23.3 %all-to-all-start.2 = ((bf16[16,320,64]{1,2,0:T(8,128)(2,1)}), bf16[16,320,64]{1,2,0:T(8,128)(2,1)S(1)}, u32[]{:S(2)}, u32[]{:S(2)}) async-start(bf16[16,320,64]{1,2,0:T(8,128)(2,1)} %broadcast_in_dim.28), calls=%async_computation.2 | async-start | bytes 1572864 | tf_op jit(solution)/shard_map/all_to_all | solution.py:214
  25.3 1.0 copy-start.4
  26.3 28.0 %all-to-all-start = ((bf16[8,8,16,128]{3,2,1,0:T(8,128)(2,1)}), bf16[8,8,16,128]{3,2,1,0:T(8,128)(2,1)S(1)}, u32[]{:S(2)}, u32[]{:S(2)}) async-start(bf16[8,8,16,128]{3,2,1,0:T(8,128)(2,1)} %bitcast.52), calls=%async_computation | async-start | bytes 524288 | tf_op jit(solution)/shard_map/all_to_all | solution.py:207
  43.0 23.4 %copy-start.7 = (bf16[2,2,4,16]{3,2,1,0:T(4,128)(2,1)S(1)}, bf16[2,2,4,16]{3,2,1,0:T(4,128)(2,1)}, u32[]{:S(2)}) copy-start(bf16[2,2,4,16]{3,2,1,0:T(4,128)(2,1)} %param.23) | copy-start | bytes 1540
  55.4 35.9 %all-to-all-start.1 = ((bf16[8,528,128]{2,1,0:T(8,128)(2,1)}), bf16[8,528,128]{2,1,0:T(8,128)(2,1)}, u32[]{:S(2)}, u32[]{:S(2)}) async-start(bf16[8,528,128]{2,1,0:T(8,128)(2,1)} %bitcast.42), calls=%async_computation.1 | async-start | bytes 2162688 | tf_op jit(solution)/shard_map/all_to_all | solution.py:212
  66.6 24.7 %copy-start.3 = (s32[4,4]{1,0:T(4,128)S(1)}, s32[4,4]{1,0:T(4,128)}, u32[]{:S(2)}) copy-start(s32[4,4]{1,0:T(4,128)} %fm_ref.1) | copy-start | bytes 196
  99.5 37.2 %copy-start.5 = (bf16[3,3,3,16,384]{4,3,2,1,0:T(8,128)(2,1)S(1)}, bf16[3,3,3,16,384]{4,3,2,1,0:T(8,128)(2,1)}, u32[]{:S(2)}) copy-start(bf16[3,3,3,16,384]{4,3,2,1,0:T(8,128)(2,1)} %param.24) | copy-start | bytes 995332
  117.7 1.7 %copy-start.2 = (bf16[1536,768]{1,0:T(8,128)(2,1)S(1)}, bf16[1536,768]{1,0:T(8,128)(2,1)}, u32[]{:S(2)}) copy-start(bf16[1536,768]{1,0:T(8,128)(2,1)} %constant.25.clone.pick_ref) | copy-start | bytes 7077892
  121.5 25.5 %all-to-all-start.4 = ((bf16[32,48,128]{2,1,0:T(8,128)(2,1)}), bf16[32,48,128]{2,1,0:T(8,128)(2,1)S(1)}, u32[]{:S(2)}, u32[]{:S(2)}) async-start(bf16[32,48,128]{2,1,0:T(8,128)(2,1)} %spread.1), calls=%async_computation.4 | async-start | bytes 786432 | tf_op jit(solution)/shard_map/all_to_all | solution.py:241
  137.0 0.7 copy-start.8
  137.0 0.7 copy-start.9
  147.0 1.7 %copy-start.1 = (bf16[4,3,256,384]{3,2,1,0:T(8,128)(2,1)S(1)}, bf16[4,3,256,384]{3,2,1,0:T(8,128)(2,1)}, u32[]{:S(2)}) copy-start(bf16[4,3,256,384]{3,2,1,0:T(8,128)(2,1)} %pad_maximum_fusion) | copy-start | bytes 7077892

commit v2 on v1

v2 whole, which is shorter than its diff:
```python
import functools
import math

import jax
import jax.numpy as jnp
from jax import lax
from jax.experimental import pallas as pl
from jax.experimental.pallas import tpu as pltpu
from jax.sharding import Mesh, PartitionSpec as P

HD = 128
LATC = 16
CH = 384
FR = 4
NZ = 16
NEG = -1e30
C2 = math.log2(math.e) / math.sqrt(HD)
F32 = jnp.float32
BF16 = jnp.bfloat16
FAR = [[(4 * j + i) * 2 + k for j in range(4) for k in range(2)] for i in range(4)]
NT = (((1,), (1,)), ((), ()))


def dot_nt(a, b):
    return lax.dot_general(a, b, NT, preferred_element_type=F32)


def pack_kernel(
    h, len_ref, q_hbm, ck_hbm, sk_hbm, cv_hbm, sv_hbm, keep_ref, give_ref, qo_ref, buf, sems
):
    copies = []
    for n, ref in enumerate((ck_hbm, sk_hbm, cv_hbm, sv_hbm, q_hbm)):
        copies.append(pltpu.make_async_copy(ref, buf.at[n], sems.at[n]))
        copies[n].start()
    first = h[0] == 0
    filled = (jnp.zeros((16, HD), F32) + len_ref[0].astype(F32)).astype(BF16)
    keep_ref[512:528] = filled
    give_ref[512:528] = filled
    for n in range(4):
        copies[n].wait()
        one, two = buf[n, :, 0:HD], buf[n, :, HD : 2 * HD]
        keep_ref[128 * n : 128 * n + 128] = jnp.where(first, one, two)
        give_ref[128 * n : 128 * n + 128] = jnp.where(first, two, one)
    copies[4].wait()
    for k in range(2):
        for b in range(8):
            for r in range(2):
                part = buf[4, 64 * r + 8 * b : 64 * r + 8 * b + 8, HD * k : HD * k + HD]
                for j in range(4):
                    qo_ref[2 * j + k, b, 8 * r : 8 * r + 8] = part


def pair_kernel(pos_ref, keep_ref, got_ref, hw_ref, ow_hbm, kv_ref, ow_ref, full_ref, sem):
    copy = pltpu.make_async_copy(ow_hbm.at[pl.ds(pos_ref[1] * HD, HD)], ow_ref, sem)
    copy.start()
    kv_ref[0, 0:528] = keep_ref[...]
    kv_ref[1, 0:528] = got_ref[...]
    full_ref[...] = jnp.zeros_like(full_ref)
    share = 80 * (pos_ref[0] % 4)
    for m in range(16):
        full_ref[pl.ds(pl.multiple_of(320 * m + share, 16), 80)] = hw_ref[m]
    copy.wait()
    both = jnp.dot(ow_ref[...], full_ref[...], preferred_element_type=F32)
    both = both.T.astype(BF16)
    for k in range(2):
        kv_ref[k, 528:560] = both[32 * k : 32 * k + 32]


def attend_kernel(
    fm_ref,
    pos_ref,
    q_ref,
    kv0_ref,
    kv1_ref,
    kv2_ref,
    kv3_ref,
    prev_ref,
    out_ref,
    pt_ref,
    level_ref,
):
    z, core = pos_ref[0], pos_ref[2] % 2
    planes = (z, z + NZ - 1, z + 1, z + NZ - 2 + 4 * core)
    lane = lax.broadcasted_iota(jnp.int32, (1, HD), 1)
    row_frame = lax.broadcasted_iota(jnp.int32, (128, 1), 0) // 32
    sources = []
    both = jnp.zeros((64, HD), F32)
    for kv_ref, plane in zip((kv0_ref, kv1_ref, kv2_ref, kv3_ref), planes):
        frame = (plane % NZ) // 4
        block_bias = jnp.zeros((128, 1), F32)
        for f in range(FR):
            here = jnp.where(fm_ref[f, frame] == 1, 0.0, NEG)
            block_bias = jnp.where(row_frame == f, here, block_bias)
        block_bias = jnp.broadcast_to(block_bias, (128, 128))
        both = both + jnp.concatenate([kv_ref[0, 528:560], kv_ref[1, 528:560]], 0).astype(F32)
        for k in range(2):
            filled = kv_ref[k, 512:528, :].astype(F32)[0:1]
            cache_bias = jnp.where(lane.astype(F32) < filled, 0.0, NEG)
            sources.append((kv_ref, k, cache_bias, block_bias))
    both = both.astype(BF16)
    part = lax.broadcasted_iota(jnp.int32, (8, 128), 0)

    def block(b, carry):
        q = q_ref[:, b].reshape(128, HD)
        scores = []
        for kv_ref, k, cache_bias, block_bias in sources:
            raw = dot_nt(q, kv_ref[k, 0:256, :]) * C2
            bias = jnp.concatenate(
                [jnp.broadcast_to(cache_bias, (128, 128)), block_bias], axis=1
            )
            scores.append(raw + bias)
        top = functools.reduce(jnp.maximum, scores)
        top = jnp.max(top, axis=1, keepdims=True)
        total = jnp.zeros((128, 256), F32)
        acc = jnp.zeros((128, HD), F32)
        for score, (kv_ref, k, _, _) in zip(scores, sources):
            weights = jnp.exp2(score - top)
            total = total + weights
            acc = acc + jnp.dot(
                weights.astype(BF16), kv_ref[k, 256:512, :], preferred_element_type=F32
            )
        total = jnp.sum(total, axis=1, keepdims=True)
        pt_ref[b] = dot_nt(both, (acc / total).astype(BF16))
        level = jnp.broadcast_to(top + jnp.log2(total), (128, 128)).T[0:8]
        high = level.astype(BF16).astype(F32)
        mid = (level - high).astype(BF16).astype(F32)
        low = level - high - mid
        level_ref[b] = jnp.where(
            part == 0, high, jnp.where(part == 1, mid, jnp.where(part == 2, low, 0.0))
        )
        return carry

    lax.fori_loop(0, 8, block, 0)
    ship(prev_ref, pt_ref, level_ref, out_ref)


def slots(odd, n):
    at = lax.broadcasted_iota(jnp.int32, (128, 128), 0)
    to = lax.broadcasted_iota(jnp.int32, (128, 128), 1)
    free = 5 - 4 * odd
    one = (2 * n + 3 * odd) if n < 2 else (4 - 4 * odd)
    two = (2 * n + 1 + 3 * odd) if n < 2 else 7
    hit = (at % 8 == free) & (to % 8 == one) | (at % 8 == free + 1) & (to % 8 == two)
    return jnp.where((at // 8 == to // 8) & hit, 1.0, 0.0).astype(BF16)


def ship(prev_ref, pt_ref, level_ref, out_ref):
    rims = []
    for side in range(2):
        for f in range(2):
            rims += [prev_ref[f, a, 3 * side : 3 * side + 1, :].astype(F32) for a in range(2)]
    rims = [jnp.concatenate(rims[2 * n : 2 * n + 2], axis=1) for n in range(4)]
    rims = jnp.concatenate(rims + [jnp.zeros((4, 32), F32)], axis=0).astype(BF16)
    column = lax.broadcasted_iota(jnp.int32, (64, 128), 1) % 8
    few = column[0:8]
    item = lax.broadcasted_iota(jnp.int32, (32, 128), 0)
    to = lax.broadcasted_iota(jnp.int32, (32, 128), 1)
    for odd in range(2):
        move = to == 8 * (item // 2) + item % 2 + 5 - 4 * odd
        edge = jnp.dot(rims, jnp.where(move, 1.0, 0.0).astype(BF16), preferred_element_type=F32)
        merged = []
        for b in range(8):
            own, beside = level_ref[b], level_ref[min(max(b - 1 + 2 * odd, 0), 7)]
            merged.append(jnp.where(few == 7 - 7 * odd, beside, own).astype(BF16))
        merged = jnp.concatenate(merged, axis=0)
        tails = [dot_nt(merged, slots(odd, n)) for n in range(3)]
        for b in range(8):
            keep = (column >= 3) if odd else (column <= 4)
            chunk = jnp.where(keep, pt_ref[b], 0.0)
            if 0 <= b - 1 + 2 * odd < 8:
                chunk = jnp.where(column == 7 - 7 * odd, pt_ref[b - 1 + 2 * odd], chunk)
            tail = [t[8 * b : 8 * b + 8] for t in tails] + [edge]
            tail = jnp.concatenate(tail + [jnp.zeros((32, 128), F32)], axis=0)
            out_ref[2 * b + odd] = (chunk + tail).astype(BF16)


def spread_kernel(pos_ref, y_ref, prev_ref, out_ref, rows_ref):
    own = []
    for c in range(2):
        for f in range(2):
            parts = [
                prev_ref[f, a, 2 * c + b : 2 * c + b + 1, :].astype(F32)
                for a in range(2)
                for b in range(2)
            ]
            own.append(jnp.concatenate([jnp.zeros((1, 64), F32)] + parts, axis=1))
    own = jnp.concatenate(own + [jnp.zeros((4, 128), F32)], axis=0).astype(BF16)
    z, h, m = pos_ref[0], pos_ref[1], pos_ref[2]
    odd = z % 2
    to = lax.broadcasted_iota(jnp.int32, (128, 128), 0)
    at = lax.broadcasted_iota(jnp.int32, (128, 128), 1)
    cell = 2 * ((to // 16) % 2) + (to // 4) % 4 + 7 + 4 * odd
    pick = (at // 32 == to % 4) & ((at // 8) % 4 == to // 32) & (at % 8 == cell % 8)
    pick = jnp.where(pick, 1.0, 0.0).astype(BF16)
    to = lax.broadcasted_iota(jnp.int32, (32, 8), 0)
    item = lax.broadcasted_iota(jnp.int32, (32, 8), 1)
    cell_to = 2 * (to // 16) + (to // 4) % 4
    place = (item < 4) & (cell_to == 2 * h + item // 2 + 1) & (to % 4 == item % 2)
    place = jnp.where(place, 1.0, 0.0).astype(BF16)
    earlier = jnp.dot(place, own, preferred_element_type=F32)
    at = lax.broadcasted_iota(jnp.int32, (128, 128), 0)
    to128 = lax.broadcasted_iota(jnp.int32, (128, 128), 1)
    slot = at % 8 - (5 - 4 * odd)
    value = 2 * (at // 8) + slot
    for side in range(2):
        source = jnp.maximum(z - 1, 0) if side == 0 else jnp.minimum(z + 1, NZ - 1)
        there = (z > 0) & (h == 1) if side == 0 else (z < NZ - 1) & (h == 0)
        goal = 64 + 32 * (value // 16) + value % 16 + (16 if side == 0 else 0)
        move = (slot >= 0) & (slot < 2) & (to128 == goal)
        move = jnp.where(move, 1.0, 0.0).astype(BF16)
        rim = jnp.dot(y_ref[source, 16:32], move, preferred_element_type=F32)[8:16]
        rim = jnp.where(there, rim, 0.0).astype(BF16)
        place = (item // 2 == 1 - side) & (item < 4) & (cell_to == 5 * side) & (to % 4 == item % 2)
        place = jnp.where(place, 1.0, 0.0).astype(BF16)
        earlier = earlier + jnp.dot(place, rim, preferred_element_type=F32)
    tails = [[y_ref[n, 0:16], y_ref[n, 16:32]] for n in range(NZ)]
    stacked = jnp.concatenate([t[0] for t in tails], axis=0)
    both = [jnp.where(odd == 1, slots(1, n), slots(0, n)) for n in range(3)]
    first = jnp.dot(stacked, both[0], preferred_element_type=F32)
    second = jnp.dot(stacked, both[1], preferred_element_type=F32)
    stacked = jnp.concatenate([t[1] for t in tails], axis=0)
    third = jnp.dot(stacked, both[2], preferred_element_type=F32)
    for r in range(4):
        levels = []
        for g in range(4):
            n = 16 * (4 * g + r)
            tail = first[n : n + 8] + second[n + 8 : n + 16] + third[n : n + 8]
            levels.append(tail[0:1] + tail[1:2] + tail[2:3])
        top = jnp.maximum(jnp.maximum(levels[0], levels[1]), jnp.maximum(levels[2], levels[3]))
        shares = [jnp.exp2(level - top) for level in levels]
        whole = shares[0] + shares[1] + shares[2] + shares[3]
        value = jnp.zeros((64, 128), F32)
        for g in range(4):
            value = value + (shares[g] / whole) * y_ref[4 * g + r].astype(F32)
        value = jnp.concatenate([value, jnp.zeros((64, 128), F32)], axis=0).astype(BF16)
        moved = dot_nt(pick, value)
        for i in range(4):
            row = 4 * r + i
            rows_ref[row] = moved[32 * i : 32 * i + 32] + jnp.where(m == row, earlier, 0.0)
    below = lax.broadcasted_iota(jnp.int32, (32, 128), 1) % 64 < 32
    for row in range(16):
        under = rows_ref[row + 1] if row < 15 else jnp.zeros((32, 128), F32)
        over = rows_ref[row - 1] if row > 0 else jnp.zeros((32, 128), F32)
        beside = jnp.where(below, under, over).astype(BF16)
        own = rows_ref[row].astype(BF16)
        for k in range(2):
            out_ref[16 * k + row, 0:16] = own[16 * k : 16 * k + 16]
            out_ref[16 * k + row, 16:32] = beside[16 * k : 16 * k + 16]


def decode_kernel(r_ref, w_ref, bias_ref, gain_ref, out_ref, z_ref, taps_ref):
    nothing = jnp.zeros((16, CH), BF16)
    for a in range(2):
        for b in range(2):
            for dt in range(3):
                for k in range(16):
                    i, j, pa, pb = k // 8, k // 4 % 2, k // 2 % 2, k % 2
                    dy, dx = 2 * i + pa + a - 1, 2 * j + pb + b - 1
                    inside = 0 <= dy < 3 and 0 <= dx < 3
                    tap = w_ref[dt, dy, dx] if inside else nothing
                    taps_ref[a, b, dt, 16 * k : 16 * k + 16] = tap
    total = jnp.zeros((32, 128), F32)
    for s in range(32):
        total = total + r_ref[s].astype(F32)
    total = total.astype(BF16).astype(F32)
    z_ref[...] = jnp.zeros_like(z_ref)
    for dr in range(2):
        for cc in range(4):
            at = dr * 16 + cc * 4
            z_ref[dr, cc * 6 + 2 : cc * 6 + 6] = total[at : at + 4, 0:64]
            z_ref[dr, cc * 6 : cc * 6 + 2] = total[at : at + 2, 64:128]
    for a in range(2):
        for b in range(2):
            conv = jnp.zeros((16, CH), F32)
            for dt in range(3):
                pieces = []
                for i in range(2):
                    for j in range(2):
                        start = (b + j) * 6 + dt
                        pieces.append(z_ref[(a + i + 1) % 2, start : start + 16])
                lhs = jnp.concatenate(pieces, axis=1).astype(BF16)
                conv = conv + jnp.dot(lhs, taps_ref[a, b, dt], preferred_element_type=F32)
            conv = conv + bias_ref[...].reshape(1, CH)
            meansq = jnp.mean(conv * conv, axis=1, keepdims=True)
            normed = conv * lax.rsqrt(meansq + 1e-06) * gain_ref[...].reshape(1, CH)
            decoded = (normed / (1.0 + jnp.exp(-normed))).astype(BF16)
            for c in range(2):
                for f in range(FR):
                    out_ref[f, a, 2 * c + b] = decoded[c * 6 + f]


def body(
    queries,
    stretch_keys,
    stretch_values,
    cache_keys,
    cache_values,
    cache_lengths,
    frame_mask,
    out_weight,
    head_weight,
    previous_latent,
    conv_weight,
    conv_bias,
    norm_gain,
):
    z, h, m = lax.axis_index("z"), lax.axis_index("h"), lax.axis_index("mp")
    pos = jnp.stack([z, h, m]).astype(jnp.int32)
    vmem = pl.BlockSpec(memory_space=pltpu.VMEM)
    whole = pl.BlockSpec()
    hbm = pl.BlockSpec(memory_space=pltpu.HBM)
    smem = pl.BlockSpec(memory_space=pltpu.SMEM)

    def call(kernel, name, outs, specs, scratch=(), limit=16, **kw):
        shapes = [jax.ShapeDtypeStruct(shape, kind) for shape, kind in outs]
        return pl.pallas_call(
            kernel,
            out_shape=shapes if len(shapes) > 1 else shapes[0],
            in_specs=specs,
            out_specs=[vmem] * len(shapes) if len(shapes) > 1 else vmem,
            scratch_shapes=scratch,
            compiler_params=pltpu.CompilerParams(vmem_limit_bytes=limit * 1024 * 1024),
            name=name,
            **kw,
        )

    keep, give, q = call(
        pack_kernel,
        "pack",
        (((528, HD), BF16), ((528, HD), BF16), ((8, 8, 16, HD), BF16)),
        [smem] * 2 + [hbm] * 5,
        [pltpu.VMEM((5, 128, 2 * HD), BF16), pltpu.SemaphoreType.DMA((5,))],
        limit=60,
    )(h.reshape(1), cache_lengths, queries, cache_keys, stretch_keys, cache_values, stretch_values)
    got = lax.ppermute(give, "h", [(0, 1), (1, 0)])
    hw = lax.dynamic_slice_in_dim(head_weight, 80 * (z % 4), 80, 0)
    hw = lax.all_to_all(jnp.broadcast_to(hw[None], (16, 80, 64)), "mp", 0, 0, tiled=True)
    q, hw = lax.optimization_barrier((q, hw))
    q = lax.all_to_all(q, ("z", "h"), 0, 0, tiled=True, axis_index_groups=FAR)
    kv = call(
        pair_kernel,
        "pair",
        (((2, 560, HD), BF16),),
        [smem] + [vmem] * 3 + [hbm],
        [pltpu.VMEM((HD, 5120), BF16), pltpu.VMEM((5120, 64), BF16), pltpu.SemaphoreType.DMA],
        limit=32,
        cost_estimate=pl.CostEstimate(flops=10**11, bytes_accessed=10**6, transcendentals=0),
    )(pos, keep, got, hw, out_weight)
    up = lax.ppermute(kv, "z", [(i, (i + 1) % NZ) for i in range(NZ)])
    down = lax.ppermute(kv, "z", [((i + 1) % NZ, i) for i in range(NZ)])
    two = lax.ppermute(
        kv,
        ("z", "mp"),
        [(16 * i + j, 16 * ((i + (2 if j % 2 == 0 else 14)) % NZ) + j) for i in range(NZ) for j in range(16)],
    )
    partial = call(
        attend_kernel,
        "attend",
        (((NZ, 64, 128), BF16),),
        [smem] * 2 + [vmem] * 6,
        [pltpu.VMEM((8, 64, 128), F32), pltpu.VMEM((8, 8, 128), F32)],
        cost_estimate=pl.CostEstimate(flops=10**10, bytes_accessed=10**6, transcendentals=10**6),
    )(frame_mask, pos, q, kv, up, down, two, previous_latent)
    partial = lax.all_to_all(partial, "z", 0, 0, tiled=True)
    spread = call(spread_kernel, "spread", (((32, 32, 128), BF16),), [smem, vmem, whole], [pltpu.VMEM((16, 32, 128), F32)])(
        pos, partial, previous_latent
    )
    spread = lax.all_to_all(spread, ("h", "mp"), 0, 0, tiled=True)
    return call(
        decode_kernel,
        "decode",
        (((FR, 2, 4, CH), BF16),),
        [vmem] + [whole] * 3,
        [pltpu.VMEM((2, 40, 64), F32), pltpu.VMEM((2, 2, 3, 256, CH), BF16)],
    )(spread, conv_weight, conv_bias, norm_gain)


def solution(mesh):
    fine = Mesh(mesh.devices.reshape(NZ, 2, 16), ("z", "h", "mp"))
    seq = ("z", "h")
    return jax.shard_map(
        body,
        mesh=fine,
        in_specs=(
            P(seq, "mp"),
            P(seq, "mp"),
            P(seq, "mp"),
            P(seq, "mp"),
            P(seq, "mp"),
            P(seq),
            P(),
            P("mp", None),
            P("mp", None),
            P(None, "mp", seq, None),
            P(),
            P(),
            P(),
        ),
        out_specs=P(None, "mp", seq, None),
        check_vma=False,
    )
```

time: 151 us -> 114 us (0.75)
  waiting for transfers between devices: 48.9 us -> 13.2 us
  blocking collectives: 18.1 us -> 43.3 us
  starting transfers between devices: 50 us -> 37.5 us
  local copies, waits for them, and re-layouts: 16.9 us -> 4.49 us
  Pallas kernels: 11.7 us -> 13.7 us
  other arithmetic: 1.87 us -> 0.08 us
  matrix products: 1.66 us -> 0 us
    all_to_all x3 -> x1, waiting for transfers between devices: 38.6 us -> 2.75 us  [body(): lax.all_to_all(jnp.broadcast_to(hw[None], (16, 80, 64)), 'mp', 0, 0, tile...]
    all_to_all x3 -> x1, starting transfers between devices: 36.5 us -> 10.2 us  [body(): lax.all_to_all(jnp.broadcast_to(hw[None], (16, 80, 64)), 'mp', 0, 0, tile...]
    all_to_all x0 -> x1, blocking collectives: none -> 19.6 us  [body(): spread = lax.all_to_all(spread, ('h', 'mp'), 0, 0, tiled=True)]
    ppermute x0 -> x4, starting transfers between devices: none -> 13.7 us  [the longest x1 6.52 us: body(): lax.ppermute(kv, ('z', 'mp'), [(16 * i + j, 16 * ((i + (2 if j % 2 == 0 e...]
    ppermute x0 -> x4, waiting for transfers between devices: none -> 10.5 us  [the longest x1 4.95 us: body(): lax.ppermute(kv, ('z', 'mp'), [(16 * i + j, 16 * ((i + (2 if j % 2 == 0 e...]
    all_to_all x1, waiting for transfers between devices: 10.3 us -> 0.01 us  [body(): q = lax.all_to_all(q, ('z', 'h'), 0, 0, tiled=True, axis_index_groups=FAR)]
    all_to_all x1, blocking collectives: 18.1 us -> 23.7 us  [body(): partial = lax.all_to_all(partial, 'z', 0, 0, tiled=True)]
    unnamed x24 -> x16, local copies, waits for them, and re-layouts: 7.27 us -> 3.47 us
  transfers between devices with their start and end apart: 4 -> 6, of which waited for: 4 -> 4; matrix products, arithmetic and copies ran while one was open for 8% -> 0% of each run, Pallas kernels for 0% -> 3%
where the time goes in v2:
time: 114 us; the launch traced here: 113 us
  blocking collectives  43.3 us (38%)
  starting transfers between devices  37.5 us (33%)
  Pallas kernels  13.7 us (12%)
  waiting for transfers between devices  13.2 us (12%)
  local copies, waits for them, and re-layouts  4.49 us (4%)
    all_to_all x1, blocking collectives, body(): partial = lax.all_to_all(partial, 'z', 0, 0, tiled=True)  23.7 us
    all_to_all x1, blocking collectives, body(): spread = lax.all_to_all(spread, ('h', 'mp'), 0, 0, tiled=True)  19.6 us
    all_to_all x1, starting transfers between devices, body(): q = lax.all_to_all(q, ('z', 'h'), 0, 0, tiled=True, axis_index_groups=FAR)  13.6 us
    all_to_all x1, starting transfers between devices, body(): lax.all_to_all(jnp.broadcast_to(hw[None], (16, 80, 64)), 'mp', 0, 0, tile...  10.2 us
    pallas_call x1, Pallas kernels, body(): call(attend_kernel, 'attend', (((NZ, 64, 128), BF16),), [smem] * 2 + [vme...  7.82 us
    ppermute x1, starting transfers between devices, body(): lax.ppermute(kv, ('z', 'mp'), [(16 * i + j, 16 * ((i + (2 if j % 2 == 0 e...  6.52 us
    ppermute x1, waiting for transfers between devices, body(): lax.ppermute(kv, ('z', 'mp'), [(16 * i + j, 16 * ((i + (2 if j % 2 == 0 e...  4.95 us
    ppermute x1, waiting for transfers between devices, body(): down = lax.ppermute(kv, 'z', [((i + 1) % NZ, i) for i in range(NZ)])  4.82 us
  transfers between devices with their start and end apart: 6, of which 4 were waited for; matrix products, arithmetic and copies ran while one was open for 0% of the time, Pallas kernels for 3%

profile of v2, /device:TPU:1, one launch (start us, length us, event | category | flops | bytes accessed | tf_op | source)
XLA Modules:
  0.0 113.1 jit_solution(12983653401475412294)
XLA Ops:
  0.0 0.0 copy-start
  0.0 0.8 copy-done
  0.8 0.1 constant_dynamic-slice_fusion
  0.9 0.7 broadcast_in_dim.2
  1.6 10.2 %all-to-all-start = ((bf16[16,80,64]{1,2,0:T(8,128)(2,1)}), bf16[16,80,64]{1,2,0:T(8,128)(2,1)S(1)}, u32[]{:S(2)}, u32[]{:S(2)}) async-start(bf16[16,80,64]{1,2,0:T(8,128)(2,1)} %broadcast_in_dim.2), calls=%async_computation | async-start | bytes 524288 | tf_op jit(solution)/shard_map/all_to_all | solution.py:337
  12.5 1.8 %pack.1 = (bf16[528,128]{1,0:T(8,128)(2,1)}, bf16[528,128]{1,0:T(8,128)(2,1)}, bf16[8,8,16,128]{3,2,1,0:T(8,128)(2,1)}) custom-call(s32[1]{0:T(128)} %bitcast.1.h, s32[1]{0:T(128)S(6)} %copy.16.len_ref, bf16[128,256]{1,0:T(8,128)(2,1)} %q_hbm.1, bf16[128,256]{1,0:T(8,128)(2,1)} %ck_hbm.1, bf16[128,256]{1,0:T(8,128)(2,1)} %sk_hbm.1, bf16[128,256]{1,0:T(8,128)(2,1)} %cv_hbm.1, ...), custom_call_target="tpu_custom_call" | custom-call | tf_op jit(solution)/shard_map/pack/pallas_call | solution.py:327
  14.3 1.9 %collective-permute-start = (bf16[528,128]{1,0:T(8,128)(2,1)}, bf16[528,128]{1,0:T(8,128)(2,1)S(1)}, u32[]{:S(2)}, u32[]{:S(2)}) collective-permute-start(bf16[528,128]{1,0:T(8,128)(2,1)} %get-tuple-element.13), channel_id=1, source_target_pairs={{0,16},{16,0},{1,17},{17,1},{2,18},{18,2},{3,19},{19,3},{4,20},{20... | collective-permute-start | bytes 405512 | tf_op jit(solution)/shard_map/ppermute | solution.py:335
  16.2 0.1 pad_add_fusion.pos_ref
  16.3 2.8 %all-to-all-done = bf16[16,80,64]{1,2,0:T(8,128)(2,1)S(1)} async-done(((bf16[16,80,64]{1,2,0:T(8,128)(2,1)}), bf16[16,80,64]{1,2,0:T(8,128)(2,1)S(1)}, u32[]{:S(2)}, u32[]{:S(2)}) %all-to-all-start) | async-done | bytes 163872 | tf_op jit(solution)/shard_map/all_to_all | solution.py:337
  19.1 13.6 %all-to-all-start.1 = ((bf16[8,8,16,128]{3,2,1,0:T(8,128)(2,1)}), bf16[8,8,16,128]{3,2,1,0:T(8,128)(2,1)S(1)}, u32[]{:S(2)}, u32[]{:S(2)}) async-start(bf16[8,8,16,128]{3,2,1,0:T(8,128)(2,1)} %get-tuple-element.11), calls=%async_computation.1 | async-start | bytes 524288 | tf_op jit(solution)/shard_map/all_to_all | solution.py:339
  32.7 0.2 copy.15.hw_ref
  32.9 0.0 collective-permute-done.got_ref
  32.9 0.0 copy-start.5
  32.9 1.7 %copy-done.5 = bf16[256,5120]{1,0:T(8,128)(2,1)S(1)} copy-done((bf16[256,5120]{1,0:T(8,128)(2,1)S(1)}, bf16[256,5120]{1,0:T(8,128)(2,1)}, u32[]{:S(2)}) %copy-start.5) | copy-done | bytes 2621464
  34.7 0.0 copy-start.6
  34.7 0.9 copy-done.6
  35.6 0.0 copy-start.2
  35.6 0.0 copy-start.7
  35.6 1.4 %pair.1.kv0_ref = bf16[2,560,128]{2,1,0:T(8,128)(2,1)S(1)} custom-call(s32[3]{0:T(128)S(1)} %pad_add_fusion.pos_ref, bf16[528,128]{1,0:T(8,128)(2,1)S(1)} %copy-done.6, bf16[528,128]{1,0:T(8,128)(2,1)S(1)} %collective-permute-done.got_ref, bf16[16,80,64]{2,1,0:T(8,128)(2,1)S(1)} %copy.15.hw_ref, bf16[256,5120]{1,0:T(8,128)(2,1)S(1)} %copy-done.5), custom_call_target="tpu_custom_call" | custom-call | flops 99999997952 | bytes 1000000 | tf_op jit(solution)/shard_map/pair/pallas_call | solution.py:340
  37.0 0.0 copy-start.1
  37.0 0.0 copy-start.3
  37.0 0.0 copy-start.4
  37.0 6.5 %collective-permute-start.3 = (bf16[2,560,128]{2,1,0:T(8,128)(2,1)S(1)}, bf16[2,560,128]{2,1,0:T(8,128)(2,1)S(1)}, u32[]{:S(2)}, u32[]{:S(2)}) collective-permute-start(bf16[2,560,128]{2,1,0:T(8,128)(2,1)S(1)} %pair.1.kv0_ref), channel_id=1, source_target_pairs={{0,64},{1,449},{2,66},{3,451},{4,68},{5,453},{6,70},{7,455},{8,72}... | collective-permute-start | bytes 860168 | tf_op jit(solution)/shard_map/ppermute | solution.py:351
  43.6 2.6 %collective-permute-start.2 = (bf16[2,560,128]{2,1,0:T(8,128)(2,1)S(1)}, bf16[2,560,128]{2,1,0:T(8,128)(2,1)S(1)}, u32[]{:S(2)}, u32[]{:S(2)}) collective-permute-start(bf16[2,560,128]{2,1,0:T(8,128)(2,1)S(1)} %pair.1.kv0_ref), channel_id=1, source_target_pairs={{32,0},{64,32},{96,64},{128,96},{160,128},{192,160},{224,192},{256... | collective-permute-start | bytes 860168 | tf_op jit(solution)/shard_map/ppermute | solution.py:350
  46.2 2.6 %collective-permute-start.1 = (bf16[2,560,128]{2,1,0:T(8,128)(2,1)S(1)}, bf16[2,560,128]{2,1,0:T(8,128)(2,1)S(1)}, u32[]{:S(2)}, u32[]{:S(2)}) collective-permute-start(bf16[2,560,128]{2,1,0:T(8,128)(2,1)S(1)} %pair.1.kv0_ref), channel_id=1, source_target_pairs={{0,32},{32,64},{64,96},{96,128},{128,160},{160,192},{192,224},{224... | collective-permute-start | bytes 860168 | tf_op jit(solution)/shard_map/ppermute | solution.py:349
  48.9 5.0 %collective-permute-done.3.kv3_ref = bf16[2,560,128]{2,1,0:T(8,128)(2,1)S(1)} collective-permute-done((bf16[2,560,128]{2,1,0:T(8,128)(2,1)S(1)}, bf16[2,560,128]{2,1,0:T(8,128)(2,1)S(1)}, u32[]{:S(2)}, u32[]{:S(2)}) %collective-permute-start.3) | collective-permute-done | bytes 286752 | tf_op jit(solution)/shard_map/ppermute | solution.py:351
  53.8 4.8 %collective-permute-done.2.kv2_ref = bf16[2,560,128]{2,1,0:T(8,128)(2,1)S(1)} collective-permute-done((bf16[2,560,128]{2,1,0:T(8,128)(2,1)S(1)}, bf16[2,560,128]{2,1,0:T(8,128)(2,1)S(1)}, u32[]{:S(2)}, u32[]{:S(2)}) %collective-permute-start.2) | collective-permute-done | bytes 286752 | tf_op jit(solution)/shard_map/ppermute | solution.py:350
  58.6 0.7 collective-permute-done.1.kv1_ref
  59.3 0.0 all-to-all-done.1.q_ref
  59.3 0.0 copy-done.2
  59.3 0.0 copy-done.7
  59.3 7.8 %attend.1 = bf16[16,64,128]{2,1,0:T(8,128)(2,1)S(1)} custom-call(s32[4,4]{1,0:T(4,128)S(1)} %copy-done.7, s32[3]{0:T(128)S(1)} %pad_add_fusion.pos_ref, bf16[8,8,16,128]{3,2,1,0:T(8,128)(2,1)S(1)} %all-to-all-done.1.q_ref, bf16[2,560,128]{2,1,0:T(8,128)(2,1)S(1)} %pair.1.kv0_ref, bf16[2,560,128]{2,1,0:T(8,128)(2,1)S(1)} %collective-permute-done.1.kv1_ref, ...), custom_call_target="tpu_custom_call" | custom-call | flops 10000000000 | bytes 1000000 | tf_op jit(solution)/shard_map/attend/pallas_call | solution.py:356
  67.2 23.7 %all_to_all.20.y_ref = bf16[16,64,128]{2,1,0:T(8,128)(2,1)S(1)} all-to-all(bf16[16,64,128]{2,1,0:T(8,128)(2,1)S(1)} %attend.1), channel_id=1, replica_groups=mesh['z'=16,'h'=2,'mp'=16] {'z'}, dimensions={0} | all-to-all | bytes 524288 | tf_op jit(solution)/shard_map/all_to_all | solution.py:364
  90.9 1.3 %spread.1 = bf16[32,32,128]{2,1,0:T(8,128)(2,1)S(1)} custom-call(s32[3]{0:T(128)S(1)} %pad_add_fusion.pos_ref, bf16[16,64,128]{2,1,0:T(8,128)(2,1)S(1)} %all_to_all.20.y_ref, bf16[2,2,4,16]{3,2,1,0:T(4,128)(2,1)S(1)} %copy-done.2), custom_call_target="tpu_custom_call" | custom-call | tf_op jit(solution)/shard_map/spread/pallas_call | solution.py:365
  92.2 19.6 %all_to_all.21.r_ref = bf16[32,32,128]{2,1,0:T(8,128)(2,1)S(1)} all-to-all(bf16[32,32,128]{2,1,0:T(8,128)(2,1)S(1)} %spread.1), channel_id=1, replica_groups=mesh['z'=16,'h'=2,'mp'=16] {'h','mp'}, dimensions={0} | all-to-all | bytes 524288 | tf_op jit(solution)/shard_map/all_to_all | solution.py:368
  111.8 0.0 copy-done.1
  111.8 0.0 copy-done.3
  111.8 0.0 copy-done.4
  111.8 1.3 %decode.1 = bf16[4,2,4,384]{3,2,1,0:T(4,128)(2,1)} custom-call(bf16[32,32,128]{2,1,0:T(8,128)(2,1)S(1)} %all_to_all.21.r_ref, bf16[3,3,3,16,384]{4,3,2,1,0:T(8,128)(2,1)S(1)} %copy-done.1, f32[384]{0:T(512)S(1)} %copy-done.3, f32[384]{0:T(512)S(1)} %copy-done.4), custom_call_target="tpu_custom_call" | custom-call | tf_op jit(solution)/shard_map/decode/pallas_call | solution.py:369
Async XLA Ops:
  0.0 0.8 copy-start
  1.6 17.4 %all-to-all-start = ((bf16[16,80,64]{1,2,0:T(8,128)(2,1)}), bf16[16,80,64]{1,2,0:T(8,128)(2,1)S(1)}, u32[]{:S(2)}, u32[]{:S(2)}) async-start(bf16[16,80,64]{1,2,0:T(8,128)(2,1)} %broadcast_in_dim.2), calls=%async_computation | async-start | bytes 524288 | tf_op jit(solution)/shard_map/all_to_all | solution.py:337
  14.3 18.6 %collective-permute-start = (bf16[528,128]{1,0:T(8,128)(2,1)}, bf16[528,128]{1,0:T(8,128)(2,1)S(1)}, u32[]{:S(2)}, u32[]{:S(2)}) collective-permute-start(bf16[528,128]{1,0:T(8,128)(2,1)} %get-tuple-element.13), channel_id=1, source_target_pairs={{0,16},{16,0},{1,17},{17,1},{2,18},{18,2},{3,19},{19,3},{4,20},{20... | collective-permute-start | bytes 405512 | tf_op jit(solution)/shard_map/ppermute | solution.py:335
  19.1 40.3 %all-to-all-start.1 = ((bf16[8,8,16,128]{3,2,1,0:T(8,128)(2,1)}), bf16[8,8,16,128]{3,2,1,0:T(8,128)(2,1)S(1)}, u32[]{:S(2)}, u32[]{:S(2)}) async-start(bf16[8,8,16,128]{3,2,1,0:T(8,128)(2,1)} %get-tuple-element.11), calls=%async_computation.1 | async-start | bytes 524288 | tf_op jit(solution)/shard_map/all_to_all | solution.py:339
  32.9 1.7 %copy-start.5 = (bf16[256,5120]{1,0:T(8,128)(2,1)S(1)}, bf16[256,5120]{1,0:T(8,128)(2,1)}, u32[]{:S(2)}) copy-start(bf16[256,5120]{1,0:T(8,128)(2,1)} %ow_hbm.1) | copy-start | bytes 7864324
  34.7 0.9 copy-start.6
  35.6 23.8 %copy-start.2 = (bf16[2,2,4,16]{3,2,1,0:T(4,128)(2,1)S(1)}, bf16[2,2,4,16]{3,2,1,0:T(4,128)(2,1)}, u32[]{:S(2)}) copy-start(bf16[2,2,4,16]{3,2,1,0:T(4,128)(2,1)} %prev_ref.3) | copy-start | bytes 1540
  35.6 23.8 %copy-start.7 = (s32[4,4]{1,0:T(4,128)S(1)}, s32[4,4]{1,0:T(4,128)}, u32[]{:S(2)}) copy-start(s32[4,4]{1,0:T(4,128)} %fm_ref.1) | copy-start | bytes 196
  37.0 74.8 %copy-start.1 = (bf16[3,3,3,16,384]{4,3,2,1,0:T(8,128)(2,1)S(1)}, bf16[3,3,3,16,384]{4,3,2,1,0:T(8,128)(2,1)}, u32[]{:S(2)}) copy-start(bf16[3,3,3,16,384]{4,3,2,1,0:T(8,128)(2,1)} %w_ref.1) | copy-start | bytes 995332
  37.0 74.8 %copy-start.3 = (f32[384]{0:T(512)S(1)}, f32[384]{0:T(512)}, u32[]{:S(2)}) copy-start(f32[384]{0:T(512)} %bias_ref.1) | copy-start | bytes 4612
  37.0 74.8 %copy-start.4 = (f32[384]{0:T(512)S(1)}, f32[384]{0:T(512)}, u32[]{:S(2)}) copy-start(f32[384]{0:T(512)} %gain_ref.1) | copy-start | bytes 4612
  37.0 16.8 %collective-permute-start.3 = (bf16[2,560,128]{2,1,0:T(8,128)(2,1)S(1)}, bf16[2,560,128]{2,1,0:T(8,128)(2,1)S(1)}, u32[]{:S(2)}, u32[]{:S(2)}) collective-permute-start(bf16[2,560,128]{2,1,0:T(8,128)(2,1)S(1)} %pair.1.kv0_ref), channel_id=1, source_target_pairs={{0,64},{1,449},{2,66},{3,451},{4,68},{5,453},{6,70},{7,455},{8,72}... | collective-permute-start | bytes 860168 | tf_op jit(solution)/shard_map/ppermute | solution.py:351
  43.6 15.1 %collective-permute-start.2 = (bf16[2,560,128]{2,1,0:T(8,128)(2,1)S(1)}, bf16[2,560,128]{2,1,0:T(8,128)(2,1)S(1)}, u32[]{:S(2)}, u32[]{:S(2)}) collective-permute-start(bf16[2,560,128]{2,1,0:T(8,128)(2,1)S(1)} %pair.1.kv0_ref), channel_id=1, source_target_pairs={{32,0},{64,32},{96,64},{128,96},{160,128},{192,160},{224,192},{256... | collective-permute-start | bytes 860168 | tf_op jit(solution)/shard_map/ppermute | solution.py:350
  46.2 13.1 %collective-permute-start.1 = (bf16[2,560,128]{2,1,0:T(8,128)(2,1)S(1)}, bf16[2,560,128]{2,1,0:T(8,128)(2,1)S(1)}, u32[]{:S(2)}, u32[]{:S(2)}) collective-permute-start(bf16[2,560,128]{2,1,0:T(8,128)(2,1)S(1)} %pair.1.kv0_ref), channel_id=1, source_target_pairs={{0,32},{32,64},{64,96},{96,128},{128,160},{160,192},{192,224},{224... | collective-permute-start | bytes 860168 | tf_op jit(solution)/shard_map/ppermute | solution.py:349

commit v3 on v2

v3 whole, which is shorter than its diff:
```python
import functools
import math

import jax
import jax.numpy as jnp
from jax import lax
from jax.experimental import pallas as pl
from jax.experimental.pallas import tpu as pltpu
from jax.sharding import Mesh, PartitionSpec as P

HD = 128
LATC = 16
CH = 384
FR = 4
NZ = 16
NEG = -1e30
C2 = math.log2(math.e) / math.sqrt(HD)
F32 = jnp.float32
BF16 = jnp.bfloat16
FAR = [[(4 * j + i) * 2 + k for j in range(4) for k in range(2)] for i in range(4)]
NT = (((1,), (1,)), ((), ()))


def dot_nt(a, b):
    return lax.dot_general(a, b, NT, preferred_element_type=F32)


def pack_kernel(
    len_hbm, q_hbm, ck_hbm, sk_hbm, cv_hbm, sv_hbm, keep_ref, give_ref, qo_ref, buf, len_ref, sems
):
    copies = []
    for n, ref in enumerate((ck_hbm, sk_hbm, cv_hbm, sv_hbm, q_hbm)):
        copies.append(pltpu.make_async_copy(ref, buf.at[n], sems.at[n]))
        copies[n].start()
    length = pltpu.make_async_copy(len_hbm, len_ref, sems.at[5])
    length.start()
    first = lax.axis_index("h") == 0
    length.wait()
    filled = (jnp.zeros((16, HD), F32) + len_ref[0].astype(F32)).astype(BF16)
    keep_ref[512:528] = filled
    give_ref[512:528] = filled
    for n in range(4):
        copies[n].wait()
        one, two = buf[n, :, 0:HD], buf[n, :, HD : 2 * HD]
        keep_ref[128 * n : 128 * n + 128] = jnp.where(first, one, two)
        give_ref[128 * n : 128 * n + 128] = jnp.where(first, two, one)
    copies[4].wait()
    for k in range(2):
        for b in range(8):
            for r in range(2):
                part = buf[4, 64 * r + 8 * b : 64 * r + 8 * b + 8, HD * k : HD * k + HD]
                for j in range(4):
                    qo_ref[2 * j + k, b, 8 * r : 8 * r + 8] = part


def pair_kernel(keep_ref, got_ref, hw_ref, ow_hbm, kv_ref, ow_ref, full_ref, sem):
    copy = pltpu.make_async_copy(ow_hbm.at[pl.ds(lax.axis_index("h") * HD, HD)], ow_ref, sem)
    copy.start()
    kv_ref[0, 0:528] = keep_ref[...]
    kv_ref[1, 0:528] = got_ref[...]
    full_ref[...] = jnp.zeros_like(full_ref)
    share = 80 * lax.rem(lax.axis_index("z"), 4)
    for m in range(16):
        full_ref[pl.ds(pl.multiple_of(320 * m + share, 16), 80)] = hw_ref[m]
    copy.wait()
    both = jnp.dot(ow_ref[...], full_ref[...], preferred_element_type=F32)
    both = both.T.astype(BF16)
    for k in range(2):
        for a in range(2):
            at = 32 * a + 16 * k
            kv_ref[k, 528 + 16 * a : 544 + 16 * a] = both[at : at + 16]


def attend_kernel(
    fm_ref,
    q_ref,
    kv0_ref,
    kv1_ref,
    kv2_ref,
    kv3_ref,
    prev_ref,
    out_ref,
    pt_ref,
    level_ref,
):
    z, core = lax.axis_index("z"), lax.rem(lax.axis_index("mp"), 2)
    planes = (z, z + NZ - 1, z + 1, z + NZ - 2 + 4 * core)
    lane = lax.broadcasted_iota(jnp.int32, (1, HD), 1)
    row_frame = lax.broadcasted_iota(jnp.int32, (256, 1), 0) % 128 // 32
    sources = []
    both = jnp.zeros((64, HD), F32)
    for kv_ref, plane in zip((kv0_ref, kv1_ref, kv2_ref, kv3_ref), planes):
        frame = (plane % NZ) // 4
        block_bias = jnp.zeros((256, 1), F32)
        for f in range(FR):
            here = jnp.where(fm_ref[f, frame] == 1, 0.0, NEG)
            block_bias = jnp.where(row_frame == f, here, block_bias)
        block_bias = jnp.broadcast_to(block_bias, (256, 128))
        both = both + jnp.concatenate([kv_ref[0, 528:560], kv_ref[1, 528:560]], 0).astype(F32)
        for k in range(2):
            filled = kv_ref[k, 512:528, :].astype(F32)[0:1]
            cache_bias = jnp.where(lane.astype(F32) < filled, 0.0, NEG)
            sources.append((kv_ref, k, cache_bias, block_bias))
    both = both.astype(BF16)
    part = lax.broadcasted_iota(jnp.int32, (8, 128), 0)

    def block(step, carry):
        q = jnp.concatenate([q_ref[:, 2 * step + i].reshape(128, HD) for i in range(2)], axis=0)
        scores = []
        for kv_ref, k, cache_bias, block_bias in sources:
            raw = dot_nt(q, kv_ref[k, 0:256, :]) * C2
            bias = jnp.concatenate(
                [jnp.broadcast_to(cache_bias, (256, 128)), block_bias], axis=1
            )
            scores.append(raw + bias)
        top = functools.reduce(jnp.maximum, scores)
        top = jnp.max(top, axis=1, keepdims=True)
        total = jnp.zeros((256, 256), F32)
        acc = jnp.zeros((256, HD), F32)
        for score, (kv_ref, k, _, _) in zip(scores, sources):
            weights = jnp.exp2(score - top)
            total = total + weights
            acc = acc + jnp.dot(
                weights.astype(BF16), kv_ref[k, 256:512, :], preferred_element_type=F32
            )
        total = jnp.sum(total, axis=1, keepdims=True)
        attended = (acc / total).astype(BF16)
        level = top + jnp.log2(total)
        for i in range(2):
            b, here = 2 * step + i, slice(128 * i, 128 * i + 128)
            pt_ref[b] = dot_nt(both, attended[here])
            turned = jnp.broadcast_to(level[here], (128, 128)).T[0:8]
            high = turned.astype(BF16).astype(F32)
            mid = (turned - high).astype(BF16).astype(F32)
            low = turned - high - mid
            level_ref[b] = jnp.where(
                part == 0, high, jnp.where(part == 1, mid, jnp.where(part == 2, low, 0.0))
            )
        return carry

    lax.fori_loop(0, 4, block, 0, unroll=4)
    ship(prev_ref, pt_ref, level_ref, out_ref)


def ship(prev_ref, pt_ref, level_ref, out_ref):
    edge = [prev_ref[f, a, 3 * e : 3 * e + 1, :] for e in range(2) for f in range(2) for a in range(2)]
    edge = jnp.concatenate([x.astype(F32) for x in edge], axis=1)
    column = lax.broadcasted_iota(jnp.int32, (32, 128), 1) % 8
    few = column[0:8]
    part = lax.broadcasted_iota(jnp.int32, (8, 128), 0)
    for z in range(NZ):
        b, odd = z // 2, z % 2
        beside = b - 1 + 2 * odd
        low, high = pt_ref[b, 0:32], pt_ref[b, 32:64]
        if odd:
            main = jnp.where(column >= 4, low, pltpu.roll(high, 124, 1))
        else:
            main = jnp.where(column < 4, low, pltpu.roll(high, 4, 1))
        halo = jnp.zeros((8, 128), F32)
        level = level_ref[b]
        for q in range(4):
            if not odd or beside < 8:
                right = pt_ref[beside if odd else b, 8 * q : 8 * q + 8]
                right = pltpu.roll(right, (q if odd else q - 4) % 128, 1)
                halo = jnp.where(few == q, right, halo)
            if odd or beside >= 0:
                left = pt_ref[b if odd else beside, 32 + 8 * q : 40 + 8 * q]
                left = pltpu.roll(left, (q + 1 if odd else q - 3) % 128, 1)
                halo = jnp.where(few == 4 + q, left, halo)
        if 0 <= beside < 8:
            level = jnp.where(few == 7 - 7 * odd, level_ref[beside], level)
        level = jnp.where(part == 3, edge, level)
        out_ref[z] = jnp.concatenate([main, halo, level], axis=0).astype(BF16)


def spread_kernel(y_ref, prev_ref, out_ref, rows_ref):
    z, h, m = (lax.axis_index(axis) for axis in ("z", "h", "mp"))
    odd = lax.rem(z, 2)
    level = []
    for n in range(NZ):
        tail = y_ref[n, 32:48].astype(F32)
        level.append(tail[8:9] + tail[9:10] + tail[10:11])
    level = jnp.concatenate(level, axis=0)
    top = jnp.maximum(
        jnp.maximum(level[0:4], level[4:8]), jnp.maximum(level[8:12], level[12:16])
    )
    share = jnp.exp2(level - jnp.concatenate([top] * 4, axis=0))
    whole = share[0:4] + share[4:8] + share[8:12] + share[12:16]
    share = share / jnp.concatenate([whole] * 4, axis=0)
    column = lax.broadcasted_iota(jnp.int32, (16, 128), 1) % 8
    main_share = jnp.where(odd == 1, pltpu.roll(share, 124, 1), share)
    main_share = jnp.where(column < 4, main_share, pltpu.roll(main_share, 4, 1))
    share = jnp.where(odd == 1, pltpu.roll(share, 4, 1), share)
    halo_share = jnp.zeros((16, 128), F32)
    for q in range(4):
        halo_share = jnp.where(column == q, pltpu.roll(share, (q - 4) % 128, 1), halo_share)
        halo_share = jnp.where(column == 4 + q, pltpu.roll(share, (q - 3) % 128, 1), halo_share)
    to = lax.broadcasted_iota(jnp.int32, (128, 128), 0)
    at = lax.broadcasted_iota(jnp.int32, (128, 128), 1)
    same = (at // 32 == to % 4) & ((at // 8) % 4 == to // 32)
    goal = 2 * ((to // 16) % 2) + (to // 4) % 4 - 1
    own = same & (goal >= 0) & (goal < 4)
    pick = [
        own & (at % 8 == goal + 4 * odd),
        own & (at % 8 == goal + 4 - 4 * odd),
        same & ((goal == 4) & (at % 8 < 4) | (goal == -1) & (at % 8 >= 4)),
    ]
    pick = jnp.concatenate([jnp.where(x, 1.0, 0.0).astype(BF16) for x in pick], axis=1)
    lane = lax.broadcasted_iota(jnp.int32, (1, 128), 1)
    earlier = []
    for c in range(2):
        for f in range(2):
            parts = [
                prev_ref[f, a, 2 * c + b : 2 * c + b + 1, :].astype(F32)
                for b in range(2)
                for a in range(2)
            ]
            earlier.append(jnp.concatenate([jnp.zeros((1, 64), F32)] + parts, axis=1))
    rim = y_ref[jnp.maximum(z - 1, 0), 32:48].astype(F32)[11:12]
    rim = jnp.where((z > 0) & (h == 1), rim, 0.0)
    for f in range(2):
        earlier.append(jnp.where(lane >= 96, pltpu.roll(rim, 32 - 32 * f, 1), 0.0))
    rim = y_ref[jnp.minimum(z + 1, NZ - 1), 32:48].astype(F32)[11:12]
    rim = jnp.where((z < NZ - 1) & (h == 0), rim, 0.0)
    for f in range(2):
        earlier.append(
            jnp.where((lane >= 64) & (lane < 96), pltpu.roll(rim, 64 - 32 * f, 1), 0.0)
        )
    to = lax.broadcasted_iota(jnp.int32, (32, 8), 0)
    item = lax.broadcasted_iota(jnp.int32, (32, 8), 1)
    cell = 2 * (to // 16) + (to // 4) % 4
    place = (item < 4) & (cell == 2 * h + item // 2 + 1)
    place = place | (item // 2 == 2) & (cell == 0) | (item // 2 == 3) & (cell == 5)
    place = jnp.where(place & (to % 4 == item % 2), 1.0, 0.0).astype(BF16)
    earlier = jnp.dot(
        place, jnp.concatenate(earlier, axis=0).astype(BF16), preferred_element_type=F32
    )
    few = column[0:8]
    blank = jnp.zeros((32, 128), F32)
    for r in range(4):
        main = jnp.zeros((32, 128), F32)
        halo = jnp.zeros((8, 128), F32)
        for g in range(4):
            n = 4 * g + r
            main = main + main_share[n : n + 1] * y_ref[n, 0:32].astype(F32)
            halo = halo + halo_share[n : n + 1] * y_ref[n, 32:48].astype(F32)[0:8]
        right = jnp.concatenate([jnp.where(few == q, halo, 0.0) for q in range(4)], axis=0)
        left = jnp.concatenate([jnp.where(few == 4 + q, halo, 0.0) for q in range(4)], axis=0)
        value = jnp.concatenate(
            [
                jnp.concatenate([main, blank, right], axis=1),
                jnp.concatenate([blank, main, left], axis=1),
                jnp.zeros((64, 384), F32),
            ],
            axis=0,
        )
        moved = dot_nt(pick, value.astype(BF16))
        for i in range(4):
            row = 4 * r + i
            rows_ref[row] = moved[32 * i : 32 * i + 32] + jnp.where(m == row, earlier, 0.0)
    below = lax.broadcasted_iota(jnp.int32, (32, 128), 1) % 32 < 16
    for row in range(16):
        under = rows_ref[row + 1] if row < 15 else jnp.zeros((32, 128), F32)
        over = rows_ref[row - 1] if row > 0 else jnp.zeros((32, 128), F32)
        beside = jnp.where(below, under, over).astype(BF16)
        own = rows_ref[row].astype(BF16)
        for k in range(2):
            out_ref[16 * k + row, 0:16] = own[16 * k : 16 * k + 16]
            out_ref[16 * k + row, 16:32] = beside[16 * k : 16 * k + 16]


def decode_kernel(r_ref, w_ref, bias_ref, gain_ref, out_ref, z_ref, taps_ref):
    nothing = jnp.zeros((16, CH), BF16)
    for a in range(2):
        for b in range(2):
            for dt in range(3):
                for k in range(16):
                    i, j, pb, pa = k // 8, k // 4 % 2, k // 2 % 2, k % 2
                    dy, dx = 2 * i + pa + a - 1, 2 * j + pb + b - 1
                    inside = 0 <= dy < 3 and 0 <= dx < 3
                    tap = w_ref[dt, dy, dx] if inside else nothing
                    taps_ref[a, b, dt, 16 * k : 16 * k + 16] = tap
    total = jnp.zeros((32, 128), F32)
    for s in range(32):
        total = total + r_ref[s].astype(F32)
    total = total.astype(BF16).astype(F32)
    z_ref[...] = jnp.zeros_like(z_ref)
    for dr in range(2):
        for cc in range(4):
            at = dr * 16 + cc * 4
            z_ref[dr, cc * 6 + 2 : cc * 6 + 6] = total[at : at + 4, 0:64]
            z_ref[dr, cc * 6 : cc * 6 + 2] = total[at : at + 2, 64:128]
    for a in range(2):
        for b in range(2):
            conv = jnp.zeros((16, CH), F32)
            for dt in range(3):
                pieces = []
                for i in range(2):
                    for j in range(2):
                        start = (b + j) * 6 + dt
                        pieces.append(z_ref[(a + i + 1) % 2, start : start + 16])
                lhs = jnp.concatenate(pieces, axis=1).astype(BF16)
                conv = conv + jnp.dot(lhs, taps_ref[a, b, dt], preferred_element_type=F32)
            conv = conv + bias_ref[...].reshape(1, CH)
            meansq = jnp.mean(conv * conv, axis=1, keepdims=True)
            normed = conv * lax.rsqrt(meansq + 1e-06) * gain_ref[...].reshape(1, CH)
            decoded = (normed / (1.0 + jnp.exp(-normed))).astype(BF16)
            for c in range(2):
                for f in range(FR):
                    out_ref[f, a, 2 * c + b] = decoded[c * 6 + f]


def body(
    queries,
    stretch_keys,
    stretch_values,
    cache_keys,
    cache_values,
    cache_lengths,
    frame_mask,
    out_weight,
    head_weight,
    previous_latent,
    conv_weight,
    conv_bias,
    norm_gain,
):
    z = lax.axis_index("z")
    vmem = pl.BlockSpec(memory_space=pltpu.VMEM)
    whole = pl.BlockSpec()
    hbm = pl.BlockSpec(memory_space=pltpu.HBM)
    smem = pl.BlockSpec(memory_space=pltpu.SMEM)

    def call(kernel, name, outs, specs, scratch=(), limit=16, **kw):
        shapes = [jax.ShapeDtypeStruct(shape, kind) for shape, kind in outs]
        return pl.pallas_call(
            kernel,
            out_shape=shapes if len(shapes) > 1 else shapes[0],
            in_specs=specs,
            out_specs=[vmem] * len(shapes) if len(shapes) > 1 else vmem,
            scratch_shapes=scratch,
            compiler_params=pltpu.CompilerParams(vmem_limit_bytes=limit * 1024 * 1024),
            name=name,
            **kw,
        )

    keep, give, q = call(
        pack_kernel,
        "pack",
        (((528, HD), BF16), ((528, HD), BF16), ((8, 8, 16, HD), BF16)),
        [hbm] * 6,
        [
            pltpu.VMEM((5, 128, 2 * HD), BF16),
            pltpu.SMEM((1,), jnp.int32),
            pltpu.SemaphoreType.DMA((6,)),
        ],
        limit=60,
    )(cache_lengths, queries, cache_keys, stretch_keys, cache_values, stretch_values)
    got = lax.ppermute(give, "h", [(0, 1), (1, 0)])
    hw = lax.dynamic_slice_in_dim(head_weight, 80 * (z % 4), 80, 0)
    hw = lax.all_to_all(jnp.broadcast_to(hw[None], (16, 80, 64)), "mp", 0, 0, tiled=True)
    q, hw = lax.optimization_barrier((q, hw))
    q = lax.all_to_all(q, ("z", "h"), 0, 0, tiled=True, axis_index_groups=FAR)
    kv = call(
        pair_kernel,
        "pair",
        (((2, 560, HD), BF16),),
        [vmem] * 3 + [hbm],
        [pltpu.VMEM((HD, 5120), BF16), pltpu.VMEM((5120, 64), BF16), pltpu.SemaphoreType.DMA],
        limit=52,
        cost_estimate=pl.CostEstimate(flops=10**11, bytes_accessed=10**6, transcendentals=0),
    )(keep, got, hw, out_weight)
    up = lax.ppermute(kv, "z", [(i, (i + 1) % NZ) for i in range(NZ)])
    down = lax.ppermute(kv, "z", [((i + 1) % NZ, i) for i in range(NZ)])
    two = lax.ppermute(
        kv,
        ("z", "mp"),
        [(16 * i + j, 16 * ((i + (2 if j % 2 == 0 else 14)) % NZ) + j) for i in range(NZ) for j in range(16)],
    )
    partial = call(
        attend_kernel,
        "attend",
        (((NZ, 48, 128), BF16),),
        [smem] + [vmem] * 6,
        [pltpu.VMEM((8, 64, 128), F32), pltpu.VMEM((8, 8, 128), F32)],
        cost_estimate=pl.CostEstimate(flops=10**10, bytes_accessed=10**6, transcendentals=10**6),
    )(frame_mask, q, kv, up, down, two, previous_latent)
    partial = lax.all_to_all(partial, "z", 0, 0, tiled=True)
    spread = call(spread_kernel, "spread", (((32, 32, 128), BF16),), [vmem, whole], [pltpu.VMEM((16, 32, 128), F32)])(
        partial, previous_latent
    )
    spread = lax.all_to_all(spread, ("h", "mp"), 0, 0, tiled=True)
    return call(
        decode_kernel,
        "decode",
        (((FR, 2, 4, CH), BF16),),
        [vmem] + [whole] * 3,
        [pltpu.VMEM((2, 40, 64), F32), pltpu.VMEM((2, 2, 3, 256, CH), BF16)],
    )(spread, conv_weight, conv_bias, norm_gain)


def solution(mesh):
    fine = Mesh(mesh.devices.reshape(NZ, 2, 16), ("z", "h", "mp"))
    seq = ("z", "h")
    return jax.shard_map(
        body,
        mesh=fine,
        in_specs=(
            P(seq, "mp"),
            P(seq, "mp"),
            P(seq, "mp"),
            P(seq, "mp"),
            P(seq, "mp"),
            P(seq),
            P(),
            P("mp", None),
            P("mp", None),
            P(None, "mp", seq, None),
            P(),
            P(),
            P(),
        ),
        out_specs=P(None, "mp", seq, None),
        check_vma=False,
    )
```

time: 114 us -> 107 us (0.939)
  blocking collectives: 43.3 us -> 39.8 us
  Pallas kernels: 13.7 us -> 11 us
  local copies, waits for them, and re-layouts: 4.49 us -> 2.76 us
  waiting for transfers between devices: 13.2 us -> 14.8 us
    all_to_all x1, blocking collectives: 19.6 us -> 16.3 us  [body(): spread = lax.all_to_all(spread, ('h', 'mp'), 0, 0, tiled=True)]
    pallas_call x3, Pallas kernels: 10.6 us -> 7.83 us  [the longest x1 5.27 us: body(): call(attend_kernel, 'attend', (((NZ, 48, 128), BF16),), [smem] + [vmem] *...]
    ppermute x1, waiting for transfers between devices: 4.95 us -> 7.26 us  [body(): lax.ppermute(kv, ('z', 'mp'), [(16 * i + j, 16 * ((i + (2 if j % 2 == 0 e...]
    unnamed x16 -> x14, local copies, waits for them, and re-layouts: 3.47 us -> 1.72 us
    ppermute x1, waiting for transfers between devices: 4.82 us -> 3.41 us  [body(): down = lax.ppermute(kv, 'z', [((i + 1) % NZ, i) for i in range(NZ)])]
  transfers between devices with their start and end apart: 6 -> 6, of which waited for: 4 -> 4; matrix products, arithmetic and copies ran while one was open for 0% -> 0% of each run, Pallas kernels for 3% -> 4%
where the time goes in v3:
time: 107 us
  blocking collectives  39.8 us (37%)
  starting transfers between devices  37.5 us (35%)
  waiting for transfers between devices  14.8 us (14%)
  Pallas kernels  11 us (10%)
  local copies, waits for them, and re-layouts  2.76 us (3%)
    all_to_all x1, blocking collectives, body(): partial = lax.all_to_all(partial, 'z', 0, 0, tiled=True)  23.5 us
    all_to_all x1, blocking collectives, body(): spread = lax.all_to_all(spread, ('h', 'mp'), 0, 0, tiled=True)  16.3 us
    all_to_all x1, starting transfers between devices, body(): q = lax.all_to_all(q, ('z', 'h'), 0, 0, tiled=True, axis_index_groups=FAR)  13.6 us
    all_to_all x1, starting transfers between devices, body(): lax.all_to_all(jnp.broadcast_to(hw[None], (16, 80, 64)), 'mp', 0, 0, tile...  10.2 us
    ppermute x1, waiting for transfers between devices, body(): lax.ppermute(kv, ('z', 'mp'), [(16 * i + j, 16 * ((i + (2 if j % 2 == 0 e...  7.26 us
    ppermute x1, starting transfers between devices, body(): lax.ppermute(kv, ('z', 'mp'), [(16 * i + j, 16 * ((i + (2 if j % 2 == 0 e...  6.52 us
    pallas_call x1, Pallas kernels, body(): call(attend_kernel, 'attend', (((NZ, 48, 128), BF16),), [smem] + [vmem] *...  5.27 us
    ppermute x1, waiting for transfers between devices, body(): down = lax.ppermute(kv, 'z', [((i + 1) % NZ, i) for i in range(NZ)])  3.41 us
  transfers between devices with their start and end apart: 6, of which 4 were waited for; matrix products, arithmetic and copies ran while one was open for 0% of the time, Pallas kernels for 4%

profile of v3, /device:TPU:1, one launch (start us, length us, event | category | flops | bytes accessed | tf_op | source)
XLA Modules:
  0.0 106.6 jit_solution(17985823436372648738)
XLA Ops:
  0.0 0.0 copy-start
  0.0 0.8 copy-done
  0.8 0.1 constant_dynamic-slice_fusion
  0.9 0.8 broadcast_in_dim.2
  1.6 10.2 %all-to-all-start = ((bf16[16,80,64]{1,2,0:T(8,128)(2,1)}), bf16[16,80,64]{1,2,0:T(8,128)(2,1)S(1)}, u32[]{:S(2)}, u32[]{:S(2)}) async-start(bf16[16,80,64]{1,2,0:T(8,128)(2,1)} %broadcast_in_dim.2), calls=%async_computation | async-start | bytes 524288 | tf_op jit(solution)/shard_map/all_to_all | solution.py:361
  12.5 1.8 %pack.1 = (bf16[528,128]{1,0:T(8,128)(2,1)}, bf16[528,128]{1,0:T(8,128)(2,1)}, bf16[8,8,16,128]{3,2,1,0:T(8,128)(2,1)}) custom-call(s32[1]{0:T(128)S(6)} %copy.16.len_hbm, bf16[128,256]{1,0:T(8,128)(2,1)} %q_hbm.1, bf16[128,256]{1,0:T(8,128)(2,1)} %ck_hbm.1, bf16[128,256]{1,0:T(8,128)(2,1)} %sk_hbm.1, bf16[128,256]{1,0:T(8,128)(2,1)} %cv_hbm.1, ...), custom_call_target="tpu_custom_call" | custom-call | tf_op jit(solution)/shard_map/pack/pallas_call | solution.py:347
  14.3 1.9 %collective-permute-start = (bf16[528,128]{1,0:T(8,128)(2,1)}, bf16[528,128]{1,0:T(8,128)(2,1)S(1)}, u32[]{:S(2)}, u32[]{:S(2)}) collective-permute-start(bf16[528,128]{1,0:T(8,128)(2,1)} %get-tuple-element.13), channel_id=1, source_target_pairs={{0,16},{16,0},{1,17},{17,1},{2,18},{18,2},{3,19},{19,3},{4,20},{20... | collective-permute-start | bytes 405512 | tf_op jit(solution)/shard_map/ppermute | solution.py:359
  16.2 2.8 %all-to-all-done = bf16[16,80,64]{1,2,0:T(8,128)(2,1)S(1)} async-done(((bf16[16,80,64]{1,2,0:T(8,128)(2,1)}), bf16[16,80,64]{1,2,0:T(8,128)(2,1)S(1)}, u32[]{:S(2)}, u32[]{:S(2)}) %all-to-all-start) | async-done | bytes 163872 | tf_op jit(solution)/shard_map/all_to_all | solution.py:361
  19.1 13.6 %all-to-all-start.1 = ((bf16[8,8,16,128]{3,2,1,0:T(8,128)(2,1)}), bf16[8,8,16,128]{3,2,1,0:T(8,128)(2,1)S(1)}, u32[]{:S(2)}, u32[]{:S(2)}) async-start(bf16[8,8,16,128]{3,2,1,0:T(8,128)(2,1)} %get-tuple-element.11), calls=%async_computation.1 | async-start | bytes 524288 | tf_op jit(solution)/shard_map/all_to_all | solution.py:363
  32.7 0.2 copy.15.hw_ref
  32.9 0.0 collective-permute-done.got_ref
  32.9 0.0 copy-start.5
  32.9 0.9 copy-done.5
  33.8 0.0 copy-start.2
  33.8 0.0 copy-start.6
  33.8 2.1 %pair.1.kv0_ref = bf16[2,560,128]{2,1,0:T(8,128)(2,1)S(1)} custom-call(bf16[528,128]{1,0:T(8,128)(2,1)S(1)} %copy-done.5, bf16[528,128]{1,0:T(8,128)(2,1)S(1)} %collective-permute-done.got_ref, bf16[16,80,64]{2,1,0:T(8,128)(2,1)S(1)} %copy.15.hw_ref, bf16[256,5120]{1,0:T(8,128)(2,1)} %ow_hbm.1), custom_call_target="tpu_custom_call" | custom-call | flops 99999997952 | bytes 1000000 | tf_op jit(solution)/shard_map/pair/pallas_call | solution.py:364
  35.9 0.0 copy-start.1
  35.9 0.0 copy-start.3
  35.9 0.0 copy-start.4
  36.0 6.5 %collective-permute-start.3 = (bf16[2,560,128]{2,1,0:T(8,128)(2,1)S(1)}, bf16[2,560,128]{2,1,0:T(8,128)(2,1)S(1)}, u32[]{:S(2)}, u32[]{:S(2)}) collective-permute-start(bf16[2,560,128]{2,1,0:T(8,128)(2,1)S(1)} %pair.1.kv0_ref), channel_id=1, source_target_pairs={{0,64},{1,449},{2,66},{3,451},{4,68},{5,453},{6,70},{7,455},{8,72}... | collective-permute-start | bytes 860168 | tf_op jit(solution)/shard_map/ppermute | solution.py:375
  42.5 2.6 %collective-permute-start.2 = (bf16[2,560,128]{2,1,0:T(8,128)(2,1)S(1)}, bf16[2,560,128]{2,1,0:T(8,128)(2,1)S(1)}, u32[]{:S(2)}, u32[]{:S(2)}) collective-permute-start(bf16[2,560,128]{2,1,0:T(8,128)(2,1)S(1)} %pair.1.kv0_ref), channel_id=1, source_target_pairs={{32,0},{64,32},{96,64},{128,96},{160,128},{192,160},{224,192},{256... | collective-permute-start | bytes 860168 | tf_op jit(solution)/shard_map/ppermute | solution.py:374
  45.1 2.6 %collective-permute-start.1 = (bf16[2,560,128]{2,1,0:T(8,128)(2,1)S(1)}, bf16[2,560,128]{2,1,0:T(8,128)(2,1)S(1)}, u32[]{:S(2)}, u32[]{:S(2)}) collective-permute-start(bf16[2,560,128]{2,1,0:T(8,128)(2,1)S(1)} %pair.1.kv0_ref), channel_id=1, source_target_pairs={{0,32},{32,64},{64,96},{96,128},{128,160},{160,192},{192,224},{224... | collective-permute-start | bytes 860168 | tf_op jit(solution)/shard_map/ppermute | solution.py:373
  47.8 7.3 %collective-permute-done.3.kv3_ref = bf16[2,560,128]{2,1,0:T(8,128)(2,1)S(1)} collective-permute-done((bf16[2,560,128]{2,1,0:T(8,128)(2,1)S(1)}, bf16[2,560,128]{2,1,0:T(8,128)(2,1)S(1)}, u32[]{:S(2)}, u32[]{:S(2)}) %collective-permute-start.3) | collective-permute-done | bytes 286752 | tf_op jit(solution)/shard_map/ppermute | solution.py:375
  55.0 3.4 %collective-permute-done.2.kv2_ref = bf16[2,560,128]{2,1,0:T(8,128)(2,1)S(1)} collective-permute-done((bf16[2,560,128]{2,1,0:T(8,128)(2,1)S(1)}, bf16[2,560,128]{2,1,0:T(8,128)(2,1)S(1)}, u32[]{:S(2)}, u32[]{:S(2)}) %collective-permute-start.2) | collective-permute-done | bytes 286752 | tf_op jit(solution)/shard_map/ppermute | solution.py:374
  58.5 1.2 %collective-permute-done.1.kv1_ref = bf16[2,560,128]{2,1,0:T(8,128)(2,1)S(1)} collective-permute-done((bf16[2,560,128]{2,1,0:T(8,128)(2,1)S(1)}, bf16[2,560,128]{2,1,0:T(8,128)(2,1)S(1)}, u32[]{:S(2)}, u32[]{:S(2)}) %collective-permute-start.1) | collective-permute-done | bytes 286752 | tf_op jit(solution)/shard_map/ppermute | solution.py:373
  59.7 0.0 all-to-all-done.1.q_ref
  59.7 0.0 copy-done.2
  59.7 0.0 copy-done.6
  59.7 5.3 %attend.1 = bf16[16,48,128]{2,1,0:T(8,128)(2,1)S(1)} custom-call(s32[4,4]{1,0:T(4,128)S(1)} %copy-done.6, bf16[8,8,16,128]{3,2,1,0:T(8,128)(2,1)S(1)} %all-to-all-done.1.q_ref, bf16[2,560,128]{2,1,0:T(8,128)(2,1)S(1)} %pair.1.kv0_ref, bf16[2,560,128]{2,1,0:T(8,128)(2,1)S(1)} %collective-permute-done.1.kv1_ref, ...), custom_call_target="tpu_custom_call" | custom-call | flops 10000000000 | bytes 1000000 | tf_op jit(solution)/shard_map/attend/pallas_call | solution.py:380
  65.0 23.5 %all_to_all.20.y_ref = bf16[16,48,128]{2,1,0:T(8,128)(2,1)S(1)} all-to-all(bf16[16,48,128]{2,1,0:T(8,128)(2,1)S(1)} %attend.1), channel_id=1, replica_groups=mesh['z'=16,'h'=2,'mp'=16] {'z'}, dimensions={0} | all-to-all | bytes 393216 | tf_op jit(solution)/shard_map/all_to_all | solution.py:388
  88.5 0.5 spread.1
  89.0 16.3 %all_to_all.21.r_ref = bf16[32,32,128]{2,1,0:T(8,128)(2,1)S(1)} all-to-all(bf16[32,32,128]{2,1,0:T(8,128)(2,1)S(1)} %spread.1), channel_id=1, replica_groups=mesh['z'=16,'h'=2,'mp'=16] {'h','mp'}, dimensions={0} | all-to-all | bytes 524288 | tf_op jit(solution)/shard_map/all_to_all | solution.py:392
  105.3 0.0 copy-done.1
  105.3 0.0 copy-done.3
  105.3 0.0 copy-done.4
  105.3 1.3 %decode.1 = bf16[4,2,4,384]{3,2,1,0:T(4,128)(2,1)} custom-call(bf16[32,32,128]{2,1,0:T(8,128)(2,1)S(1)} %all_to_all.21.r_ref, bf16[3,3,3,16,384]{4,3,2,1,0:T(8,128)(2,1)S(1)} %copy-done.1, f32[384]{0:T(512)S(1)} %copy-done.3, f32[384]{0:T(512)S(1)} %copy-done.4), custom_call_target="tpu_custom_call" | custom-call | tf_op jit(solution)/shard_map/decode/pallas_call | solution.py:393
Async XLA Ops:
  0.0 0.8 copy-start
  1.6 17.4 %all-to-all-start = ((bf16[16,80,64]{1,2,0:T(8,128)(2,1)}), bf16[16,80,64]{1,2,0:T(8,128)(2,1)S(1)}, u32[]{:S(2)}, u32[]{:S(2)}) async-start(bf16[16,80,64]{1,2,0:T(8,128)(2,1)} %broadcast_in_dim.2), calls=%async_computation | async-start | bytes 524288 | tf_op jit(solution)/shard_map/all_to_all | solution.py:361
  14.3 18.6 %collective-permute-start = (bf16[528,128]{1,0:T(8,128)(2,1)}, bf16[528,128]{1,0:T(8,128)(2,1)S(1)}, u32[]{:S(2)}, u32[]{:S(2)}) collective-permute-start(bf16[528,128]{1,0:T(8,128)(2,1)} %get-tuple-element.13), channel_id=1, source_target_pairs={{0,16},{16,0},{1,17},{17,1},{2,18},{18,2},{3,19},{19,3},{4,20},{20... | collective-permute-start | bytes 405512 | tf_op jit(solution)/shard_map/ppermute | solution.py:359
  19.1 40.6 %all-to-all-start.1 = ((bf16[8,8,16,128]{3,2,1,0:T(8,128)(2,1)}), bf16[8,8,16,128]{3,2,1,0:T(8,128)(2,1)S(1)}, u32[]{:S(2)}, u32[]{:S(2)}) async-start(bf16[8,8,16,128]{3,2,1,0:T(8,128)(2,1)} %get-tuple-element.11), calls=%async_computation.1 | async-start | bytes 524288 | tf_op jit(solution)/shard_map/all_to_all | solution.py:363
  32.9 0.9 copy-start.5
  33.8 25.9 %copy-start.2 = (bf16[2,2,4,16]{3,2,1,0:T(4,128)(2,1)S(1)}, bf16[2,2,4,16]{3,2,1,0:T(4,128)(2,1)}, u32[]{:S(2)}) copy-start(bf16[2,2,4,16]{3,2,1,0:T(4,128)(2,1)} %prev_ref.3) | copy-start | bytes 1540
  33.8 25.9 %copy-start.6 = (s32[4,4]{1,0:T(4,128)S(1)}, s32[4,4]{1,0:T(4,128)}, u32[]{:S(2)}) copy-start(s32[4,4]{1,0:T(4,128)} %fm_ref.1) | copy-start | bytes 196
  35.9 69.3 %copy-start.1 = (bf16[3,3,3,16,384]{4,3,2,1,0:T(8,128)(2,1)S(1)}, bf16[3,3,3,16,384]{4,3,2,1,0:T(8,128)(2,1)}, u32[]{:S(2)}) copy-start(bf16[3,3,3,16,384]{4,3,2,1,0:T(8,128)(2,1)} %w_ref.1) | copy-start | bytes 995332
  35.9 69.3 %copy-start.3 = (f32[384]{0:T(512)S(1)}, f32[384]{0:T(512)}, u32[]{:S(2)}) copy-start(f32[384]{0:T(512)} %bias_ref.1) | copy-start | bytes 4612
  35.9 69.3 %copy-start.4 = (f32[384]{0:T(512)S(1)}, f32[384]{0:T(512)}, u32[]{:S(2)}) copy-start(f32[384]{0:T(512)} %gain_ref.1) | copy-start | bytes 4612
  36.0 19.1 %collective-permute-start.3 = (bf16[2,560,128]{2,1,0:T(8,128)(2,1)S(1)}, bf16[2,560,128]{2,1,0:T(8,128)(2,1)S(1)}, u32[]{:S(2)}, u32[]{:S(2)}) collective-permute-start(bf16[2,560,128]{2,1,0:T(8,128)(2,1)S(1)} %pair.1.kv0_ref), channel_id=1, source_target_pairs={{0,64},{1,449},{2,66},{3,451},{4,68},{5,453},{6,70},{7,455},{8,72}... | collective-permute-start | bytes 860168 | tf_op jit(solution)/shard_map/ppermute | solution.py:375
  42.5 16.0 %collective-permute-start.2 = (bf16[2,560,128]{2,1,0:T(8,128)(2,1)S(1)}, bf16[2,560,128]{2,1,0:T(8,128)(2,1)S(1)}, u32[]{:S(2)}, u32[]{:S(2)}) collective-permute-start(bf16[2,560,128]{2,1,0:T(8,128)(2,1)S(1)} %pair.1.kv0_ref), channel_id=1, source_target_pairs={{32,0},{64,32},{96,64},{128,96},{160,128},{192,160},{224,192},{256... | collective-permute-start | bytes 860168 | tf_op jit(solution)/shard_map/ppermute | solution.py:374
  45.1 14.6 %collective-permute-start.1 = (bf16[2,560,128]{2,1,0:T(8,128)(2,1)S(1)}, bf16[2,560,128]{2,1,0:T(8,128)(2,1)S(1)}, u32[]{:S(2)}, u32[]{:S(2)}) collective-permute-start(bf16[2,560,128]{2,1,0:T(8,128)(2,1)S(1)} %pair.1.kv0_ref), channel_id=1, source_target_pairs={{0,32},{32,64},{64,96},{96,128},{128,160},{160,192},{192,224},{224... | collective-permute-start | bytes 860168 | tf_op jit(solution)/shard_map/ppermute | solution.py:373

commit v4 on v3

--- a/solution.py
+++ b/solution.py
@@ -71,38 +71,21 @@
             kv_ref[k, 528 + 16 * a : 544 + 16 * a] = both[at : at + 16]
 
 
-def attend_kernel(
-    fm_ref,
-    q_ref,
-    kv0_ref,
-    kv1_ref,
-    kv2_ref,
-    kv3_ref,
-    prev_ref,
-    out_ref,
-    pt_ref,
-    level_ref,
-):
-    z, core = lax.axis_index("z"), lax.rem(lax.axis_index("mp"), 2)
-    planes = (z, z + NZ - 1, z + 1, z + NZ - 2 + 4 * core)
+def attend(fm_ref, q_ref, planes, emit):
     lane = lax.broadcasted_iota(jnp.int32, (1, HD), 1)
     row_frame = lax.broadcasted_iota(jnp.int32, (256, 1), 0) % 128 // 32
     sources = []
-    both = jnp.zeros((64, HD), F32)
-    for kv_ref, plane in zip((kv0_ref, kv1_ref, kv2_ref, kv3_ref), planes):
+    for kv_ref, plane in planes:
         frame = (plane % NZ) // 4
         block_bias = jnp.zeros((256, 1), F32)
         for f in range(FR):
             here = jnp.where(fm_ref[f, frame] == 1, 0.0, NEG)
             block_bias = jnp.where(row_frame == f, here, block_bias)
         block_bias = jnp.broadcast_to(block_bias, (256, 128))
-        both = both + jnp.concatenate([kv_ref[0, 528:560], kv_ref[1, 528:560]], 0).astype(F32)
         for k in range(2):
             filled = kv_ref[k, 512:528, :].astype(F32)[0:1]
             cache_bias = jnp.where(lane.astype(F32) < filled, 0.0, NEG)
             sources.append((kv_ref, k, cache_bias, block_bias))
-    both = both.astype(BF16)
-    part = lax.broadcasted_iota(jnp.int32, (8, 128), 0)
 
     def block(step, carry):
         q = jnp.concatenate([q_ref[:, 2 * step + i].reshape(128, HD) for i in range(2)], axis=0)
@@ -127,18 +110,62 @@
         attended = (acc / total).astype(BF16)
         level = top + jnp.log2(total)
         for i in range(2):
-            b, here = 2 * step + i, slice(128 * i, 128 * i + 128)
-            pt_ref[b] = dot_nt(both, attended[here])
+            here = slice(128 * i, 128 * i + 128)
             turned = jnp.broadcast_to(level[here], (128, 128)).T[0:8]
-            high = turned.astype(BF16).astype(F32)
-            mid = (turned - high).astype(BF16).astype(F32)
-            low = turned - high - mid
-            level_ref[b] = jnp.where(
-                part == 0, high, jnp.where(part == 1, mid, jnp.where(part == 2, low, 0.0))
-            )
+            emit(2 * step + i, attended[here], turned)
         return carry
 
     lax.fori_loop(0, 4, block, 0, unroll=4)
+
+
+def shares(*refs):
+    return sum(jnp.concatenate([ref[0, 528:560], ref[1, 528:560]], 0).astype(F32) for ref in refs)
+
+
+def first_kernel(fm_ref, q_ref, kv0_ref, kv3_ref, out_ref, level_ref, both_ref):
+    z, core = lax.axis_index("z"), lax.rem(lax.axis_index("mp"), 2)
+
+    def emit(b, attended, level):
+        out_ref[b] = attended
+        level_ref[b] = level
+
+    attend(fm_ref, q_ref, ((kv0_ref, z), (kv3_ref, z + NZ - 2 + 4 * core)), emit)
+    both_ref[...] = shares(kv0_ref, kv3_ref)
+
+
+def second_kernel(
+    fm_ref,
+    q_ref,
+    kv1_ref,
+    kv2_ref,
+    first_ref,
+    first_level_ref,
+    first_both_ref,
+    prev_ref,
+    out_ref,
+    pt_ref,
+    level_ref,
+):
+    z = lax.axis_index("z")
+    both = (first_both_ref[...] + shares(kv1_ref, kv2_ref)).astype(BF16)
+    part = lax.broadcasted_iota(jnp.int32, (8, 128), 0)
+
+    def emit(b, attended, level):
+        other = first_level_ref[b]
+        top = jnp.maximum(level, other)
+        share, other = jnp.exp2(level - top), jnp.exp2(other - top)
+        whole = share + other
+        here, there = dot_nt(both, attended), dot_nt(both, first_ref[b])
+        pt_ref[b] = (share / whole)[0:1] * here + (other / whole)[0:1] * there
+        level = top + jnp.log2(whole)
+        high = level.astype(BF16).astype(F32)
+        mid = (level - high).astype(BF16).astype(F32)
+        low = level - high - mid
+        level_ref[b] = jnp.where(
+            part == 0, high, jnp.where(part == 1, mid, jnp.where(part == 2, low, 0.0))
+        )
+
+    attend(fm_ref, q_ref, ((kv1_ref, z + NZ - 1), (kv2_ref, z + 1)), emit)
     ship(prev_ref, pt_ref, level_ref, out_ref)
 
 
@@ -377,14 +404,22 @@
         ("z", "mp"),
         [(16 * i + j, 16 * ((i + (2 if j % 2 == 0 else 14)) % NZ) + j) for i in range(NZ) for j in range(16)],
     )
+    cost = pl.CostEstimate(flops=10**10, bytes_accessed=10**6, transcendentals=10**6)
+    first = call(
+        first_kernel,
+        "first",
+        (((8, 128, HD), BF16), ((8, 8, 128), F32), ((64, HD), F32)),
+        [smem] + [vmem] * 3,
+        cost_estimate=cost,
+    )(frame_mask, q, kv, two)
     partial = call(
-        attend_kernel,
-        "attend",
+        second_kernel,
+        "second",
         (((NZ, 48, 128), BF16),),
-        [smem] + [vmem] * 6,
+        [smem] + [vmem] * 7,
         [pltpu.VMEM((8, 64, 128), F32), pltpu.VMEM((8, 8, 128), F32)],
-        cost_estimate=pl.CostEstimate(flops=10**10, bytes_accessed=10**6, transcendentals=10**6),
-    )(frame_mask, q, kv, up, down, two, previous_latent)
+        cost_estimate=cost,
+    )(frame_mask, q, up, down, *first, previous_latent)
     partial = lax.all_to_all(partial, "z", 0, 0, tiled=True)
     spread = call(spread_kernel, "spread", (((32, 32, 128), BF16),), [vmem, whole], [pltpu.VMEM((16, 32, 128), F32)])(
         partial, previous_latent

time: 107 us -> 105 us (0.981)
  waiting for transfers between devices: 14.8 us -> 12.2 us
    ppermute x1, waiting for transfers between devices: 3.41 us -> 1.13 us  [body(): down = lax.ppermute(kv, 'z', [((i + 1) % NZ, i) for i in range(NZ)])]
    pallas_call x1 -> x2, Pallas kernels: 5.27 us -> 6.23 us  [the longest x1 3.45 us: body(): call(second_kernel, 'second', (((NZ, 48, 128), BF16),), [smem] + [vmem] *...]
  transfers between devices with their start and end apart: 6 -> 6, of which waited for: 4 -> 4; matrix products, arithmetic and copies ran while one was open for 0% -> 0% of each run, Pallas kernels for 4% -> 6%
where the time goes in v4:
time: 105 us
  blocking collectives  39.7 us (38%)
  starting transfers between devices  37.4 us (36%)
  waiting for transfers between devices  12.2 us (12%)
  Pallas kernels  11.9 us (11%)
  local copies, waits for them, and re-layouts  2.75 us (3%)
    all_to_all x1, blocking collectives, body(): partial = lax.all_to_all(partial, 'z', 0, 0, tiled=True)  23.6 us
    all_to_all x1, blocking collectives, body(): spread = lax.all_to_all(spread, ('h', 'mp'), 0, 0, tiled=True)  16 us
    all_to_all x1, starting transfers between devices, body(): q = lax.all_to_all(q, ('z', 'h'), 0, 0, tiled=True, axis_index_groups=FAR)  13.6 us
    all_to_all x1, starting transfers between devices, body(): lax.all_to_all(jnp.broadcast_to(hw[None], (16, 80, 64)), 'mp', 0, 0, tile...  10.2 us
    ppermute x1, waiting for transfers between devices, body(): lax.ppermute(kv, ('z', 'mp'), [(16 * i + j, 16 * ((i + (2 if j % 2 == 0 e...  6.91 us
    ppermute x1, starting transfers between devices, body(): lax.ppermute(kv, ('z', 'mp'), [(16 * i + j, 16 * ((i + (2 if j % 2 == 0 e...  6.39 us
    pallas_call x1, Pallas kernels, body(): call(second_kernel, 'second', (((NZ, 48, 128), BF16),), [smem] + [vmem] *...  3.45 us
    all_to_all x1, waiting for transfers between devices, body(): lax.all_to_all(jnp.broadcast_to(hw[None], (16, 80, 64)), 'mp', 0, 0, tile...  2.85 us
  transfers between devices with their start and end apart: 6, of which 4 were waited for; matrix products, arithmetic and copies ran while one was open for 0% of the time, Pallas kernels for 6%

profile of v4, /device:TPU:1, one launch (start us, length us, event | category | flops | bytes accessed | tf_op | source)
XLA Modules:
  0.0 104.7 jit_solution(3723724797904528587)
XLA Ops:
  0.0 0.0 copy-start
  0.0 0.8 copy-done
  0.8 0.1 constant_dynamic-slice_fusion
  0.9 0.7 broadcast_in_dim.2
  1.6 10.2 %all-to-all-start = ((bf16[16,80,64]{1,2,0:T(8,128)(2,1)}), bf16[16,80,64]{1,2,0:T(8,128)(2,1)S(1)}, u32[]{:S(2)}, u32[]{:S(2)}) async-start(bf16[16,80,64]{1,2,0:T(8,128)(2,1)} %broadcast_in_dim.2), calls=%async_computation | async-start | bytes 524288 | tf_op jit(solution)/shard_map/all_to_all | solution.py:388
  12.5 1.8 %pack.1 = (bf16[528,128]{1,0:T(8,128)(2,1)}, bf16[528,128]{1,0:T(8,128)(2,1)}, bf16[8,8,16,128]{3,2,1,0:T(8,128)(2,1)}) custom-call(s32[1]{0:T(128)S(6)} %copy.16.len_hbm, bf16[128,256]{1,0:T(8,128)(2,1)} %q_hbm.1, bf16[128,256]{1,0:T(8,128)(2,1)} %ck_hbm.1, bf16[128,256]{1,0:T(8,128)(2,1)} %sk_hbm.1, bf16[128,256]{1,0:T(8,128)(2,1)} %cv_hbm.1, ...), custom_call_target="tpu_custom_call" | custom-call | tf_op jit(solution)/shard_map/pack/pallas_call | solution.py:374
  14.3 1.9 %collective-permute-start = (bf16[528,128]{1,0:T(8,128)(2,1)}, bf16[528,128]{1,0:T(8,128)(2,1)S(1)}, u32[]{:S(2)}, u32[]{:S(2)}) collective-permute-start(bf16[528,128]{1,0:T(8,128)(2,1)} %get-tuple-element.16), channel_id=1, source_target_pairs={{0,16},{16,0},{1,17},{17,1},{2,18},{18,2},{3,19},{19,3},{4,20},{20... | collective-permute-start | bytes 405512 | tf_op jit(solution)/shard_map/ppermute | solution.py:386
  16.2 2.9 %all-to-all-done = bf16[16,80,64]{1,2,0:T(8,128)(2,1)S(1)} async-done(((bf16[16,80,64]{1,2,0:T(8,128)(2,1)}), bf16[16,80,64]{1,2,0:T(8,128)(2,1)S(1)}, u32[]{:S(2)}, u32[]{:S(2)}) %all-to-all-start) | async-done | bytes 163872 | tf_op jit(solution)/shard_map/all_to_all | solution.py:388
  19.1 13.6 %all-to-all-start.1 = ((bf16[8,8,16,128]{3,2,1,0:T(8,128)(2,1)}), bf16[8,8,16,128]{3,2,1,0:T(8,128)(2,1)S(1)}, u32[]{:S(2)}, u32[]{:S(2)}) async-start(bf16[8,8,16,128]{3,2,1,0:T(8,128)(2,1)} %get-tuple-element.14), calls=%async_computation.1 | async-start | bytes 524288 | tf_op jit(solution)/shard_map/all_to_all | solution.py:390
  32.7 0.2 copy.15.hw_ref
  32.9 0.0 collective-permute-done.got_ref
  32.9 0.0 copy-start.5
  32.9 0.9 copy-done.5
  33.8 0.0 copy-start.6
  33.8 2.1 %pair.1.kv0_ref = bf16[2,560,128]{2,1,0:T(8,128)(2,1)S(1)} custom-call(bf16[528,128]{1,0:T(8,128)(2,1)S(1)} %copy-done.5, bf16[528,128]{1,0:T(8,128)(2,1)S(1)} %collective-permute-done.got_ref, bf16[16,80,64]{2,1,0:T(8,128)(2,1)S(1)} %copy.15.hw_ref, bf16[256,5120]{1,0:T(8,128)(2,1)} %ow_hbm.1), custom_call_target="tpu_custom_call" | custom-call | flops 99999997952 | bytes 1000000 | tf_op jit(solution)/shard_map/pair/pallas_call | solution.py:391
  35.9 0.0 copy-start.2
  35.9 6.4 %collective-permute-start.3 = (bf16[2,560,128]{2,1,0:T(8,128)(2,1)S(1)}, bf16[2,560,128]{2,1,0:T(8,128)(2,1)S(1)}, u32[]{:S(2)}, u32[]{:S(2)}) collective-permute-start(bf16[2,560,128]{2,1,0:T(8,128)(2,1)S(1)} %pair.1.kv0_ref), channel_id=1, source_target_pairs={{0,64},{1,449},{2,66},{3,451},{4,68},{5,453},{6,70},{7,455},{8,72}... | collective-permute-start | bytes 860168 | tf_op jit(solution)/shard_map/ppermute | solution.py:402
  42.3 2.6 %collective-permute-start.2 = (bf16[2,560,128]{2,1,0:T(8,128)(2,1)S(1)}, bf16[2,560,128]{2,1,0:T(8,128)(2,1)S(1)}, u32[]{:S(2)}, u32[]{:S(2)}) collective-permute-start(bf16[2,560,128]{2,1,0:T(8,128)(2,1)S(1)} %pair.1.kv0_ref), channel_id=1, source_target_pairs={{32,0},{64,32},{96,64},{128,96},{160,128},{192,160},{224,192},{256... | collective-permute-start | bytes 860168 | tf_op jit(solution)/shard_map/ppermute | solution.py:401
  45.0 2.6 %collective-permute-start.1 = (bf16[2,560,128]{2,1,0:T(8,128)(2,1)S(1)}, bf16[2,560,128]{2,1,0:T(8,128)(2,1)S(1)}, u32[]{:S(2)}, u32[]{:S(2)}) collective-permute-start(bf16[2,560,128]{2,1,0:T(8,128)(2,1)S(1)} %pair.1.kv0_ref), channel_id=1, source_target_pairs={{0,32},{32,64},{64,96},{96,128},{128,160},{160,192},{192,224},{224... | collective-permute-start | bytes 860168 | tf_op jit(solution)/shard_map/ppermute | solution.py:400
  47.6 6.9 %collective-permute-done.3.kv3_ref = bf16[2,560,128]{2,1,0:T(8,128)(2,1)S(1)} collective-permute-done((bf16[2,560,128]{2,1,0:T(8,128)(2,1)S(1)}, bf16[2,560,128]{2,1,0:T(8,128)(2,1)S(1)}, u32[]{:S(2)}, u32[]{:S(2)}) %collective-permute-start.3) | collective-permute-done | bytes 286752 | tf_op jit(solution)/shard_map/ppermute | solution.py:402
  54.5 0.0 all-to-all-done.1.q_ref
  54.5 0.0 copy-done.6
  54.5 2.8 %first.1 = (bf16[8,128,128]{2,1,0:T(8,128)(2,1)S(1)}, f32[8,8,128]{2,1,0:T(8,128)S(1)}, f32[64,128]{1,0:T(8,128)S(1)}) custom-call(s32[4,4]{1,0:T(4,128)S(1)} %copy-done.6, bf16[8,8,16,128]{3,2,1,0:T(8,128)(2,1)S(1)} %all-to-all-done.1.q_ref, bf16[2,560,128]{2,1,0:T(8,128)(2,1)S(1)} %pair.1.kv0_ref, bf16[2,560,128]{2,1,0:T(8,128)(2,1)S(1)} %collective-permute-done.3.kv3_ref), custom_call_target="tpu_custom_call" | custom-call | flops 10000000000 | bytes 1000000 | tf_op jit(solution)/shard_map/first/pallas_call | solution.py:408
  57.3 1.1 %collective-permute-done.2.kv2_ref = bf16[2,560,128]{2,1,0:T(8,128)(2,1)S(1)} collective-permute-done((bf16[2,560,128]{2,1,0:T(8,128)(2,1)S(1)}, bf16[2,560,128]{2,1,0:T(8,128)(2,1)S(1)}, u32[]{:S(2)}, u32[]{:S(2)}) %collective-permute-start.2) | collective-permute-done | bytes 286752 | tf_op jit(solution)/shard_map/ppermute | solution.py:401
  58.5 1.3 %collective-permute-done.1.kv1_ref = bf16[2,560,128]{2,1,0:T(8,128)(2,1)S(1)} collective-permute-done((bf16[2,560,128]{2,1,0:T(8,128)(2,1)S(1)}, bf16[2,560,128]{2,1,0:T(8,128)(2,1)S(1)}, u32[]{:S(2)}, u32[]{:S(2)}) %collective-permute-start.1) | collective-permute-done | bytes 286752 | tf_op jit(solution)/shard_map/ppermute | solution.py:400
  59.7 0.0 copy-done.2
  59.7 0.0 copy-start.1
  59.7 0.0 copy-start.3
  59.7 0.0 copy-start.4
  59.7 3.4 %second.1 = bf16[16,48,128]{2,1,0:T(8,128)(2,1)S(1)} custom-call(s32[4,4]{1,0:T(4,128)S(1)} %copy-done.6, bf16[8,8,16,128]{3,2,1,0:T(8,128)(2,1)S(1)} %all-to-all-done.1.q_ref, bf16[2,560,128]{2,1,0:T(8,128)(2,1)S(1)} %collective-permute-done.1.kv1_ref, bf16[2,560,128]{2,1,0:T(8,128)(2,1)S(1)} %collective-permute-done.2.kv2_ref, ...), custom_call_target="tpu_custom_call" | custom-call | flops 10000000000 | bytes 1000000 | tf_op jit(solution)/shard_map/second/pallas_call | solution.py:415
  63.2 23.6 %all_to_all.20.y_ref = bf16[16,48,128]{2,1,0:T(8,128)(2,1)S(1)} all-to-all(bf16[16,48,128]{2,1,0:T(8,128)(2,1)S(1)} %second.1), channel_id=1, replica_groups=mesh['z'=16,'h'=2,'mp'=16] {'z'}, dimensions={0} | all-to-all | bytes 393216 | tf_op jit(solution)/shard_map/all_to_all | solution.py:423
  86.8 0.5 spread.1
  87.3 16.0 %all_to_all.21.r_ref = bf16[32,32,128]{2,1,0:T(8,128)(2,1)S(1)} all-to-all(bf16[32,32,128]{2,1,0:T(8,128)(2,1)S(1)} %spread.1), channel_id=1, replica_groups=mesh['z'=16,'h'=2,'mp'=16] {'h','mp'}, dimensions={0} | all-to-all | bytes 524288 | tf_op jit(solution)/shard_map/all_to_all | solution.py:427
  103.3 0.0 copy-done.1
  103.3 0.0 copy-done.3
  103.4 0.0 copy-done.4
  103.4 1.3 %decode.1 = bf16[4,2,4,384]{3,2,1,0:T(4,128)(2,1)} custom-call(bf16[32,32,128]{2,1,0:T(8,128)(2,1)S(1)} %all_to_all.21.r_ref, bf16[3,3,3,16,384]{4,3,2,1,0:T(8,128)(2,1)S(1)} %copy-done.1, f32[384]{0:T(512)S(1)} %copy-done.3, f32[384]{0:T(512)S(1)} %copy-done.4), custom_call_target="tpu_custom_call" | custom-call | tf_op jit(solution)/shard_map/decode/pallas_call | solution.py:428
Async XLA Ops:
  0.0 0.8 copy-start
  1.6 17.4 %all-to-all-start = ((bf16[16,80,64]{1,2,0:T(8,128)(2,1)}), bf16[16,80,64]{1,2,0:T(8,128)(2,1)S(1)}, u32[]{:S(2)}, u32[]{:S(2)}) async-start(bf16[16,80,64]{1,2,0:T(8,128)(2,1)} %broadcast_in_dim.2), calls=%async_computation | async-start | bytes 524288 | tf_op jit(solution)/shard_map/all_to_all | solution.py:388
  14.3 18.6 %collective-permute-start = (bf16[528,128]{1,0:T(8,128)(2,1)}, bf16[528,128]{1,0:T(8,128)(2,1)S(1)}, u32[]{:S(2)}, u32[]{:S(2)}) collective-permute-start(bf16[528,128]{1,0:T(8,128)(2,1)} %get-tuple-element.16), channel_id=1, source_target_pairs={{0,16},{16,0},{1,17},{17,1},{2,18},{18,2},{3,19},{19,3},{4,20},{20... | collective-permute-start | bytes 405512 | tf_op jit(solution)/shard_map/ppermute | solution.py:386
  19.1 35.5 %all-to-all-start.1 = ((bf16[8,8,16,128]{3,2,1,0:T(8,128)(2,1)}), bf16[8,8,16,128]{3,2,1,0:T(8,128)(2,1)S(1)}, u32[]{:S(2)}, u32[]{:S(2)}) async-start(bf16[8,8,16,128]{3,2,1,0:T(8,128)(2,1)} %get-tuple-element.14), calls=%async_computation.1 | async-start | bytes 524288 | tf_op jit(solution)/shard_map/all_to_all | solution.py:390
  32.9 0.9 copy-start.5
  33.8 20.7 %copy-start.6 = (s32[4,4]{1,0:T(4,128)S(1)}, s32[4,4]{1,0:T(4,128)}, u32[]{:S(2)}) copy-start(s32[4,4]{1,0:T(4,128)} %fm_ref.3) | copy-start | bytes 196
  35.9 23.8 %copy-start.2 = (bf16[2,2,4,16]{3,2,1,0:T(4,128)(2,1)S(1)}, bf16[2,2,4,16]{3,2,1,0:T(4,128)(2,1)}, u32[]{:S(2)}) copy-start(bf16[2,2,4,16]{3,2,1,0:T(4,128)(2,1)} %prev_ref.3) | copy-start | bytes 1540
  35.9 18.6 %collective-permute-start.3 = (bf16[2,560,128]{2,1,0:T(8,128)(2,1)S(1)}, bf16[2,560,128]{2,1,0:T(8,128)(2,1)S(1)}, u32[]{:S(2)}, u32[]{:S(2)}) collective-permute-start(bf16[2,560,128]{2,1,0:T(8,128)(2,1)S(1)} %pair.1.kv0_ref), channel_id=1, source_target_pairs={{0,64},{1,449},{2,66},{3,451},{4,68},{5,453},{6,70},{7,455},{8,72}... | collective-permute-start | bytes 860168 | tf_op jit(solution)/shard_map/ppermute | solution.py:402
  42.3 16.1 %collective-permute-start.2 = (bf16[2,560,128]{2,1,0:T(8,128)(2,1)S(1)}, bf16[2,560,128]{2,1,0:T(8,128)(2,1)S(1)}, u32[]{:S(2)}, u32[]{:S(2)}) collective-permute-start(bf16[2,560,128]{2,1,0:T(8,128)(2,1)S(1)} %pair.1.kv0_ref), channel_id=1, source_target_pairs={{32,0},{64,32},{96,64},{128,96},{160,128},{192,160},{224,192},{256... | collective-permute-start | bytes 860168 | tf_op jit(solution)/shard_map/ppermute | solution.py:401
  45.0 14.8 %collective-permute-start.1 = (bf16[2,560,128]{2,1,0:T(8,128)(2,1)S(1)}, bf16[2,560,128]{2,1,0:T(8,128)(2,1)S(1)}, u32[]{:S(2)}, u32[]{:S(2)}) collective-permute-start(bf16[2,560,128]{2,1,0:T(8,128)(2,1)S(1)} %pair.1.kv0_ref), channel_id=1, source_target_pairs={{0,32},{32,64},{64,96},{96,128},{128,160},{160,192},{192,224},{224... | collective-permute-start | bytes 860168 | tf_op jit(solution)/shard_map/ppermute | solution.py:400
  59.7 43.6 %copy-start.1 = (bf16[3,3,3,16,384]{4,3,2,1,0:T(8,128)(2,1)S(1)}, bf16[3,3,3,16,384]{4,3,2,1,0:T(8,128)(2,1)}, u32[]{:S(2)}) copy-start(bf16[3,3,3,16,384]{4,3,2,1,0:T(8,128)(2,1)} %w_ref.1) | copy-start | bytes 995332
  59.7 43.6 %copy-start.3 = (f32[384]{0:T(512)S(1)}, f32[384]{0:T(512)}, u32[]{:S(2)}) copy-start(f32[384]{0:T(512)} %bias_ref.1) | copy-start | bytes 4612
  59.7 43.6 %copy-start.4 = (f32[384]{0:T(512)S(1)}, f32[384]{0:T(512)}, u32[]{:S(2)}) copy-start(f32[384]{0:T(512)} %gain_ref.1) | copy-start | bytes 4612

commit v5 on v4

--- a/solution.py
+++ b/solution.py
@@ -26,7 +26,7 @@
 
 
 def pack_kernel(
-    len_hbm, q_hbm, ck_hbm, sk_hbm, cv_hbm, sv_hbm, keep_ref, give_ref, qo_ref, buf, len_ref, sems
+    len_hbm, q_hbm, ck_hbm, sk_hbm, cv_hbm, sv_hbm, keep_ref, give_ref, raw_ref, qo_ref, buf, len_ref, sems
 ):
     copies = []
     for n, ref in enumerate((ck_hbm, sk_hbm, cv_hbm, sv_hbm, q_hbm)):
@@ -39,8 +39,10 @@
     filled = (jnp.zeros((16, HD), F32) + len_ref[0].astype(F32)).astype(BF16)
     keep_ref[512:528] = filled
     give_ref[512:528] = filled
+    raw_ref[512:528] = jnp.concatenate([filled, filled], axis=1)
     for n in range(4):
         copies[n].wait()
+        raw_ref[128 * n : 128 * n + 128] = buf[n]
         one, two = buf[n, :, 0:HD], buf[n, :, HD : 2 * HD]
         keep_ref[128 * n : 128 * n + 128] = jnp.where(first, one, two)
         give_ref[128 * n : 128 * n + 128] = jnp.where(first, two, one)
@@ -59,9 +61,9 @@
     kv_ref[0, 0:528] = keep_ref[...]
     kv_ref[1, 0:528] = got_ref[...]
     full_ref[...] = jnp.zeros_like(full_ref)
-    share = 80 * lax.rem(lax.axis_index("z"), 4)
+    share = 160 * lax.rem(lax.axis_index("z"), 2)
     for m in range(16):
-        full_ref[pl.ds(pl.multiple_of(320 * m + share, 16), 80)] = hw_ref[m]
+        full_ref[pl.ds(pl.multiple_of(320 * m + share, 16), 160)] = hw_ref[m]
     copy.wait()
     both = jnp.dot(ow_ref[...], full_ref[...], preferred_element_type=F32)
     both = both.T.astype(BF16)
@@ -71,27 +73,34 @@
             kv_ref[k, 528 + 16 * a : 544 + 16 * a] = both[at : at + 16]
 
 
+def split_kernel(far_ref, keep_ref, give_ref):
+    first = lax.axis_index("h") == 0
+    one, two = far_ref[:, 0:HD], far_ref[:, HD : 2 * HD]
+    keep_ref[...] = jnp.where(first, one, two)
+    give_ref[...] = jnp.where(first, two, one)
+
+
 def attend(fm_ref, q_ref, planes, emit):
     lane = lax.broadcasted_iota(jnp.int32, (1, HD), 1)
     row_frame = lax.broadcasted_iota(jnp.int32, (256, 1), 0) % 128 // 32
     sources = []
-    for kv_ref, plane in planes:
+    for kv_refs, plane in planes:
         frame = (plane % NZ) // 4
         block_bias = jnp.zeros((256, 1), F32)
         for f in range(FR):
             here = jnp.where(fm_ref[f, frame] == 1, 0.0, NEG)
             block_bias = jnp.where(row_frame == f, here, block_bias)
         block_bias = jnp.broadcast_to(block_bias, (256, 128))
-        for k in range(2):
-            filled = kv_ref[k, 512:528, :].astype(F32)[0:1]
+        for kv_ref in kv_refs:
+            filled = kv_ref[512:528, :].astype(F32)[0:1]
             cache_bias = jnp.where(lane.astype(F32) < filled, 0.0, NEG)
-            sources.append((kv_ref, k, cache_bias, block_bias))
+            sources.append((kv_ref, cache_bias, block_bias))
 
     def block(step, carry):
         q = jnp.concatenate([q_ref[:, 2 * step + i].reshape(128, HD) for i in range(2)], axis=0)
         scores = []
-        for kv_ref, k, cache_bias, block_bias in sources:
-            raw = dot_nt(q, kv_ref[k, 0:256, :]) * C2
+        for kv_ref, cache_bias, block_bias in sources:
+            raw = dot_nt(q, kv_ref[0:256, :]) * C2
             bias = jnp.concatenate(
                 [jnp.broadcast_to(cache_bias, (256, 128)), block_bias], axis=1
             )
@@ -100,11 +109,11 @@
         top = jnp.max(top, axis=1, keepdims=True)
         total = jnp.zeros((256, 256), F32)
         acc = jnp.zeros((256, HD), F32)
-        for score, (kv_ref, k, _, _) in zip(scores, sources):
+        for score, (kv_ref, _, _) in zip(scores, sources):
             weights = jnp.exp2(score - top)
             total = total + weights
             acc = acc + jnp.dot(
-                weights.astype(BF16), kv_ref[k, 256:512, :], preferred_element_type=F32
+                weights.astype(BF16), kv_ref[256:512, :], preferred_element_type=F32
             )
         total = jnp.sum(total, axis=1, keepdims=True)
         attended = (acc / total).astype(BF16)
@@ -118,36 +127,33 @@
     lax.fori_loop(0, 4, block, 0, unroll=4)
 
 
-def shares(*refs):
-    return sum(jnp.concatenate([ref[0, 528:560], ref[1, 528:560]], 0).astype(F32) for ref in refs)
-
-
-def first_kernel(fm_ref, q_ref, kv0_ref, kv3_ref, out_ref, level_ref, both_ref):
+def first_kernel(fm_ref, q_ref, kv_ref, keep_ref, got_ref, out_ref, level_ref):
     z, core = lax.axis_index("z"), lax.rem(lax.axis_index("mp"), 2)
 
     def emit(b, attended, level):
         out_ref[b] = attended
         level_ref[b] = level
 
-    attend(fm_ref, q_ref, ((kv0_ref, z), (kv3_ref, z + NZ - 2 + 4 * core)), emit)
-    both_ref[...] = shares(kv0_ref, kv3_ref)
+    planes = (([kv_ref.at[0], kv_ref.at[1]], z), ([keep_ref, got_ref], z + NZ - 2 + 4 * core))
+    attend(fm_ref, q_ref, planes, emit)
 
 
 def second_kernel(
     fm_ref,
     q_ref,
+    own_ref,
     kv1_ref,
     kv2_ref,
     first_ref,
     first_level_ref,
-    first_both_ref,
     prev_ref,
     out_ref,
     pt_ref,
     level_ref,
 ):
     z = lax.axis_index("z")
-    both = (first_both_ref[...] + shares(kv1_ref, kv2_ref)).astype(BF16)
+    shares = [jnp.concatenate([ref[0, 528:560], ref[1, 528:560]], 0) for ref in (own_ref, kv1_ref)]
+    both = (shares[0].astype(F32) + shares[1].astype(F32)).astype(BF16)
     part = lax.broadcasted_iota(jnp.int32, (8, 128), 0)
 
     def emit(b, attended, level):
@@ -165,7 +171,8 @@
             part == 0, high, jnp.where(part == 1, mid, jnp.where(part == 2, low, 0.0))
         )
 
-    attend(fm_ref, q_ref, ((kv1_ref, z + NZ - 1), (kv2_ref, z + 1)), emit)
+    halves = [[ref.at[0], ref.at[1]] for ref in (kv1_ref, kv2_ref)]
+    attend(fm_ref, q_ref, ((halves[0], z + NZ - 1), (halves[1], z + 1)), emit)
     ship(prev_ref, pt_ref, level_ref, out_ref)
 
 
@@ -371,10 +378,10 @@
             **kw,
         )
 
-    keep, give, q = call(
+    keep, give, raw, q = call(
         pack_kernel,
         "pack",
-        (((528, HD), BF16), ((528, HD), BF16), ((8, 8, 16, HD), BF16)),
+        (((528, HD), BF16), ((528, HD), BF16), ((528, 2 * HD), BF16), ((8, 8, 16, HD), BF16)),
         [hbm] * 6,
         [
             pltpu.VMEM((5, 128, 2 * HD), BF16),
@@ -383,9 +390,17 @@
         ],
         limit=60,
     )(cache_lengths, queries, cache_keys, stretch_keys, cache_values, stretch_values)
-    got = lax.ppermute(give, "h", [(0, 1), (1, 0)])
-    hw = lax.dynamic_slice_in_dim(head_weight, 80 * (z % 4), 80, 0)
-    hw = lax.all_to_all(jnp.broadcast_to(hw[None], (16, 80, 64)), "mp", 0, 0, tiled=True)
+    def swap(x):
+        return lax.ppermute(x, "h", [(0, 1), (1, 0)])
+
+    got = swap(give)
+    far = lax.ppermute(
+        raw,
+        ("z", "mp"),
+        [(16 * i + j, 16 * ((i + (2 if j % 2 == 0 else 14)) % NZ) + j) for i in range(NZ) for j in range(16)],
+    )
+    hw = lax.dynamic_slice_in_dim(head_weight, 160 * (z % 2), 160, 0)
+    hw = lax.all_to_all(jnp.broadcast_to(hw[None], (16, 160, 64)), "mp", 0, 0, tiled=True)
     q, hw = lax.optimization_barrier((q, hw))
     q = lax.all_to_all(q, ("z", "h"), 0, 0, tiled=True, axis_index_groups=FAR)
     kv = call(
@@ -395,23 +410,26 @@
         [vmem] * 3 + [hbm],
         [pltpu.VMEM((HD, 5120), BF16), pltpu.VMEM((5120, 64), BF16), pltpu.SemaphoreType.DMA],
         limit=52,
-        cost_estimate=pl.CostEstimate(flops=10**11, bytes_accessed=10**6, transcendentals=0),
+        cost_estimate=pl.CostEstimate(flops=0, bytes_accessed=10**6, transcendentals=0),
     )(keep, got, hw, out_weight)
     up = lax.ppermute(kv, "z", [(i, (i + 1) % NZ) for i in range(NZ)])
     down = lax.ppermute(kv, "z", [((i + 1) % NZ, i) for i in range(NZ)])
-    two = lax.ppermute(
-        kv,
-        ("z", "mp"),
-        [(16 * i + j, 16 * ((i + (2 if j % 2 == 0 else 14)) % NZ) + j) for i in range(NZ) for j in range(16)],
-    )
     cost = pl.CostEstimate(flops=10**10, bytes_accessed=10**6, transcendentals=10**6)
+    far_keep, far_give = call(
+        split_kernel,
+        "split",
+        (((528, HD), BF16), ((528, HD), BF16)),
+        [vmem],
+        cost_estimate=pl.CostEstimate(flops=10**10, bytes_accessed=10**6, transcendentals=0),
+    )(far)
+    far_got = swap(far_give)
     first = call(
         first_kernel,
         "first",
-        (((8, 128, HD), BF16), ((8, 8, 128), F32), ((64, HD), F32)),
-        [smem] + [vmem] * 3,
+        (((8, 128, HD), BF16), ((8, 8, 128), F32)),
+        [smem] + [vmem] * 4,
         cost_estimate=cost,
-    )(frame_mask, q, kv, two)
+    )(frame_mask, q, kv, far_keep, far_got)
     partial = call(
         second_kernel,
         "second",
@@ -419,7 +437,7 @@
         [smem] + [vmem] * 7,
         [pltpu.VMEM((8, 64, 128), F32), pltpu.VMEM((8, 8, 128), F32)],
         cost_estimate=cost,
-    )(frame_mask, q, up, down, *first, previous_latent)
+    )(frame_mask, q, kv, up, down, *first, previous_latent)
     partial = lax.all_to_all(partial, "z", 0, 0, tiled=True)
     spread = call(spread_kernel, "spread", (((32, 32, 128), BF16),), [vmem, whole], [pltpu.VMEM((16, 32, 128), F32)])(
         partial, previous_latent

time: 105 us -> 104 us (level)
  waiting for transfers between devices: 12.2 us -> 5.18 us
  starting transfers between devices: 37.4 us -> 43.5 us
    ppermute x2 -> x3, starting transfers between devices: 8.31 us -> 17.5 us  [the longest x2 9.22 us: swap(): return lax.ppermute(x, 'h', [(0, 1), (1, 0)])]
    ppermute x2 -> x3, waiting for transfers between devices: 6.91 us -> 0.01 us  [the longest x2 0.01 us: swap(): return lax.ppermute(x, 'h', [(0, 1), (1, 0)])]
    all_to_all x1, starting transfers between devices: 13.6 us -> 8.23 us  [body(): q = lax.all_to_all(q, ('z', 'h'), 0, 0, tiled=True, axis_index_groups=FAR)]
    all_to_all x1, blocking collectives: 23.6 us -> 19.7 us  [body(): partial = lax.all_to_all(partial, 'z', 0, 0, tiled=True)]
    all_to_all x1, blocking collectives: 16 us -> 19.4 us  [body(): spread = lax.all_to_all(spread, ('h', 'mp'), 0, 0, tiled=True)]
    ppermute x1, starting transfers between devices: 2.64 us -> 5.67 us  [body(): down = lax.ppermute(kv, 'z', [((i + 1) % NZ, i) for i in range(NZ)])]
    all_to_all x1, waiting for transfers between devices: 2.85 us -> 0.01 us  [body(): lax.all_to_all(jnp.broadcast_to(hw[None], (16, 160, 64)), 'mp', 0, 0, til...]
    ppermute x1, waiting for transfers between devices: 1.28 us -> 3.33 us  [body(): up = lax.ppermute(kv, 'z', [(i, (i + 1) % NZ) for i in range(NZ)])]
  transfers between devices with their start and end apart: 6 -> 7, of which waited for: 4 -> 2; matrix products, arithmetic and copies ran while one was open for 0% -> 0% of each run, Pallas kernels for 6% -> 7%
where the time goes in v5:
time: 104 us; the launch traced here: 103 us
  starting transfers between devices  43.5 us (42%)
  blocking collectives  39.1 us (38%)
  Pallas kernels  12.2 us (12%)
  waiting for transfers between devices  5.18 us (5%)
  local copies, waits for them, and re-layouts  2.14 us (2%)
    all_to_all x1, blocking collectives, body(): partial = lax.all_to_all(partial, 'z', 0, 0, tiled=True)  19.7 us
    all_to_all x1, blocking collectives, body(): spread = lax.all_to_all(spread, ('h', 'mp'), 0, 0, tiled=True)  19.4 us
    all_to_all x1, starting transfers between devices, body(): lax.all_to_all(jnp.broadcast_to(hw[None], (16, 160, 64)), 'mp', 0, 0, til...  10.2 us
    ppermute x2, starting transfers between devices, swap(): return lax.ppermute(x, 'h', [(0, 1), (1, 0)])  9.22 us
    ppermute x1, starting transfers between devices, body(): lax.ppermute(raw, ('z', 'mp'), [(16 * i + j, 16 * ((i + (2 if j % 2 == 0...  8.24 us
    all_to_all x1, starting transfers between devices, body(): q = lax.all_to_all(q, ('z', 'h'), 0, 0, tiled=True, axis_index_groups=FAR)  8.23 us
    ppermute x1, starting transfers between devices, body(): down = lax.ppermute(kv, 'z', [((i + 1) % NZ, i) for i in range(NZ)])  5.67 us
    pallas_call x1, Pallas kernels, body(): call(second_kernel, 'second', (((NZ, 48, 128), BF16),), [smem] + [vmem] *...  3.45 us
  transfers between devices with their start and end apart: 7, of which 2 were waited for; matrix products, arithmetic and copies ran while one was open for 0% of the time, Pallas kernels for 7%

profile of v5, /device:TPU:1, one launch (start us, length us, event | category | flops | bytes accessed | tf_op | source)
XLA Modules:
  0.0 102.9 jit_solution(14879469110236224418)
XLA Ops:
  0.0 0.0 copy-start
  0.0 0.8 copy-done
  0.8 0.1 constant_dynamic-slice_fusion
  0.9 0.9 broadcast_in_dim.2
  1.7 10.2 %all-to-all-start = ((bf16[16,160,64]{1,2,0:T(8,128)(2,1)}), bf16[16,160,64]{1,2,0:T(8,128)(2,1)S(1)}, u32[]{:S(2)}, u32[]{:S(2)}) async-start(bf16[16,160,64]{1,2,0:T(8,128)(2,1)} %broadcast_in_dim.2), calls=%async_computation | async-start | bytes 1048576 | tf_op jit(solution)/shard_map/all_to_all | solution.py:403
  12.6 1.9 %pack.1 = (bf16[528,128]{1,0:T(8,128)(2,1)}, bf16[528,128]{1,0:T(8,128)(2,1)}, bf16[528,256]{1,0:T(8,128)(2,1)}, bf16[8,8,16,128]{3,2,1,0:T(8,128)(2,1)}) custom-call(s32[1]{0:T(128)S(6)} %copy.16.len_hbm, bf16[128,256]{1,0:T(8,128)(2,1)} %q_hbm.1, bf16[128,256]{1,0:T(8,128)(2,1)} %ck_hbm.1, bf16[128,256]{1,0:T(8,128)(2,1)} %sk_hbm.1, ...), custom_call_target="tpu_custom_call" | custom-call | tf_op jit(solution)/shard_map/pack/pallas_call | solution.py:381
  14.6 8.2 %collective-permute-start.3 = (bf16[528,256]{1,0:T(8,128)(2,1)}, bf16[528,256]{1,0:T(8,128)(2,1)S(1)}, u32[]{:S(2)}, u32[]{:S(2)}) collective-permute-start(bf16[528,256]{1,0:T(8,128)(2,1)} %get-tuple-element.20), channel_id=1, source_target_pairs={{0,64},{1,449},{2,66},{3,451},{4,68},{5,453},{6,70},{7,455},{8,72}... | collective-permute-start | bytes 811016 | tf_op jit(solution)/shard_map/ppermute | solution.py:397
  22.8 4.4 %collective-permute-start = (bf16[528,128]{1,0:T(8,128)(2,1)}, bf16[528,128]{1,0:T(8,128)(2,1)S(1)}, u32[]{:S(2)}, u32[]{:S(2)}) collective-permute-start(bf16[528,128]{1,0:T(8,128)(2,1)} %get-tuple-element.18), channel_id=1, source_target_pairs={{0,16},{16,0},{1,17},{17,1},{2,18},{18,2},{3,19},{19,3},{4,20},{20... | collective-permute-start | bytes 405512 | tf_op jit(solution)/shard_map/ppermute | solution.py:394
  27.2 0.0 all-to-all-done
  27.2 8.2 %all-to-all-start.1 = ((bf16[8,8,16,128]{3,2,1,0:T(8,128)(2,1)}), bf16[8,8,16,128]{3,2,1,0:T(8,128)(2,1)S(1)}, u32[]{:S(2)}, u32[]{:S(2)}) async-start(bf16[8,8,16,128]{3,2,1,0:T(8,128)(2,1)} %get-tuple-element.16), calls=%async_computation.1 | async-start | bytes 524288 | tf_op jit(solution)/shard_map/all_to_all | solution.py:405
  35.4 0.0 copy-start.2
  35.4 0.0 collective-permute-done.3.far_ref
  35.5 0.1 split.1
  35.5 0.0 copy-start.6
  35.5 4.9 %collective-permute-start.4 = (bf16[528,128]{1,0:T(8,128)(2,1)S(1)}, bf16[528,128]{1,0:T(8,128)(2,1)S(1)}, u32[]{:S(2)}, u32[]{:S(2)}) collective-permute-start(bf16[528,128]{1,0:T(8,128)(2,1)S(1)} %get-tuple-element.22), channel_id=1, source_target_pairs={{0,16},{16,0},{1,17},{17,1},{2,18},{18,2},{3,19},{19,3},{4,20},{20... | collective-permute-start | bytes 405512 | tf_op jit(solution)/shard_map/ppermute | solution.py:394
  40.4 0.4 copy.15.hw_ref
  40.8 0.0 collective-permute-done.got_ref
  40.8 0.0 copy-done.2
  40.8 2.1 %pair.1.kv_ref.own_ref = bf16[2,560,128]{2,1,0:T(8,128)(2,1)S(1)} custom-call(bf16[528,128]{1,0:T(8,128)(2,1)S(1)} %copy-done.2, bf16[528,128]{1,0:T(8,128)(2,1)S(1)} %collective-permute-done.got_ref, bf16[16,160,64]{2,1,0:T(8,128)(2,1)S(1)} %copy.15.hw_ref, bf16[256,5120]{1,0:T(8,128)(2,1)} %ow_hbm.1), custom_call_target="tpu_custom_call" | custom-call | bytes 1000000 | tf_op jit(solution)/shard_map/pair/pallas_call | solution.py:406
  42.9 5.7 %collective-permute-start.2 = (bf16[2,560,128]{2,1,0:T(8,128)(2,1)S(1)}, bf16[2,560,128]{2,1,0:T(8,128)(2,1)S(1)}, u32[]{:S(2)}, u32[]{:S(2)}) collective-permute-start(bf16[2,560,128]{2,1,0:T(8,128)(2,1)S(1)} %pair.1.kv_ref.own_ref), channel_id=1, source_target_pairs={{32,0},{64,32},{96,64},{128,96},{160,128},{192,160},{224,192},{256... | collective-permute-start | bytes 860168 | tf_op jit(solution)/shard_map/ppermute | solution.py:416
  48.6 1.9 %collective-permute-start.1 = (bf16[2,560,128]{2,1,0:T(8,128)(2,1)S(1)}, bf16[2,560,128]{2,1,0:T(8,128)(2,1)S(1)}, u32[]{:S(2)}, u32[]{:S(2)}) collective-permute-start(bf16[2,560,128]{2,1,0:T(8,128)(2,1)S(1)} %pair.1.kv_ref.own_ref), channel_id=1, source_target_pairs={{0,32},{32,64},{64,96},{96,128},{128,160},{160,192},{192,224},{224... | collective-permute-start | bytes 860168 | tf_op jit(solution)/shard_map/ppermute | solution.py:415
  50.6 0.0 collective-permute-done.4.got_ref
  50.6 0.0 all-to-all-done.1.q_ref
  50.6 0.0 copy-done.6
  50.6 0.0 copy-start.3
  50.6 2.8 %first.1 = (bf16[8,128,128]{2,1,0:T(8,128)(2,1)S(1)}, f32[8,8,128]{2,1,0:T(8,128)S(1)}) custom-call(s32[4,4]{1,0:T(4,128)S(1)} %copy-done.6, bf16[8,8,16,128]{3,2,1,0:T(8,128)(2,1)S(1)} %all-to-all-done.1.q_ref, bf16[2,560,128]{2,1,0:T(8,128)(2,1)S(1)} %pair.1.kv_ref.own_ref, bf16[528,128]{1,0:T(8,128)(2,1)S(1)} %get-tuple-element.21.keep_ref, ...), custom_call_target="tpu_custom_call" | custom-call | flops 10000000000 | bytes 1000000 | tf_op jit(solution)/shard_map/first/pallas_call | solution.py:426
  53.4 1.8 %collective-permute-done.2.kv2_ref = bf16[2,560,128]{2,1,0:T(8,128)(2,1)S(1)} collective-permute-done((bf16[2,560,128]{2,1,0:T(8,128)(2,1)S(1)}, bf16[2,560,128]{2,1,0:T(8,128)(2,1)S(1)}, u32[]{:S(2)}, u32[]{:S(2)}) %collective-permute-start.2) | collective-permute-done | bytes 286752 | tf_op jit(solution)/shard_map/ppermute | solution.py:416
  55.2 3.3 %collective-permute-done.1.kv1_ref = bf16[2,560,128]{2,1,0:T(8,128)(2,1)S(1)} collective-permute-done((bf16[2,560,128]{2,1,0:T(8,128)(2,1)S(1)}, bf16[2,560,128]{2,1,0:T(8,128)(2,1)S(1)}, u32[]{:S(2)}, u32[]{:S(2)}) %collective-permute-start.1) | collective-permute-done | bytes 286752 | tf_op jit(solution)/shard_map/ppermute | solution.py:415
  58.5 0.0 copy-done.3
  58.5 0.0 copy-start.1
  58.5 0.0 copy-start.4
  58.5 0.0 copy-start.5
  58.5 3.5 %second.1 = bf16[16,48,128]{2,1,0:T(8,128)(2,1)S(1)} custom-call(s32[4,4]{1,0:T(4,128)S(1)} %copy-done.6, bf16[8,8,16,128]{3,2,1,0:T(8,128)(2,1)S(1)} %all-to-all-done.1.q_ref, bf16[2,560,128]{2,1,0:T(8,128)(2,1)S(1)} %pair.1.kv_ref.own_ref, bf16[2,560,128]{2,1,0:T(8,128)(2,1)S(1)} %collective-permute-done.1.kv1_ref, ...), custom_call_target="tpu_custom_call" | custom-call | flops 10000000000 | bytes 1000000 | tf_op jit(solution)/shard_map/second/pallas_call | solution.py:433
  62.0 19.7 %all_to_all.20.y_ref = bf16[16,48,128]{2,1,0:T(8,128)(2,1)S(1)} all-to-all(bf16[16,48,128]{2,1,0:T(8,128)(2,1)S(1)} %second.1), channel_id=1, replica_groups=mesh['z'=16,'h'=2,'mp'=16] {'z'}, dimensions={0} | all-to-all | bytes 393216 | tf_op jit(solution)/shard_map/all_to_all | solution.py:441
  81.7 0.5 spread.1
  82.2 19.4 %all_to_all.21.r_ref = bf16[32,32,128]{2,1,0:T(8,128)(2,1)S(1)} all-to-all(bf16[32,32,128]{2,1,0:T(8,128)(2,1)S(1)} %spread.1), channel_id=1, replica_groups=mesh['z'=16,'h'=2,'mp'=16] {'h','mp'}, dimensions={0} | all-to-all | bytes 524288 | tf_op jit(solution)/shard_map/all_to_all | solution.py:445
  101.6 0.0 copy-done.1
  101.6 0.0 copy-done.4
  101.6 0.0 copy-done.5
  101.6 1.3 %decode.1 = bf16[4,2,4,384]{3,2,1,0:T(4,128)(2,1)} custom-call(bf16[32,32,128]{2,1,0:T(8,128)(2,1)S(1)} %all_to_all.21.r_ref, bf16[3,3,3,16,384]{4,3,2,1,0:T(8,128)(2,1)S(1)} %copy-done.1, f32[384]{0:T(512)S(1)} %copy-done.4, f32[384]{0:T(512)S(1)} %copy-done.5), custom_call_target="tpu_custom_call" | custom-call | tf_op jit(solution)/shard_map/decode/pallas_call | solution.py:446
Async XLA Ops:
  0.0 0.8 copy-start
  1.7 25.5 %all-to-all-start = ((bf16[16,160,64]{1,2,0:T(8,128)(2,1)}), bf16[16,160,64]{1,2,0:T(8,128)(2,1)S(1)}, u32[]{:S(2)}, u32[]{:S(2)}) async-start(bf16[16,160,64]{1,2,0:T(8,128)(2,1)} %broadcast_in_dim.2), calls=%async_computation | async-start | bytes 1048576 | tf_op jit(solution)/shard_map/all_to_all | solution.py:403
  14.6 20.9 %collective-permute-start.3 = (bf16[528,256]{1,0:T(8,128)(2,1)}, bf16[528,256]{1,0:T(8,128)(2,1)S(1)}, u32[]{:S(2)}, u32[]{:S(2)}) collective-permute-start(bf16[528,256]{1,0:T(8,128)(2,1)} %get-tuple-element.20), channel_id=1, source_target_pairs={{0,64},{1,449},{2,66},{3,451},{4,68},{5,453},{6,70},{7,455},{8,72}... | collective-permute-start | bytes 811016 | tf_op jit(solution)/shard_map/ppermute | solution.py:397
  22.8 17.9 %collective-permute-start = (bf16[528,128]{1,0:T(8,128)(2,1)}, bf16[528,128]{1,0:T(8,128)(2,1)S(1)}, u32[]{:S(2)}, u32[]{:S(2)}) collective-permute-start(bf16[528,128]{1,0:T(8,128)(2,1)} %get-tuple-element.18), channel_id=1, source_target_pairs={{0,16},{16,0},{1,17},{17,1},{2,18},{18,2},{3,19},{19,3},{4,20},{20... | collective-permute-start | bytes 405512 | tf_op jit(solution)/shard_map/ppermute | solution.py:394
  27.2 23.4 %all-to-all-start.1 = ((bf16[8,8,16,128]{3,2,1,0:T(8,128)(2,1)}), bf16[8,8,16,128]{3,2,1,0:T(8,128)(2,1)S(1)}, u32[]{:S(2)}, u32[]{:S(2)}) async-start(bf16[8,8,16,128]{3,2,1,0:T(8,128)(2,1)} %get-tuple-element.16), calls=%async_computation.1 | async-start | bytes 524288 | tf_op jit(solution)/shard_map/all_to_all | solution.py:405
  35.4 5.4 %copy-start.2 = (bf16[528,128]{1,0:T(8,128)(2,1)S(1)}, bf16[528,128]{1,0:T(8,128)(2,1)}, u32[]{:S(2)}) copy-start(bf16[528,128]{1,0:T(8,128)(2,1)} %get-tuple-element.17.keep_ref) | copy-start | bytes 405508
  35.5 15.1 %copy-start.6 = (s32[4,4]{1,0:T(4,128)S(1)}, s32[4,4]{1,0:T(4,128)}, u32[]{:S(2)}) copy-start(s32[4,4]{1,0:T(4,128)} %fm_ref.3) | copy-start | bytes 196
  35.5 15.0 %collective-permute-start.4 = (bf16[528,128]{1,0:T(8,128)(2,1)S(1)}, bf16[528,128]{1,0:T(8,128)(2,1)S(1)}, u32[]{:S(2)}, u32[]{:S(2)}) collective-permute-start(bf16[528,128]{1,0:T(8,128)(2,1)S(1)} %get-tuple-element.22), channel_id=1, source_target_pairs={{0,16},{16,0},{1,17},{17,1},{2,18},{18,2},{3,19},{19,3},{4,20},{20... | collective-permute-start | bytes 405512 | tf_op jit(solution)/shard_map/ppermute | solution.py:394
  42.9 12.3 %collective-permute-start.2 = (bf16[2,560,128]{2,1,0:T(8,128)(2,1)S(1)}, bf16[2,560,128]{2,1,0:T(8,128)(2,1)S(1)}, u32[]{:S(2)}, u32[]{:S(2)}) collective-permute-start(bf16[2,560,128]{2,1,0:T(8,128)(2,1)S(1)} %pair.1.kv_ref.own_ref), channel_id=1, source_target_pairs={{32,0},{64,32},{96,64},{128,96},{160,128},{192,160},{224,192},{256... | collective-permute-start | bytes 860168 | tf_op jit(solution)/shard_map/ppermute | solution.py:416
  48.6 9.9 %collective-permute-start.1 = (bf16[2,560,128]{2,1,0:T(8,128)(2,1)S(1)}, bf16[2,560,128]{2,1,0:T(8,128)(2,1)S(1)}, u32[]{:S(2)}, u32[]{:S(2)}) collective-permute-start(bf16[2,560,128]{2,1,0:T(8,128)(2,1)S(1)} %pair.1.kv_ref.own_ref), channel_id=1, source_target_pairs={{0,32},{32,64},{64,96},{96,128},{128,160},{160,192},{192,224},{224... | collective-permute-start | bytes 860168 | tf_op jit(solution)/shard_map/ppermute | solution.py:415
  50.6 7.9 %copy-start.3 = (bf16[2,2,4,16]{3,2,1,0:T(4,128)(2,1)S(1)}, bf16[2,2,4,16]{3,2,1,0:T(4,128)(2,1)}, u32[]{:S(2)}) copy-start(bf16[2,2,4,16]{3,2,1,0:T(4,128)(2,1)} %prev_ref.3) | copy-start | bytes 1540
  58.5 43.0 %copy-start.1 = (bf16[3,3,3,16,384]{4,3,2,1,0:T(8,128)(2,1)S(1)}, bf16[3,3,3,16,384]{4,3,2,1,0:T(8,128)(2,1)}, u32[]{:S(2)}) copy-start(bf16[3,3,3,16,384]{4,3,2,1,0:T(8,128)(2,1)} %w_ref.1) | copy-start | bytes 995332
  58.5 43.0 %copy-start.4 = (f32[384]{0:T(512)S(1)}, f32[384]{0:T(512)}, u32[]{:S(2)}) copy-start(f32[384]{0:T(512)} %bias_ref.1) | copy-start | bytes 4612
  58.5 43.0 %copy-start.5 = (f32[384]{0:T(512)S(1)}, f32[384]{0:T(512)}, u32[]{:S(2)}) copy-start(f32[384]{0:T(512)} %gain_ref.1) | copy-start | bytes 4612

commit v6 on v5

--- a/solution.py
+++ b/solution.py
@@ -47,12 +47,15 @@
         keep_ref[128 * n : 128 * n + 128] = jnp.where(first, one, two)
         give_ref[128 * n : 128 * n + 128] = jnp.where(first, two, one)
     copies[4].wait()
-    for k in range(2):
-        for b in range(8):
-            for r in range(2):
-                part = buf[4, 64 * r + 8 * b : 64 * r + 8 * b + 8, HD * k : HD * k + HD]
+    for n in range(4):
+        above = buf[4, 16 * n : 16 * n + 16, :].astype(F32)
+        under = buf[4, 64 + 16 * n : 80 + 16 * n, :].astype(F32)
+        for b in range(2):
+            here = slice(8 * b, 8 * b + 8)
+            rows = jnp.concatenate([above[here], under[here]], axis=0).astype(BF16)
+            for k in range(2):
                 for j in range(4):
-                    qo_ref[2 * j + k, b, 8 * r : 8 * r + 8] = part
+                    qo_ref[2 * j + k, 2 * n + b] = rows[:, HD * k : HD * k + HD]
 
 
 def pair_kernel(keep_ref, got_ref, hw_ref, ow_hbm, kv_ref, ow_ref, full_ref, sem):
@@ -177,8 +180,9 @@
 
 
 def ship(prev_ref, pt_ref, level_ref, out_ref):
-    edge = [prev_ref[f, a, 3 * e : 3 * e + 1, :] for e in range(2) for f in range(2) for a in range(2)]
-    edge = jnp.concatenate([x.astype(F32) for x in edge], axis=1)
+    cells = [[prev_ref[f, a].astype(F32) for a in range(2)] for f in range(2)]
+    edge = [cells[f][a][3 * e : 3 * e + 1] for e in range(2) for f in range(2) for a in range(2)]
+    edge = jnp.concatenate(edge, axis=1)
     column = lax.broadcasted_iota(jnp.int32, (32, 128), 1) % 8
     few = column[0:8]
     part = lax.broadcasted_iota(jnp.int32, (8, 128), 0)
@@ -241,13 +245,12 @@
     ]
     pick = jnp.concatenate([jnp.where(x, 1.0, 0.0).astype(BF16) for x in pick], axis=1)
     lane = lax.broadcasted_iota(jnp.int32, (1, 128), 1)
+    cells = [[prev_ref[f, a].astype(F32) for a in range(2)] for f in range(2)]
     earlier = []
     for c in range(2):
         for f in range(2):
             parts = [
-                prev_ref[f, a, 2 * c + b : 2 * c + b + 1, :].astype(F32)
-                for b in range(2)
-                for a in range(2)
+                cells[f][a][2 * c + b : 2 * c + b + 1] for b in range(2) for a in range(2)
             ]
             earlier.append(jnp.concatenate([jnp.zeros((1, 64), F32)] + parts, axis=1))
     rim = y_ref[jnp.maximum(z - 1, 0), 32:48].astype(F32)[11:12]

time: 104 us -> 104 us (level)
  no operation moved by 1% of the time
where the time goes in v6:
time: 104 us; the launch traced here: 103 us
  starting transfers between devices  43.5 us (42%)
  blocking collectives  39.1 us (38%)
  Pallas kernels  12.2 us (12%)
  waiting for transfers between devices  5.18 us (5%)
  local copies, waits for them, and re-layouts  2.14 us (2%)
    all_to_all x1, blocking collectives, body(): partial = lax.all_to_all(partial, 'z', 0, 0, tiled=True)  19.7 us
    all_to_all x1, blocking collectives, body(): spread = lax.all_to_all(spread, ('h', 'mp'), 0, 0, tiled=True)  19.4 us
    all_to_all x1, starting transfers between devices, body(): lax.all_to_all(jnp.broadcast_to(hw[None], (16, 160, 64)), 'mp', 0, 0, til...  10.2 us
    ppermute x2, starting transfers between devices, swap(): return lax.ppermute(x, 'h', [(0, 1), (1, 0)])  9.22 us
    ppermute x1, starting transfers between devices, body(): lax.ppermute(raw, ('z', 'mp'), [(16 * i + j, 16 * ((i + (2 if j % 2 == 0...  8.24 us
    all_to_all x1, starting transfers between devices, body(): q = lax.all_to_all(q, ('z', 'h'), 0, 0, tiled=True, axis_index_groups=FAR)  8.23 us
    ppermute x1, starting transfers between devices, body(): down = lax.ppermute(kv, 'z', [((i + 1) % NZ, i) for i in range(NZ)])  5.67 us
    pallas_call x1, Pallas kernels, body(): call(second_kernel, 'second', (((NZ, 48, 128), BF16),), [smem] + [vmem] *...  3.46 us
  transfers between devices with their start and end apart: 7, of which 2 were waited for; matrix products, arithmetic and copies ran while one was open for 0% of the time, Pallas kernels for 7%

profile of v6, /device:TPU:1, one launch (start us, length us, event | category | flops | bytes accessed | tf_op | source)
XLA Modules:
  0.0 102.9 jit_solution(13796962535387015695)
XLA Ops:
  0.0 0.0 copy-start
  0.0 0.8 copy-done
  0.8 0.1 constant_dynamic-slice_fusion
  0.9 0.9 broadcast_in_dim.2
  1.7 10.2 %all-to-all-start = ((bf16[16,160,64]{1,2,0:T(8,128)(2,1)}), bf16[16,160,64]{1,2,0:T(8,128)(2,1)S(1)}, u32[]{:S(2)}, u32[]{:S(2)}) async-start(bf16[16,160,64]{1,2,0:T(8,128)(2,1)} %broadcast_in_dim.2), calls=%async_computation | async-start | bytes 1048576 | tf_op jit(solution)/shard_map/all_to_all | solution.py:406
  12.6 1.9 %pack.1 = (bf16[528,128]{1,0:T(8,128)(2,1)}, bf16[528,128]{1,0:T(8,128)(2,1)}, bf16[528,256]{1,0:T(8,128)(2,1)}, bf16[8,8,16,128]{3,2,1,0:T(8,128)(2,1)}) custom-call(s32[1]{0:T(128)S(6)} %copy.16.len_hbm, bf16[128,256]{1,0:T(8,128)(2,1)} %q_hbm.1, bf16[128,256]{1,0:T(8,128)(2,1)} %ck_hbm.1, bf16[128,256]{1,0:T(8,128)(2,1)} %sk_hbm.1, ...), custom_call_target="tpu_custom_call" | custom-call | tf_op jit(solution)/shard_map/pack/pallas_call | solution.py:384
  14.6 8.2 %collective-permute-start.3 = (bf16[528,256]{1,0:T(8,128)(2,1)}, bf16[528,256]{1,0:T(8,128)(2,1)S(1)}, u32[]{:S(2)}, u32[]{:S(2)}) collective-permute-start(bf16[528,256]{1,0:T(8,128)(2,1)} %get-tuple-element.20), channel_id=1, source_target_pairs={{0,64},{1,449},{2,66},{3,451},{4,68},{5,453},{6,70},{7,455},{8,72}... | collective-permute-start | bytes 811016 | tf_op jit(solution)/shard_map/ppermute | solution.py:400
  22.8 4.4 %collective-permute-start = (bf16[528,128]{1,0:T(8,128)(2,1)}, bf16[528,128]{1,0:T(8,128)(2,1)S(1)}, u32[]{:S(2)}, u32[]{:S(2)}) collective-permute-start(bf16[528,128]{1,0:T(8,128)(2,1)} %get-tuple-element.18), channel_id=1, source_target_pairs={{0,16},{16,0},{1,17},{17,1},{2,18},{18,2},{3,19},{19,3},{4,20},{20... | collective-permute-start | bytes 405512 | tf_op jit(solution)/shard_map/ppermute | solution.py:397
  27.2 0.0 all-to-all-done
  27.2 8.2 %all-to-all-start.1 = ((bf16[8,8,16,128]{3,2,1,0:T(8,128)(2,1)}), bf16[8,8,16,128]{3,2,1,0:T(8,128)(2,1)S(1)}, u32[]{:S(2)}, u32[]{:S(2)}) async-start(bf16[8,8,16,128]{3,2,1,0:T(8,128)(2,1)} %get-tuple-element.16), calls=%async_computation.1 | async-start | bytes 524288 | tf_op jit(solution)/shard_map/all_to_all | solution.py:408
  35.4 0.0 copy-start.2
  35.4 0.0 collective-permute-done.3.far_ref
  35.5 0.1 split.1
  35.5 0.0 copy-start.6
  35.5 4.9 %collective-permute-start.4 = (bf16[528,128]{1,0:T(8,128)(2,1)S(1)}, bf16[528,128]{1,0:T(8,128)(2,1)S(1)}, u32[]{:S(2)}, u32[]{:S(2)}) collective-permute-start(bf16[528,128]{1,0:T(8,128)(2,1)S(1)} %get-tuple-element.22), channel_id=1, source_target_pairs={{0,16},{16,0},{1,17},{17,1},{2,18},{18,2},{3,19},{19,3},{4,20},{20... | collective-permute-start | bytes 405512 | tf_op jit(solution)/shard_map/ppermute | solution.py:397
  40.4 0.4 copy.15.hw_ref
  40.8 0.0 collective-permute-done.got_ref
  40.8 0.0 copy-done.2
  40.8 2.1 %pair.1.kv_ref.own_ref = bf16[2,560,128]{2,1,0:T(8,128)(2,1)S(1)} custom-call(bf16[528,128]{1,0:T(8,128)(2,1)S(1)} %copy-done.2, bf16[528,128]{1,0:T(8,128)(2,1)S(1)} %collective-permute-done.got_ref, bf16[16,160,64]{2,1,0:T(8,128)(2,1)S(1)} %copy.15.hw_ref, bf16[256,5120]{1,0:T(8,128)(2,1)} %ow_hbm.1), custom_call_target="tpu_custom_call" | custom-call | bytes 1000000 | tf_op jit(solution)/shard_map/pair/pallas_call | solution.py:409
  42.9 5.7 %collective-permute-start.2 = (bf16[2,560,128]{2,1,0:T(8,128)(2,1)S(1)}, bf16[2,560,128]{2,1,0:T(8,128)(2,1)S(1)}, u32[]{:S(2)}, u32[]{:S(2)}) collective-permute-start(bf16[2,560,128]{2,1,0:T(8,128)(2,1)S(1)} %pair.1.kv_ref.own_ref), channel_id=1, source_target_pairs={{32,0},{64,32},{96,64},{128,96},{160,128},{192,160},{224,192},{256... | collective-permute-start | bytes 860168 | tf_op jit(solution)/shard_map/ppermute | solution.py:419
  48.6 1.9 %collective-permute-start.1 = (bf16[2,560,128]{2,1,0:T(8,128)(2,1)S(1)}, bf16[2,560,128]{2,1,0:T(8,128)(2,1)S(1)}, u32[]{:S(2)}, u32[]{:S(2)}) collective-permute-start(bf16[2,560,128]{2,1,0:T(8,128)(2,1)S(1)} %pair.1.kv_ref.own_ref), channel_id=1, source_target_pairs={{0,32},{32,64},{64,96},{96,128},{128,160},{160,192},{192,224},{224... | collective-permute-start | bytes 860168 | tf_op jit(solution)/shard_map/ppermute | solution.py:418
  50.6 0.0 collective-permute-done.4.got_ref
  50.6 0.0 all-to-all-done.1.q_ref
  50.6 0.0 copy-done.6
  50.6 0.0 copy-start.3
  50.6 2.8 %first.1 = (bf16[8,128,128]{2,1,0:T(8,128)(2,1)S(1)}, f32[8,8,128]{2,1,0:T(8,128)S(1)}) custom-call(s32[4,4]{1,0:T(4,128)S(1)} %copy-done.6, bf16[8,8,16,128]{3,2,1,0:T(8,128)(2,1)S(1)} %all-to-all-done.1.q_ref, bf16[2,560,128]{2,1,0:T(8,128)(2,1)S(1)} %pair.1.kv_ref.own_ref, bf16[528,128]{1,0:T(8,128)(2,1)S(1)} %get-tuple-element.21.keep_ref, ...), custom_call_target="tpu_custom_call" | custom-call | flops 10000000000 | bytes 1000000 | tf_op jit(solution)/shard_map/first/pallas_call | solution.py:429
  53.4 1.8 %collective-permute-done.2.kv2_ref = bf16[2,560,128]{2,1,0:T(8,128)(2,1)S(1)} collective-permute-done((bf16[2,560,128]{2,1,0:T(8,128)(2,1)S(1)}, bf16[2,560,128]{2,1,0:T(8,128)(2,1)S(1)}, u32[]{:S(2)}, u32[]{:S(2)}) %collective-permute-start.2) | collective-permute-done | bytes 286752 | tf_op jit(solution)/shard_map/ppermute | solution.py:419
  55.2 3.3 %collective-permute-done.1.kv1_ref = bf16[2,560,128]{2,1,0:T(8,128)(2,1)S(1)} collective-permute-done((bf16[2,560,128]{2,1,0:T(8,128)(2,1)S(1)}, bf16[2,560,128]{2,1,0:T(8,128)(2,1)S(1)}, u32[]{:S(2)}, u32[]{:S(2)}) %collective-permute-start.1) | collective-permute-done | bytes 286752 | tf_op jit(solution)/shard_map/ppermute | solution.py:418
  58.5 0.0 copy-done.3
  58.5 0.0 copy-start.1
  58.5 0.0 copy-start.4
  58.5 0.0 copy-start.5
  58.5 3.5 %second.1 = bf16[16,48,128]{2,1,0:T(8,128)(2,1)S(1)} custom-call(s32[4,4]{1,0:T(4,128)S(1)} %copy-done.6, bf16[8,8,16,128]{3,2,1,0:T(8,128)(2,1)S(1)} %all-to-all-done.1.q_ref, bf16[2,560,128]{2,1,0:T(8,128)(2,1)S(1)} %pair.1.kv_ref.own_ref, bf16[2,560,128]{2,1,0:T(8,128)(2,1)S(1)} %collective-permute-done.1.kv1_ref, ...), custom_call_target="tpu_custom_call" | custom-call | flops 10000000000 | bytes 1000000 | tf_op jit(solution)/shard_map/second/pallas_call | solution.py:436
  62.0 19.7 %all_to_all.20.y_ref = bf16[16,48,128]{2,1,0:T(8,128)(2,1)S(1)} all-to-all(bf16[16,48,128]{2,1,0:T(8,128)(2,1)S(1)} %second.1), channel_id=1, replica_groups=mesh['z'=16,'h'=2,'mp'=16] {'z'}, dimensions={0} | all-to-all | bytes 393216 | tf_op jit(solution)/shard_map/all_to_all | solution.py:444
  81.7 0.5 spread.1
  82.2 19.4 %all_to_all.21.r_ref = bf16[32,32,128]{2,1,0:T(8,128)(2,1)S(1)} all-to-all(bf16[32,32,128]{2,1,0:T(8,128)(2,1)S(1)} %spread.1), channel_id=1, replica_groups=mesh['z'=16,'h'=2,'mp'=16] {'h','mp'}, dimensions={0} | all-to-all | bytes 524288 | tf_op jit(solution)/shard_map/all_to_all | solution.py:448
  101.6 0.0 copy-done.1
  101.6 0.0 copy-done.4
  101.6 0.0 copy-done.5
  101.6 1.3 %decode.1 = bf16[4,2,4,384]{3,2,1,0:T(4,128)(2,1)} custom-call(bf16[32,32,128]{2,1,0:T(8,128)(2,1)S(1)} %all_to_all.21.r_ref, bf16[3,3,3,16,384]{4,3,2,1,0:T(8,128)(2,1)S(1)} %copy-done.1, f32[384]{0:T(512)S(1)} %copy-done.4, f32[384]{0:T(512)S(1)} %copy-done.5), custom_call_target="tpu_custom_call" | custom-call | tf_op jit(solution)/shard_map/decode/pallas_call | solution.py:449
Async XLA Ops:
  0.0 0.8 copy-start
  1.7 25.5 %all-to-all-start = ((bf16[16,160,64]{1,2,0:T(8,128)(2,1)}), bf16[16,160,64]{1,2,0:T(8,128)(2,1)S(1)}, u32[]{:S(2)}, u32[]{:S(2)}) async-start(bf16[16,160,64]{1,2,0:T(8,128)(2,1)} %broadcast_in_dim.2), calls=%async_computation | async-start | bytes 1048576 | tf_op jit(solution)/shard_map/all_to_all | solution.py:406
  14.6 20.9 %collective-permute-start.3 = (bf16[528,256]{1,0:T(8,128)(2,1)}, bf16[528,256]{1,0:T(8,128)(2,1)S(1)}, u32[]{:S(2)}, u32[]{:S(2)}) collective-permute-start(bf16[528,256]{1,0:T(8,128)(2,1)} %get-tuple-element.20), channel_id=1, source_target_pairs={{0,64},{1,449},{2,66},{3,451},{4,68},{5,453},{6,70},{7,455},{8,72}... | collective-permute-start | bytes 811016 | tf_op jit(solution)/shard_map/ppermute | solution.py:400
  22.8 17.9 %collective-permute-start = (bf16[528,128]{1,0:T(8,128)(2,1)}, bf16[528,128]{1,0:T(8,128)(2,1)S(1)}, u32[]{:S(2)}, u32[]{:S(2)}) collective-permute-start(bf16[528,128]{1,0:T(8,128)(2,1)} %get-tuple-element.18), channel_id=1, source_target_pairs={{0,16},{16,0},{1,17},{17,1},{2,18},{18,2},{3,19},{19,3},{4,20},{20... | collective-permute-start | bytes 405512 | tf_op jit(solution)/shard_map/ppermute | solution.py:397
  27.2 23.4 %all-to-all-start.1 = ((bf16[8,8,16,128]{3,2,1,0:T(8,128)(2,1)}), bf16[8,8,16,128]{3,2,1,0:T(8,128)(2,1)S(1)}, u32[]{:S(2)}, u32[]{:S(2)}) async-start(bf16[8,8,16,128]{3,2,1,0:T(8,128)(2,1)} %get-tuple-element.16), calls=%async_computation.1 | async-start | bytes 524288 | tf_op jit(solution)/shard_map/all_to_all | solution.py:408
  35.4 5.4 %copy-start.2 = (bf16[528,128]{1,0:T(8,128)(2,1)S(1)}, bf16[528,128]{1,0:T(8,128)(2,1)}, u32[]{:S(2)}) copy-start(bf16[528,128]{1,0:T(8,128)(2,1)} %get-tuple-element.17.keep_ref) | copy-start | bytes 405508
  35.5 15.1 %copy-start.6 = (s32[4,4]{1,0:T(4,128)S(1)}, s32[4,4]{1,0:T(4,128)}, u32[]{:S(2)}) copy-start(s32[4,4]{1,0:T(4,128)} %fm_ref.3) | copy-start | bytes 196
  35.5 15.0 %collective-permute-start.4 = (bf16[528,128]{1,0:T(8,128)(2,1)S(1)}, bf16[528,128]{1,0:T(8,128)(2,1)S(1)}, u32[]{:S(2)}, u32[]{:S(2)}) collective-permute-start(bf16[528,128]{1,0:T(8,128)(2,1)S(1)} %get-tuple-element.22), channel_id=1, source_target_pairs={{0,16},{16,0},{1,17},{17,1},{2,18},{18,2},{3,19},{19,3},{4,20},{20... | collective-permute-start | bytes 405512 | tf_op jit(solution)/shard_map/ppermute | solution.py:397
  42.9 12.3 %collective-permute-start.2 = (bf16[2,560,128]{2,1,0:T(8,128)(2,1)S(1)}, bf16[2,560,128]{2,1,0:T(8,128)(2,1)S(1)}, u32[]{:S(2)}, u32[]{:S(2)}) collective-permute-start(bf16[2,560,128]{2,1,0:T(8,128)(2,1)S(1)} %pair.1.kv_ref.own_ref), channel_id=1, source_target_pairs={{32,0},{64,32},{96,64},{128,96},{160,128},{192,160},{224,192},{256... | collective-permute-start | bytes 860168 | tf_op jit(solution)/shard_map/ppermute | solution.py:419
  48.6 9.9 %collective-permute-start.1 = (bf16[2,560,128]{2,1,0:T(8,128)(2,1)S(1)}, bf16[2,560,128]{2,1,0:T(8,128)(2,1)S(1)}, u32[]{:S(2)}, u32[]{:S(2)}) collective-permute-start(bf16[2,560,128]{2,1,0:T(8,128)(2,1)S(1)} %pair.1.kv_ref.own_ref), channel_id=1, source_target_pairs={{0,32},{32,64},{64,96},{96,128},{128,160},{160,192},{192,224},{224... | collective-permute-start | bytes 860168 | tf_op jit(solution)/shard_map/ppermute | solution.py:418
  50.6 7.9 %copy-start.3 = (bf16[2,2,4,16]{3,2,1,0:T(4,128)(2,1)S(1)}, bf16[2,2,4,16]{3,2,1,0:T(4,128)(2,1)}, u32[]{:S(2)}) copy-start(bf16[2,2,4,16]{3,2,1,0:T(4,128)(2,1)} %prev_ref.3) | copy-start | bytes 1540
  58.5 43.0 %copy-start.1 = (bf16[3,3,3,16,384]{4,3,2,1,0:T(8,128)(2,1)S(1)}, bf16[3,3,3,16,384]{4,3,2,1,0:T(8,128)(2,1)}, u32[]{:S(2)}) copy-start(bf16[3,3,3,16,384]{4,3,2,1,0:T(8,128)(2,1)} %w_ref.1) | copy-start | bytes 995332
  58.5 43.0 %copy-start.4 = (f32[384]{0:T(512)S(1)}, f32[384]{0:T(512)}, u32[]{:S(2)}) copy-start(f32[384]{0:T(512)} %bias_ref.1) | copy-start | bytes 4612
  58.5 43.0 %copy-start.5 = (f32[384]{0:T(512)S(1)}, f32[384]{0:T(512)}, u32[]{:S(2)}) copy-start(f32[384]{0:T(512)} %gain_ref.1) | copy-start | bytes 4612

commit v7 on v6

--- a/solution.py
+++ b/solution.py
@@ -58,17 +58,24 @@
                     qo_ref[2 * j + k, 2 * n + b] = rows[:, HD * k : HD * k + HD]
 
 
-def pair_kernel(keep_ref, got_ref, hw_ref, ow_hbm, kv_ref, ow_ref, full_ref, sem):
-    copy = pltpu.make_async_copy(ow_hbm.at[pl.ds(lax.axis_index("h") * HD, HD)], ow_ref, sem)
-    copy.start()
+def pair_kernel(keep_ref, got_ref, hw_ref, ow_hbm, kv_ref, ow_ref, full_ref, sems):
+    rows = pl.ds(lax.axis_index("h") * HD, HD)
+    copies = []
+    for n in range(4):
+        part = slice(1280 * n, 1280 * n + 1280)
+        copies.append(pltpu.make_async_copy(ow_hbm.at[rows, part], ow_ref.at[:, part], sems.at[n]))
+        copies[n].start()
     kv_ref[0, 0:528] = keep_ref[...]
     kv_ref[1, 0:528] = got_ref[...]
     full_ref[...] = jnp.zeros_like(full_ref)
     share = 160 * lax.rem(lax.axis_index("z"), 2)
     for m in range(16):
         full_ref[pl.ds(pl.multiple_of(320 * m + share, 16), 160)] = hw_ref[m]
-    copy.wait()
-    both = jnp.dot(ow_ref[...], full_ref[...], preferred_element_type=F32)
+    both = jnp.zeros((HD, 64), F32)
+    for n in range(4):
+        copies[n].wait()
+        part = slice(1280 * n, 1280 * n + 1280)
+        both = both + jnp.dot(ow_ref[:, part], full_ref[part], preferred_element_type=F32)
     both = both.T.astype(BF16)
     for k in range(2):
         for a in range(2):
@@ -411,7 +418,11 @@
         "pair",
         (((2, 560, HD), BF16),),
         [vmem] * 3 + [hbm],
-        [pltpu.VMEM((HD, 5120), BF16), pltpu.VMEM((5120, 64), BF16), pltpu.SemaphoreType.DMA],
+        [
+            pltpu.VMEM((HD, 5120), BF16),
+            pltpu.VMEM((5120, 64), BF16),
+            pltpu.SemaphoreType.DMA((4,)),
+        ],
         limit=52,
         cost_estimate=pl.CostEstimate(flops=0, bytes_accessed=10**6, transcendentals=0),
     )(keep, got, hw, out_weight)

time: 104 us -> 104 us (level)
  no operation moved by 1% of the time
where the time goes in v7:
time: 104 us; the launch traced here: 103 us
  starting transfers between devices  43.5 us (42%)
  blocking collectives  39.1 us (38%)
  Pallas kernels  12.3 us (12%)
  waiting for transfers between devices  5 us (5%)
  local copies, waits for them, and re-layouts  2.14 us (2%)
    all_to_all x1, blocking collectives, body(): partial = lax.all_to_all(partial, 'z', 0, 0, tiled=True)  19.7 us
    all_to_all x1, blocking collectives, body(): spread = lax.all_to_all(spread, ('h', 'mp'), 0, 0, tiled=True)  19.4 us
    all_to_all x1, starting transfers between devices, body(): lax.all_to_all(jnp.broadcast_to(hw[None], (16, 160, 64)), 'mp', 0, 0, til...  10.2 us
    ppermute x2, starting transfers between devices, swap(): return lax.ppermute(x, 'h', [(0, 1), (1, 0)])  9.22 us
    ppermute x1, starting transfers between devices, body(): lax.ppermute(raw, ('z', 'mp'), [(16 * i + j, 16 * ((i + (2 if j % 2 == 0...  8.24 us
    all_to_all x1, starting transfers between devices, body(): q = lax.all_to_all(q, ('z', 'h'), 0, 0, tiled=True, axis_index_groups=FAR)  8.23 us
    ppermute x1, starting transfers between devices, body(): down = lax.ppermute(kv, 'z', [((i + 1) % NZ, i) for i in range(NZ)])  5.67 us
    pallas_call x1, Pallas kernels, body(): call(second_kernel, 'second', (((NZ, 48, 128), BF16),), [smem] + [vmem] *...  3.46 us
  transfers between devices with their start and end apart: 7, of which 2 were waited for; matrix products, arithmetic and copies ran while one was open for 0% of the time, Pallas kernels for 7%

profile of v7, /device:TPU:1, one launch (start us, length us, event | category | flops | bytes accessed | tf_op | source)
XLA Modules:
  0.0 102.9 jit_solution(6826628454823272785)
XLA Ops:
  0.0 0.0 copy-start
  0.0 0.8 copy-done
  0.8 0.1 constant_dynamic-slice_fusion
  0.9 0.9 broadcast_in_dim.2
  1.7 10.2 %all-to-all-start = ((bf16[16,160,64]{1,2,0:T(8,128)(2,1)}), bf16[16,160,64]{1,2,0:T(8,128)(2,1)S(1)}, u32[]{:S(2)}, u32[]{:S(2)}) async-start(bf16[16,160,64]{1,2,0:T(8,128)(2,1)} %broadcast_in_dim.2), calls=%async_computation | async-start | bytes 1048576 | tf_op jit(solution)/shard_map/all_to_all | solution.py:413
  12.6 1.9 %pack.1 = (bf16[528,128]{1,0:T(8,128)(2,1)}, bf16[528,128]{1,0:T(8,128)(2,1)}, bf16[528,256]{1,0:T(8,128)(2,1)}, bf16[8,8,16,128]{3,2,1,0:T(8,128)(2,1)}) custom-call(s32[1]{0:T(128)S(6)} %copy.16.len_hbm, bf16[128,256]{1,0:T(8,128)(2,1)} %q_hbm.1, bf16[128,256]{1,0:T(8,128)(2,1)} %ck_hbm.1, bf16[128,256]{1,0:T(8,128)(2,1)} %sk_hbm.1, ...), custom_call_target="tpu_custom_call" | custom-call | tf_op jit(solution)/shard_map/pack/pallas_call | solution.py:391
  14.6 8.2 %collective-permute-start.3 = (bf16[528,256]{1,0:T(8,128)(2,1)}, bf16[528,256]{1,0:T(8,128)(2,1)S(1)}, u32[]{:S(2)}, u32[]{:S(2)}) collective-permute-start(bf16[528,256]{1,0:T(8,128)(2,1)} %get-tuple-element.20), channel_id=1, source_target_pairs={{0,64},{1,449},{2,66},{3,451},{4,68},{5,453},{6,70},{7,455},{8,72}... | collective-permute-start | bytes 811016 | tf_op jit(solution)/shard_map/ppermute | solution.py:407
  22.8 4.4 %collective-permute-start = (bf16[528,128]{1,0:T(8,128)(2,1)}, bf16[528,128]{1,0:T(8,128)(2,1)S(1)}, u32[]{:S(2)}, u32[]{:S(2)}) collective-permute-start(bf16[528,128]{1,0:T(8,128)(2,1)} %get-tuple-element.18), channel_id=1, source_target_pairs={{0,16},{16,0},{1,17},{17,1},{2,18},{18,2},{3,19},{19,3},{4,20},{20... | collective-permute-start | bytes 405512 | tf_op jit(solution)/shard_map/ppermute | solution.py:404
  27.2 0.0 all-to-all-done
  27.2 8.2 %all-to-all-start.1 = ((bf16[8,8,16,128]{3,2,1,0:T(8,128)(2,1)}), bf16[8,8,16,128]{3,2,1,0:T(8,128)(2,1)S(1)}, u32[]{:S(2)}, u32[]{:S(2)}) async-start(bf16[8,8,16,128]{3,2,1,0:T(8,128)(2,1)} %get-tuple-element.16), calls=%async_computation.1 | async-start | bytes 524288 | tf_op jit(solution)/shard_map/all_to_all | solution.py:415
  35.4 0.0 copy-start.2
  35.4 0.0 collective-permute-done.3.far_ref
  35.5 0.1 split.1
  35.5 0.0 copy-start.6
  35.5 4.9 %collective-permute-start.4 = (bf16[528,128]{1,0:T(8,128)(2,1)S(1)}, bf16[528,128]{1,0:T(8,128)(2,1)S(1)}, u32[]{:S(2)}, u32[]{:S(2)}) collective-permute-start(bf16[528,128]{1,0:T(8,128)(2,1)S(1)} %get-tuple-element.22), channel_id=1, source_target_pairs={{0,16},{16,0},{1,17},{17,1},{2,18},{18,2},{3,19},{19,3},{4,20},{20... | collective-permute-start | bytes 405512 | tf_op jit(solution)/shard_map/ppermute | solution.py:404
  40.4 0.4 copy.15.hw_ref
  40.8 0.0 collective-permute-done.got_ref
  40.8 0.0 copy-done.2
  40.8 2.2 %pair.1.kv_ref.own_ref = bf16[2,560,128]{2,1,0:T(8,128)(2,1)S(1)} custom-call(bf16[528,128]{1,0:T(8,128)(2,1)S(1)} %copy-done.2, bf16[528,128]{1,0:T(8,128)(2,1)S(1)} %collective-permute-done.got_ref, bf16[16,160,64]{2,1,0:T(8,128)(2,1)S(1)} %copy.15.hw_ref, bf16[256,5120]{1,0:T(8,128)(2,1)} %ow_hbm.1), custom_call_target="tpu_custom_call" | custom-call | bytes 1000000 | tf_op jit(solution)/shard_map/pair/pallas_call | solution.py:416
  43.0 5.7 %collective-permute-start.2 = (bf16[2,560,128]{2,1,0:T(8,128)(2,1)S(1)}, bf16[2,560,128]{2,1,0:T(8,128)(2,1)S(1)}, u32[]{:S(2)}, u32[]{:S(2)}) collective-permute-start(bf16[2,560,128]{2,1,0:T(8,128)(2,1)S(1)} %pair.1.kv_ref.own_ref), channel_id=1, source_target_pairs={{32,0},{64,32},{96,64},{128,96},{160,128},{192,160},{224,192},{256... | collective-permute-start | bytes 860168 | tf_op jit(solution)/shard_map/ppermute | solution.py:430
  48.7 1.9 %collective-permute-start.1 = (bf16[2,560,128]{2,1,0:T(8,128)(2,1)S(1)}, bf16[2,560,128]{2,1,0:T(8,128)(2,1)S(1)}, u32[]{:S(2)}, u32[]{:S(2)}) collective-permute-start(bf16[2,560,128]{2,1,0:T(8,128)(2,1)S(1)} %pair.1.kv_ref.own_ref), channel_id=1, source_target_pairs={{0,32},{32,64},{64,96},{96,128},{128,160},{160,192},{192,224},{224... | collective-permute-start | bytes 860168 | tf_op jit(solution)/shard_map/ppermute | solution.py:429
  50.7 0.0 collective-permute-done.4.got_ref
  50.7 0.0 all-to-all-done.1.q_ref
  50.7 0.0 copy-done.6
  50.7 0.0 copy-start.3
  50.7 2.8 %first.1 = (bf16[8,128,128]{2,1,0:T(8,128)(2,1)S(1)}, f32[8,8,128]{2,1,0:T(8,128)S(1)}) custom-call(s32[4,4]{1,0:T(4,128)S(1)} %copy-done.6, bf16[8,8,16,128]{3,2,1,0:T(8,128)(2,1)S(1)} %all-to-all-done.1.q_ref, bf16[2,560,128]{2,1,0:T(8,128)(2,1)S(1)} %pair.1.kv_ref.own_ref, bf16[528,128]{1,0:T(8,128)(2,1)S(1)} %get-tuple-element.21.keep_ref, ...), custom_call_target="tpu_custom_call" | custom-call | flops 10000000000 | bytes 1000000 | tf_op jit(solution)/shard_map/first/pallas_call | solution.py:440
  53.5 1.8 %collective-permute-done.2.kv2_ref = bf16[2,560,128]{2,1,0:T(8,128)(2,1)S(1)} collective-permute-done((bf16[2,560,128]{2,1,0:T(8,128)(2,1)S(1)}, bf16[2,560,128]{2,1,0:T(8,128)(2,1)S(1)}, u32[]{:S(2)}, u32[]{:S(2)}) %collective-permute-start.2) | collective-permute-done | bytes 286752 | tf_op jit(solution)/shard_map/ppermute | solution.py:430
  55.3 3.1 %collective-permute-done.1.kv1_ref = bf16[2,560,128]{2,1,0:T(8,128)(2,1)S(1)} collective-permute-done((bf16[2,560,128]{2,1,0:T(8,128)(2,1)S(1)}, bf16[2,560,128]{2,1,0:T(8,128)(2,1)S(1)}, u32[]{:S(2)}, u32[]{:S(2)}) %collective-permute-start.1) | collective-permute-done | bytes 286752 | tf_op jit(solution)/shard_map/ppermute | solution.py:429
  58.5 0.0 copy-done.3
  58.5 0.0 copy-start.1
  58.5 0.0 copy-start.4
  58.5 0.0 copy-start.5
  58.5 3.5 %second.1 = bf16[16,48,128]{2,1,0:T(8,128)(2,1)S(1)} custom-call(s32[4,4]{1,0:T(4,128)S(1)} %copy-done.6, bf16[8,8,16,128]{3,2,1,0:T(8,128)(2,1)S(1)} %all-to-all-done.1.q_ref, bf16[2,560,128]{2,1,0:T(8,128)(2,1)S(1)} %pair.1.kv_ref.own_ref, bf16[2,560,128]{2,1,0:T(8,128)(2,1)S(1)} %collective-permute-done.1.kv1_ref, ...), custom_call_target="tpu_custom_call" | custom-call | flops 10000000000 | bytes 1000000 | tf_op jit(solution)/shard_map/second/pallas_call | solution.py:447
  61.9 19.7 %all_to_all.20.y_ref = bf16[16,48,128]{2,1,0:T(8,128)(2,1)S(1)} all-to-all(bf16[16,48,128]{2,1,0:T(8,128)(2,1)S(1)} %second.1), channel_id=1, replica_groups=mesh['z'=16,'h'=2,'mp'=16] {'z'}, dimensions={0} | all-to-all | bytes 393216 | tf_op jit(solution)/shard_map/all_to_all | solution.py:455
  81.7 0.5 spread.1
  82.1 19.4 %all_to_all.21.r_ref = bf16[32,32,128]{2,1,0:T(8,128)(2,1)S(1)} all-to-all(bf16[32,32,128]{2,1,0:T(8,128)(2,1)S(1)} %spread.1), channel_id=1, replica_groups=mesh['z'=16,'h'=2,'mp'=16] {'h','mp'}, dimensions={0} | all-to-all | bytes 524288 | tf_op jit(solution)/shard_map/all_to_all | solution.py:459
  101.6 0.0 copy-done.1
  101.6 0.0 copy-done.4
  101.6 0.0 copy-done.5
  101.6 1.3 %decode.1 = bf16[4,2,4,384]{3,2,1,0:T(4,128)(2,1)} custom-call(bf16[32,32,128]{2,1,0:T(8,128)(2,1)S(1)} %all_to_all.21.r_ref, bf16[3,3,3,16,384]{4,3,2,1,0:T(8,128)(2,1)S(1)} %copy-done.1, f32[384]{0:T(512)S(1)} %copy-done.4, f32[384]{0:T(512)S(1)} %copy-done.5), custom_call_target="tpu_custom_call" | custom-call | tf_op jit(solution)/shard_map/decode/pallas_call | solution.py:460
Async XLA Ops:
  0.0 0.8 copy-start
  1.7 25.5 %all-to-all-start = ((bf16[16,160,64]{1,2,0:T(8,128)(2,1)}), bf16[16,160,64]{1,2,0:T(8,128)(2,1)S(1)}, u32[]{:S(2)}, u32[]{:S(2)}) async-start(bf16[16,160,64]{1,2,0:T(8,128)(2,1)} %broadcast_in_dim.2), calls=%async_computation | async-start | bytes 1048576 | tf_op jit(solution)/shard_map/all_to_all | solution.py:413
  14.6 20.9 %collective-permute-start.3 = (bf16[528,256]{1,0:T(8,128)(2,1)}, bf16[528,256]{1,0:T(8,128)(2,1)S(1)}, u32[]{:S(2)}, u32[]{:S(2)}) collective-permute-start(bf16[528,256]{1,0:T(8,128)(2,1)} %get-tuple-element.20), channel_id=1, source_target_pairs={{0,64},{1,449},{2,66},{3,451},{4,68},{5,453},{6,70},{7,455},{8,72}... | collective-permute-start | bytes 811016 | tf_op jit(solution)/shard_map/ppermute | solution.py:407
  22.8 17.9 %collective-permute-start = (bf16[528,128]{1,0:T(8,128)(2,1)}, bf16[528,128]{1,0:T(8,128)(2,1)S(1)}, u32[]{:S(2)}, u32[]{:S(2)}) collective-permute-start(bf16[528,128]{1,0:T(8,128)(2,1)} %get-tuple-element.18), channel_id=1, source_target_pairs={{0,16},{16,0},{1,17},{17,1},{2,18},{18,2},{3,19},{19,3},{4,20},{20... | collective-permute-start | bytes 405512 | tf_op jit(solution)/shard_map/ppermute | solution.py:404
  27.2 23.5 %all-to-all-start.1 = ((bf16[8,8,16,128]{3,2,1,0:T(8,128)(2,1)}), bf16[8,8,16,128]{3,2,1,0:T(8,128)(2,1)S(1)}, u32[]{:S(2)}, u32[]{:S(2)}) async-start(bf16[8,8,16,128]{3,2,1,0:T(8,128)(2,1)} %get-tuple-element.16), calls=%async_computation.1 | async-start | bytes 524288 | tf_op jit(solution)/shard_map/all_to_all | solution.py:415
  35.4 5.4 %copy-start.2 = (bf16[528,128]{1,0:T(8,128)(2,1)S(1)}, bf16[528,128]{1,0:T(8,128)(2,1)}, u32[]{:S(2)}) copy-start(bf16[528,128]{1,0:T(8,128)(2,1)} %get-tuple-element.17.keep_ref) | copy-start | bytes 405508
  35.5 15.2 %copy-start.6 = (s32[4,4]{1,0:T(4,128)S(1)}, s32[4,4]{1,0:T(4,128)}, u32[]{:S(2)}) copy-start(s32[4,4]{1,0:T(4,128)} %fm_ref.3) | copy-start | bytes 196
  35.5 15.1 %collective-permute-start.4 = (bf16[528,128]{1,0:T(8,128)(2,1)S(1)}, bf16[528,128]{1,0:T(8,128)(2,1)S(1)}, u32[]{:S(2)}, u32[]{:S(2)}) collective-permute-start(bf16[528,128]{1,0:T(8,128)(2,1)S(1)} %get-tuple-element.22), channel_id=1, source_target_pairs={{0,16},{16,0},{1,17},{17,1},{2,18},{18,2},{3,19},{19,3},{4,20},{20... | collective-permute-start | bytes 405512 | tf_op jit(solution)/shard_map/ppermute | solution.py:404
  43.0 12.3 %collective-permute-start.2 = (bf16[2,560,128]{2,1,0:T(8,128)(2,1)S(1)}, bf16[2,560,128]{2,1,0:T(8,128)(2,1)S(1)}, u32[]{:S(2)}, u32[]{:S(2)}) collective-permute-start(bf16[2,560,128]{2,1,0:T(8,128)(2,1)S(1)} %pair.1.kv_ref.own_ref), channel_id=1, source_target_pairs={{32,0},{64,32},{96,64},{128,96},{160,128},{192,160},{224,192},{256... | collective-permute-start | bytes 860168 | tf_op jit(solution)/shard_map/ppermute | solution.py:430
  48.7 9.7 %collective-permute-start.1 = (bf16[2,560,128]{2,1,0:T(8,128)(2,1)S(1)}, bf16[2,560,128]{2,1,0:T(8,128)(2,1)S(1)}, u32[]{:S(2)}, u32[]{:S(2)}) collective-permute-start(bf16[2,560,128]{2,1,0:T(8,128)(2,1)S(1)} %pair.1.kv_ref.own_ref), channel_id=1, source_target_pairs={{0,32},{32,64},{64,96},{96,128},{128,160},{160,192},{192,224},{224... | collective-permute-start | bytes 860168 | tf_op jit(solution)/shard_map/ppermute | solution.py:429
  50.7 7.8 %copy-start.3 = (bf16[2,2,4,16]{3,2,1,0:T(4,128)(2,1)S(1)}, bf16[2,2,4,16]{3,2,1,0:T(4,128)(2,1)}, u32[]{:S(2)}) copy-start(bf16[2,2,4,16]{3,2,1,0:T(4,128)(2,1)} %prev_ref.3) | copy-start | bytes 1540
  58.5 43.1 %copy-start.1 = (bf16[3,3,3,16,384]{4,3,2,1,0:T(8,128)(2,1)S(1)}, bf16[3,3,3,16,384]{4,3,2,1,0:T(8,128)(2,1)}, u32[]{:S(2)}) copy-start(bf16[3,3,3,16,384]{4,3,2,1,0:T(8,128)(2,1)} %w_ref.1) | copy-start | bytes 995332
  58.5 43.1 %copy-start.4 = (f32[384]{0:T(512)S(1)}, f32[384]{0:T(512)}, u32[]{:S(2)}) copy-start(f32[384]{0:T(512)} %bias_ref.1) | copy-start | bytes 4612
  58.5 43.1 %copy-start.5 = (f32[384]{0:T(512)S(1)}, f32[384]{0:T(512)}, u32[]{:S(2)}) copy-start(f32[384]{0:T(512)} %gain_ref.1) | copy-start | bytes 4612
